TPU v7x, 32 devices: a whole 2x2x4 slice. The times are simulated.
32 devices in a mesh: heads: 2 (over x), seq: 16 (over z, y, core).
Axes of the slice: x: 2, y: 2, z: 4, core: 2. Of those that a mesh axis runs over, the one named last changes fastest.
Arguments:
- queries: bfloat16 [8192, 4096], P('seq', 'heads'), may hold values from -6 to 6
- key_vectors: bfloat16 [8192, 4096], P('seq', 'heads'), may hold values from -6 to 6
- values: bfloat16 [8192, 4096], P('seq', 'heads'), may hold values from -40 to 40
- level_weights: float32 [14, 32, 8192], P(None, 'heads', 'seq'), may hold values from 0.1 to 1
- gate_branch: bfloat16 [8192, 4096], P(('seq', 'heads')), may hold values from -6 to 6
- norm_gain: float32 [4096], replicated, may hold values from 0.5 to 1.5
Outputs:
- normed: bfloat16 [8192, 4096], P(('seq', 'heads'))
All inputs are finite; a program needn't handle non-finite values.
Results may differ from a plain program's by a relative error of at most 0.008.
Values may be sent and summed in bfloat16 or wider, within the bound.
No kernel may reach another device: no remote copies, remote signals or barrier semaphores. Data moves between devices by JAX's collectives and lax.ppermute only.
A program may use at most 128 MiB of HBM per device.

v0:
```python
import jax
import jax.numpy as jnp
from jax import lax
from jax.sharding import PartitionSpec as P

HEAD_DIM = 128
WINDOW = 512


EPSILON = 1e-06


def passed_along(value, axis, steps):
    count = lax.axis_size(axis)
    leading, last = (max(0, -steps), min(count, count - steps))
    return lax.ppermute(value, axis, [(source, source + steps) for source in range(leading, last)])


def from_partner(shard, axis, apart):
    return lax.ppermute(shard, axis, [(i, i ^ 1 << apart) for i in range(lax.axis_size(axis))])


def bit_count(numbers, width_bits):
    lengths = jnp.zeros(numbers.shape, jnp.int32)
    for shift_bit in range(width_bits):
        lengths = lengths + (numbers >> shift_bit > 0).astype(jnp.int32)
    return lengths


def level_scale(levels):
    return jnp.exp2(-0.5 * jnp.maximum(levels - 1, 0).astype(jnp.float32))


def local(queries, key_vectors, values, level_weights, gate_branch, norm_gain):
    tok_rows = queries.shape[0]
    head_groups = queries.shape[1] // HEAD_DIM
    near_count = tok_rows.bit_length()
    far_count = level_weights.shape[0] - near_count
    score_scale = HEAD_DIM ** (-0.5)
    seq_place = lax.axis_index("seq")
    first_token = seq_place * tok_rows
    key_pieces = [key_vectors]
    value_pieces = [values]
    moved_keys, moved_values = passed_along((key_vectors, values), "seq", 1)
    key_pieces.insert(0, moved_keys)
    value_pieces.insert(0, moved_values)
    context_keys = jnp.concatenate(key_pieces, axis=0).reshape(-1, head_groups, HEAD_DIM)
    context_values = jnp.concatenate(value_pieces, axis=0).reshape(-1, head_groups, HEAD_DIM)
    query_heads = queries.reshape(tok_rows, head_groups, HEAD_DIM)
    key_heads = key_vectors.reshape(tok_rows, head_groups, HEAD_DIM)
    value_heads = values.reshape(tok_rows, head_groups, HEAD_DIM)
    states = jnp.einsum(
        "khd,khe->hde", key_heads, value_heads, preferred_element_type=jnp.float32
    ).astype(jnp.bfloat16)
    running = states.astype(jnp.float32)
    bucket_list = []
    for level_id in range(far_count):
        partner = from_partner(running, "seq", level_id)
        bucket_list.append(partner * (seq_place >> level_id & 1).astype(jnp.float32))
        running = running + partner
    buckets = jnp.stack(bucket_list, axis=0)
    bucket_half = buckets.astype(jnp.bfloat16)
    far_proj = jnp.einsum(
        "qhd,jhde->jqhe", query_heads, bucket_half, preferred_element_type=jnp.float32
    )
    far_scale = level_scale(near_count + jnp.arange(far_count, dtype=jnp.int32)) * score_scale
    far_coef = level_weights[near_count:] * far_scale[:, None, None]
    far_out = jnp.sum(jnp.transpose(far_coef, (0, 2, 1))[:, :, :, None] * far_proj, axis=0)
    positions = jnp.arange(tok_rows, dtype=jnp.int32)
    level_table = bit_count(positions[:, None] ^ positions[None, :], near_count)
    causal = positions[:, None] >= positions[None, :]
    near_scale = level_scale(jnp.arange(near_count, dtype=jnp.int32))
    query_block = min(tok_rows, 512)
    key_low = min(0, WINDOW)
    key_high = WINDOW + query_block
    scores = (
        jnp.einsum("qhd,khd->hqk", query_heads, context_keys, preferred_element_type=jnp.float32)
        * score_scale
    )
    query_pos = 0 + jnp.arange(query_block, dtype=jnp.int32)
    key_pos = key_low - WINDOW + jnp.arange(key_high - key_low, dtype=jnp.int32)
    pos_gap = query_pos[:, None] - key_pos[None, :]
    in_window = (pos_gap >= 0) & (pos_gap < WINDOW) & (key_pos + first_token >= 0)[None, :]
    row_max = jnp.max(jnp.where(in_window[None], scores, -jnp.inf), axis=2, keepdims=True)
    exp_scores = jnp.where(in_window[None], jnp.exp(scores - row_max), 0.0)
    weights = (exp_scores / jnp.sum(exp_scores, axis=2, keepdims=True)).astype(jnp.bfloat16)
    windowed = jnp.einsum(
        "hqk,khd->qhd", weights, context_values, preferred_element_type=jnp.float32
    )
    level_mix = jnp.zeros((head_groups, query_block, query_block), jnp.float32)
    for level_id in range(near_count):
        row_weights = level_weights[level_id] * near_scale[level_id]
        level_mix = level_mix + jnp.where(
            level_table[None] == level_id, row_weights[:, :, None], 0.0
        )
    level_mix = jnp.where(causal[None], level_mix, 0.0)
    own_scores = scores[:, :, WINDOW - key_low :]
    near_weights = (own_scores * level_mix).astype(jnp.bfloat16)
    near_out = jnp.einsum(
        "hqk,khd->qhd",
        near_weights,
        context_values[WINDOW : WINDOW + query_block],
        preferred_element_type=jnp.float32,
    )
    pieces = windowed + near_out + far_out
    mixed = pieces.reshape(tok_rows, head_groups * HEAD_DIM).astype(jnp.bfloat16)
    token_rows = lax.all_to_all(mixed, "heads", split_axis=0, concat_axis=1, tiled=True)
    gated = token_rows.astype(jnp.float32) * jax.nn.silu(gate_branch.astype(jnp.float32))
    mean_square = jnp.mean(gated * gated, axis=1, keepdims=True)
    return (norm_gain * gated * lax.rsqrt(mean_square + EPSILON)).astype(jnp.bfloat16)


def solution(mesh):
    return jax.shard_map(
        local,
        mesh=mesh,
        in_specs=(
            P("seq", "heads"),
            P("seq", "heads"),
            P("seq", "heads"),
            P(None, "heads", "seq"),
            P(("seq", "heads"), None),
            P(),
        ),
        out_specs=P(("seq", "heads"), None),
        check_vma=False,
    )
```

profile of v0, /device:TPU:0, one launch (start us, length us, event | category | flops | bytes accessed | tf_op | source)
XLA Modules:
  0.0 226.4 jit_solution(11439378280267592283)
XLA Ops:
  0.0 2.9 %copy.35 = bf16[512,2048]{0,1:T(8,128)(2,1)S(1)} copy(bf16[512,2048]{1,0:T(8,128)(2,1)} %param.7) | data formatting | bytes 4194304 | tf_op args[1]
  2.9 3.7 %collective-permute-start.1 = (bf16[512,2048]{0,1:T(8,128)(2,1)S(1)}, bf16[512,2048]{0,1:T(8,128)(2,1)}, u32[]{:S(2)}, u32[]{:S(2)}) collective-permute-start(bf16[512,2048]{0,1:T(8,128)(2,1)S(1)} %copy.35), channel_id=1, source_target_pairs={{0,1},{1,2},{2,3},{3,4},{4,5},{5,6},{6,7},{7,8},{8,9},{9,10},{10,1... | collective-permute-start | bytes 6291464 | tf_op jit(solution)/shard_map/ppermute | solution.py:16
  6.6 4.5 %collective-permute-start = (bf16[512,2048]{1,0:T(8,128)(2,1)}, bf16[512,2048]{1,0:T(8,128)(2,1)}, u32[]{:S(2)}, u32[]{:S(2)}) collective-permute-start(bf16[512,2048]{1,0:T(8,128)(2,1)} %param.8), channel_id=1, source_target_pairs={{0,1},{1,2},{2,3},{3,4},{4,5},{5,6},{6,7},{7,8},{8,9},{9,10},{10,1... | collective-permute-start | bytes 6291464 | tf_op jit(solution)/shard_map/ppermute | solution.py:16
  11.1 3.4 %fusion.33 = f32[16,128,128]{2,1,0:T(8,128)} fusion(bf16[512,16,128]{0,2,1:T(8,128)(2,1)S(1)} %bitcast.93, bf16[512,2048]{1,0:T(8,128)(2,1)} %param.8), kind=kOutput, calls=%fused_computation.43 | convolution fusion | flops 268959744 | bytes 5242880 | tf_op jit(solution)/shard_map/khd,khe->hde/dot_general | solution.py:52
  14.5 0.0 collective-permute-start.2
  14.5 1.4 broadcast_compare_fusion.9
  16.0 0.7 fusion.42
  16.6 3.5 %copy.62 = bf16[64,8,16,128]{3,2,1,0:T(8,128)(2,1)} copy(bf16[64,8,16,128]{3,1,2,0:T(8,128)(2,1)} %bitcast.94) | data formatting | bytes 4194304
  20.2 0.0 copy-done.5
  20.2 0.1 multiply_bitcast_fusion.1
  20.3 0.1 copy.43
  20.4 1.1 fusion.27
  21.5 6.3 %multiply_bitcast_fusion.11 = (f32[16,512]{1,0:T(8,128)}, f32[16,512]{1,0:T(8,128)}, f32[16,512]{1,0:T(8,128)}, f32[16,512]{1,0:T(8,128)}, f32[16,512]{1,0:T(8,1...) fusion(f32[14,16,512]{2,1,0:T(8,128)S(1)} %copy-done.5, f32[]{:T(128)} %bitcast.4, ...), kind=kLoop, calls=%fused_computation.85 | loop fusion | flops 73728 | bytes 589860 | tf_op jit(solution)/shard_map/mul | solution.py:92
  27.8 2.3 %iota_compare_fusion = (pred[512,512]{0,1:T(8,128)(4,1)}, pred[512,512]{0,1:T(8,128)(4,1)}) fusion(), kind=kLoop, calls=%fused_computation.60 | loop fusion | flops 11010048 | bytes 524288 | tf_op jit(solution)/shard_map/ge | solution.py:71
  30.1 2.4 %broadcast_compare_fusion.1 = (pred[512,512]{0,1:T(8,128)(4,1)}, pred[512,512]{0,1:T(8,128)(4,1)}) fusion(), kind=kLoop, calls=%fused_computation.66 | loop fusion | flops 11010048 | bytes 524288 | tf_op jit(solution)/shard_map/eq | solution.py:94
  32.5 1.3 multiply_bitcast_fusion.2
  33.8 2.4 %broadcast_compare_fusion.3 = (pred[512,512]{0,1:T(8,128)(4,1)}, pred[512,512]{0,1:T(8,128)(4,1)}) fusion(), kind=kLoop, calls=%fused_computation.68 | loop fusion | flops 11010048 | bytes 524288 | tf_op jit(solution)/shard_map/eq | solution.py:94
  36.2 2.4 %broadcast_compare_fusion.5 = (pred[512,512]{0,1:T(8,128)(4,1)}, pred[512,512]{0,1:T(8,128)(4,1)}) fusion(), kind=kLoop, calls=%fused_computation.70 | loop fusion | flops 11010048 | bytes 524288 | tf_op jit(solution)/shard_map/eq | solution.py:94
  38.6 2.4 %broadcast_compare_fusion.7 = (pred[512,512]{0,1:T(8,128)(4,1)}, pred[512,512]{0,1:T(8,128)(4,1)}) fusion(), kind=kLoop, calls=%fused_computation.72 | loop fusion | flops 11010048 | bytes 524288 | tf_op jit(solution)/shard_map/eq | solution.py:94
  41.1 0.0 collective-permute-done.2
  41.1 2.7 %fusion.36 = (bf16[1,16,128,128]{3,2,1,0:T(8,128)(2,1)S(1)}, f32[16,128,128]{2,1,0:T(8,128)}) fusion(f32[16,128,128]{2,1,0:T(8,128)} %collective-permute-done.2, f32[]{:T(128)S(6)} %convert_element_type.593, f32[16,128,128]{2,1,0:T(8,128)} %fusion.33), kind=kLoop, calls=%fused_computation.61 | loop fusion | flops 786432 | bytes 3670020 | tf_op jit(solution)/shard_map/stack | solution.py:61
  43.8 0.2 collective-permute-start.3
  44.0 0.0 collective-permute-done.1
  44.0 4.3 %pad_maximum_fusion.1 = bf16[1024,2048]{0,1:T(8,128)(2,1)} fusion(bf16[512,2048]{0,1:T(8,128)(2,1)S(1)} %copy.35, bf16[512,2048]{0,1:T(8,128)(2,1)} %collective-permute-done.1), kind=kLoop, calls=%fused_computation.21 | loop fusion | flops 8388608 | bytes 8388608 | tf_op jit(solution)/shard_map/concatenate | solution.py:47
  48.4 18.8 %multiply_bitcast_fusion = f32[16,512,1024]{1,2,0:T(8,128)} fusion(bf16[1024,16,128]{0,2,1:T(8,128)(2,1)} %bitcast.92, bf16[512,2048]{1,0:T(8,128)(2,1)} %param.6), kind=kOutput, calls=%fused_computation.5 | convolution fusion | flops 2155872256 | bytes 39845888 | tf_op jit(solution)/shard_map/qhd,khd->hqk/dot_general | solution.py:77
  67.2 2.5 %collective-permute-done.3 = f32[16,128,128]{2,1,0:T(8,128)} collective-permute-done((f32[16,128,128]{2,1,0:T(8,128)}, f32[16,128,128]{2,1,0:T(8,128)}, u32[]{:S(2)}, u32[]{:S(2)}) %collective-permute-start.3) | collective-permute-done | bytes 1048608 | tf_op jit(solution)/shard_map/ppermute | solution.py:20
  69.7 2.6 %fusion.37 = (bf16[1,16,128,128]{3,2,1,0:T(8,128)(2,1)}, f32[16,128,128]{2,1,0:T(8,128)S(1)}) fusion(f32[16,128,128]{2,1,0:T(8,128)} %collective-permute-done.3, f32[]{:T(128)S(6)} %convert_element_type.594, f32[16,128,128]{2,1,0:T(8,128)} %get-tuple-element.6), kind=kLoop, calls=%fused_computation.62 | loop fusion | flops 786432 | bytes 3670020 | tf_op jit(solution)/shard_map/stack | solution.py:61
  72.3 9.5 %collective-permute-start.4 = (f32[16,128,128]{2,1,0:T(8,128)S(1)}, f32[16,128,128]{2,1,0:T(8,128)S(1)}, u32[]{:S(2)}, u32[]{:S(2)}) collective-permute-start(f32[16,128,128]{2,1,0:T(8,128)S(1)} %get-tuple-element.8), channel_id=1, source_target_pairs={{0,4},{1,5},{2,6},{3,7},{4,0},{5,1},{6,2},{7,3},{8,12},{9,13},{10,... | collective-permute-start | bytes 3145736 | tf_op jit(solution)/shard_map/ppermute | solution.py:20
  81.8 24.7 %fusion.9 = f32[16,512,128]{1,2,0:T(8,128)} fusion(f32[16,512,1024]{1,2,0:T(8,128)} %multiply_bitcast_fusion, f32[16,512]{1,0:T(8,128)} %multiply_bitcast_fusion.2, f32[16,512]{1,0:T(8,128)} %get-tuple-element.12, f32[16,512]{1,0:T(8,128)} %get-tuple-element.13, f32[16,512]{1,0:T(8,128)} %get-tuple-element.14, f32[16,512]{1,0:T(8,128)} %get-tuple-element.15, ...), kind=kOutput, calls=%fused_computation.13 | convolution fusion | flops 1166016512 | bytes 26279936 | tf_op jit(solution)/shard_map/hqk,khd->qhd/dot_general | solution.py:99
  106.4 0.0 collective-permute-done.4
  106.4 1.4 fusion.38
  107.8 2.6 %collective-permute-start.5 = (f32[16,128,128]{2,1,0:T(8,128)}, f32[16,128,128]{2,1,0:T(8,128)}, u32[]{:S(2)}, u32[]{:S(2)}) collective-permute-start(f32[16,128,128]{2,1,0:T(8,128)} %get-tuple-element.10), channel_id=1, source_target_pairs={{0,8},{1,9},{2,10},{3,11},{4,12},{5,13},{6,14},{7,15},{8,0},{9,1},... | collective-permute-start | bytes 3145736 | tf_op jit(solution)/shard_map/ppermute | solution.py:20
  110.4 34.6 %fusion.43 = (f32[16,512]{1,0:T(8,128)S(1)}, f32[16,512,1024]{1,2,0:T(8,128)}) fusion(f32[16,512,1024]{1,2,0:T(8,128)} %multiply_bitcast_fusion, pred[512,1024]{0,1:T(8,128)(4,1)S(1)} %fusion.27), kind=kOutput, calls=%fused_computation.94 | output fusion | flops 33555456 | bytes 67665920 | tf_op jit(solution)/shard_map/sub | solution.py:85
  145.0 0.0 collective-permute-done
  145.0 4.1 %pad_maximum_fusion = bf16[1024,2048]{1,0:T(8,128)(2,1)} fusion(bf16[512,2048]{1,0:T(8,128)(2,1)S(1)} %copy-done.2, bf16[512,2048]{1,0:T(8,128)(2,1)} %collective-permute-done), kind=kLoop, calls=%fused_computation.20 | loop fusion | flops 8388608 | bytes 8388608 | tf_op jit(solution)/shard_map/concatenate | solution.py:48
  149.1 6.5 %copy.34 = bf16[1024,2048]{0,1:T(8,128)(2,1)} copy(bf16[1024,2048]{1,0:T(8,128)(2,1)} %pad_maximum_fusion) | data formatting | bytes 8388608 | tf_op jit(solution)/shard_map/concatenate | solution.py:48
  155.7 0.5 collective-permute-done.5
  156.2 1.3 fusion.39
  157.6 6.3 %fusion.5 = f32[512,16,128]{0,2,1:T(8,128)} fusion(f32[4,512,16]{1,0,2:T(4,128)S(1)} %copy.43, bf16[512,16,128,1]{2,1,0,3:T(8,128)(2,1)S(1)} %bitcast.97, bf16[1,16,128,128]{3,2,1,0:T(8,128)(2,1)S(1)} %fusion.39, bf16[1,16,128,128]{3,2,1,0:T(8,128)(2,1)} %get-tuple-element.9, bf16[1,16,128,128]{3,2,1,0:T(8,128)(2,1)S(1)} %copy-done.4, ...), kind=kOutput, calls=%fused_computation.9 | convolution fusion | flops 1084227584 | bytes 8519680 | tf_op jit(solution)/shard_map/qhd,jhde->jqhe/dot_general | solution.py:63
  163.8 16.9 %fusion.16 = bf16[512,16,128]{0,2,1:T(8,128)(2,1)} fusion(f32[512,16,128]{0,2,1:T(8,128)} %fusion.5, f32[16,512,128]{1,2,0:T(8,128)} %fusion.9, bf16[1024,16,128]{0,2,1:T(8,128)(2,1)} %bitcast.96, f32[16,512,1024]{1,2,0:T(8,128)} %get-tuple-element.31, f32[16,512]{1,0:T(8,128)S(1)} %get-tuple-element.30), kind=kOutput, calls=%fused_computation.24 | convolution fusion | flops 2167406592 | bytes 48267264 | tf_op jit(solution)/shard_map/hqk,khd->qhd/dot_general | solution.py:87
  180.8 2.5 %convert_element_type.598 = bf16[2,256,2048]{1,0,2:T(2,128)(2,1)S(1)} reshape(bf16[512,16,128]{0,2,1:T(8,128)(2,1)} %fusion.16) | data formatting | bytes 4194304 | tf_op jit(solution)/shard_map/convert_element_type | solution.py:106
  183.3 0.3 copy.48
  183.6 27.8 %all_to_all.10 = bf16[2,256,2048]{1,2,0:T(8,128)(2,1)S(1)} all-to-all(bf16[2,256,2048]{1,2,0:T(8,128)(2,1)S(1)} %copy.48), channel_id=1, replica_groups=mesh['heads'=2,'seq'=16] {'heads'}, dimensions={0} | all-to-all | bytes 4194304 | tf_op jit(solution)/shard_map/all_to_all | solution.py:107
  211.4 2.3 %convert_element_type.605 = f32[2,256,2048]{1,2,0:T(8,128)} convert(bf16[2,256,2048]{1,2,0:T(8,128)(2,1)S(1)} %all_to_all.10) | non-fusion elementwise | flops 1048576 | bytes 6291456 | tf_op jit(solution)/shard_map/convert_element_type | solution.py:108
  213.7 5.8 %copy.49 = f32[256,4096]{1,0:T(8,128)} copy(f32[256,4096]{0,1:T(8,128)} %bitcast.95) | data formatting | bytes 8388608 | tf_op jit(solution)/shard_map/convert_element_type | solution.py:108
  219.5 0.0 copy-done.1
  219.5 3.9 %multiply_reduce_fusion = f32[256]{0:T(256)S(1)} fusion(f32[256,4096]{1,0:T(8,128)} %copy.49, bf16[256,4096]{1,0:T(8,128)(2,1)S(1)} %copy-done.1), kind=kLoop, calls=%fused_computation.26 | loop fusion | flops 8388352 | bytes 6292480 | tf_op jit(solution)/shard_map/reduce_sum | solution.py:109
  223.4 3.0 %multiply_convert_fusion = bf16[256,4096]{1,0:T(8,128)(2,1)} fusion(f32[256]{0:T(256)S(1)} %add_rsqrt_fusion, f32[4096]{0:T(1024)S(1)} %copy-done.6, f32[256,4096]{1,0:T(8,128)S(1)} %copy-done, bf16[256,4096]{1,0:T(8,128)(2,1)S(1)} %copy-done.1), kind=kLoop, calls=%fused_computation.25 | loop fusion | flops 9437184 | bytes 8406016 | tf_op jit(solution)/shard_map/convert_element_type | solution.py:110
  (17 shorter events, 0.1 us)
Async XLA Ops:
  2.9 41.2 %collective-permute-start.1 = (bf16[512,2048]{0,1:T(8,128)(2,1)S(1)}, bf16[512,2048]{0,1:T(8,128)(2,1)}, u32[]{:S(2)}, u32[]{:S(2)}) collective-permute-start(bf16[512,2048]{0,1:T(8,128)(2,1)S(1)} %copy.35), channel_id=1, source_target_pairs={{0,1},{1,2},{2,3},{3,4},{4,5},{5,6},{6,7},{7,8},{8,9},{9,10},{10,1... | collective-permute-start | bytes 6291464 | tf_op jit(solution)/shard_map/ppermute | solution.py:16
  6.6 138.5 %collective-permute-start = (bf16[512,2048]{1,0:T(8,128)(2,1)}, bf16[512,2048]{1,0:T(8,128)(2,1)}, u32[]{:S(2)}, u32[]{:S(2)}) collective-permute-start(bf16[512,2048]{1,0:T(8,128)(2,1)} %param.8), channel_id=1, source_target_pairs={{0,1},{1,2},{2,3},{3,4},{4,5},{5,6},{6,7},{7,8},{8,9},{9,10},{10,1... | collective-permute-start | bytes 6291464 | tf_op jit(solution)/shard_map/ppermute | solution.py:16
  11.1 9.1 %copy-start.5 = (f32[14,16,512]{2,1,0:T(8,128)S(1)}, f32[14,16,512]{2,1,0:T(8,128)}, u32[]{:S(2)}) copy-start(f32[14,16,512]{2,1,0:T(8,128)} %param.9) | copy-start | bytes 1376260
  14.5 26.6 %collective-permute-start.2 = (f32[16,128,128]{2,1,0:T(8,128)}, f32[16,128,128]{2,1,0:T(8,128)}, u32[]{:S(2)}, u32[]{:S(2)}) collective-permute-start(f32[16,128,128]{2,1,0:T(8,128)} %fusion.33), channel_id=1, source_target_pairs={{0,1},{1,0},{2,3},{3,2},{4,5},{5,4},{6,7},{7,6},{8,9},{9,8},{10,11... | collective-permute-start | bytes 3145736 | tf_op jit(solution)/shard_map/ppermute | solution.py:20
  43.8 25.9 %collective-permute-start.3 = (f32[16,128,128]{2,1,0:T(8,128)}, f32[16,128,128]{2,1,0:T(8,128)}, u32[]{:S(2)}, u32[]{:S(2)}) collective-permute-start(f32[16,128,128]{2,1,0:T(8,128)} %get-tuple-element.6), channel_id=1, source_target_pairs={{0,2},{1,3},{2,0},{3,1},{4,6},{5,7},{6,4},{7,5},{8,10},{9,11},{10,... | collective-permute-start | bytes 3145736 | tf_op jit(solution)/shard_map/ppermute | solution.py:20
  48.4 33.4 %copy-start.2 = (bf16[512,2048]{1,0:T(8,128)(2,1)S(1)}, bf16[512,2048]{1,0:T(8,128)(2,1)}, u32[]{:S(2)}) copy-start(bf16[512,2048]{1,0:T(8,128)(2,1)} %param.8) | copy-start | bytes 6291460
  72.3 34.2 %collective-permute-start.4 = (f32[16,128,128]{2,1,0:T(8,128)S(1)}, f32[16,128,128]{2,1,0:T(8,128)S(1)}, u32[]{:S(2)}, u32[]{:S(2)}) collective-permute-start(f32[16,128,128]{2,1,0:T(8,128)S(1)} %get-tuple-element.8), channel_id=1, source_target_pairs={{0,4},{1,5},{2,6},{3,7},{4,0},{5,1},{6,2},{7,3},{8,12},{9,13},{10,... | collective-permute-start | bytes 3145736 | tf_op jit(solution)/shard_map/ppermute | solution.py:20
  107.8 48.4 %collective-permute-start.5 = (f32[16,128,128]{2,1,0:T(8,128)}, f32[16,128,128]{2,1,0:T(8,128)}, u32[]{:S(2)}, u32[]{:S(2)}) collective-permute-start(f32[16,128,128]{2,1,0:T(8,128)} %get-tuple-element.10), channel_id=1, source_target_pairs={{0,8},{1,9},{2,10},{3,11},{4,12},{5,13},{6,14},{7,15},{8,0},{9,1},... | collective-permute-start | bytes 3145736 | tf_op jit(solution)/shard_map/ppermute | solution.py:20
  149.1 8.4 %copy-start.3 = (bf16[64,8,16,128]{3,2,1,0:T(8,128)(2,1)S(1)}, bf16[64,8,16,128]{3,2,1,0:T(8,128)(2,1)}, u32[]{:S(2)}) copy-start(bf16[64,8,16,128]{3,2,1,0:T(8,128)(2,1)} %copy.62) | copy-start | bytes 6291460
  149.1 8.4 %copy-start.4 = (bf16[1,16,128,128]{3,2,1,0:T(8,128)(2,1)S(1)}, bf16[1,16,128,128]{3,2,1,0:T(8,128)(2,1)}, u32[]{:S(2)}) copy-start(bf16[1,16,128,128]{3,2,1,0:T(8,128)(2,1)} %get-tuple-element.7) | copy-start | bytes 1572868
  213.7 5.8 %copy-start.1 = (bf16[256,4096]{1,0:T(8,128)(2,1)S(1)}, bf16[256,4096]{1,0:T(8,128)(2,1)}, u32[]{:S(2)}) copy-start(bf16[256,4096]{1,0:T(8,128)(2,1)} %param.10) | copy-start | bytes 6291460
  219.5 3.9 %copy-start = (f32[256,4096]{1,0:T(8,128)S(1)}, f32[256,4096]{1,0:T(8,128)}, u32[]{:S(2)}) copy-start(f32[256,4096]{1,0:T(8,128)} %copy.49) | copy-start | bytes 12582916
  219.5 3.9 %copy-start.6 = (f32[4096]{0:T(1024)S(1)}, f32[4096]{0:T(1024)}, u32[]{:S(2)}) copy-start(f32[4096]{0:T(1024)} %param.11) | copy-start | bytes 49156
where the time goes:
time: 227 us; the launch traced here: 226 us
  other arithmetic  82.4 us (36%)
  matrix products  70.1 us (31%)
  blocking collectives  27.8 us (12%)
  local copies, waits for them, and re-layouts  22.4 us (10%)
  starting transfers between devices  20.5 us (9%)
  waiting for transfers between devices  3.03 us (1%)
    sub x1, other arithmetic, local(): exp_scores = jnp.where(in_window[None], jnp.exp(scores - row_max), 0.0)  34.6 us
    all_to_all x1, blocking collectives, local(): lax.all_to_all(mixed, 'heads', split_axis=0, concat_axis=1, tiled=True)  27.8 us
    dot_general x1, matrix products, local(): jnp.einsum('hqk,khd->qhd', near_weights, context_values[WINDOW:WINDOW + q...  24.7 us
    dot_general x1, matrix products, local(): jnp.einsum('qhd,khd->hqk', query_heads, context_keys, preferred_element_t...  18.8 us
    dot_general x1, matrix products, local(): jnp.einsum('hqk,khd->qhd', weights, context_values, preferred_element_typ...  16.9 us
    ppermute x4, starting transfers between devices, from_partner(): lax.ppermute(shard, axis, [(i, i ^ 1 << apart) for i in range(lax.axis_si...  12.3 us
    eq x5, other arithmetic, local(): level_table[None] == level_id  11.1 us
    ppermute x2, starting transfers between devices, passed_along(): lax.ppermute(value, axis, [(source, source + steps) for source in range(l...  8.24 us
  transfers between devices with their start and end apart: 6, of which 2 were waited for; matrix products, arithmetic and copies ran while one was open for 57% of the time, Pallas kernels for 0%

commit v1 on v0

v1 whole, which is shorter than its diff:
```python
import functools

import jax
import jax.numpy as jnp
from jax import lax
from jax.experimental import pallas as pl
from jax.experimental.pallas import tpu as pltpu
from jax.sharding import PartitionSpec as P

HEAD_DIM = 128
WINDOW = 512
EPSILON = 1e-06
LOG2E = 1.4426950408889634
VMEM = 48 * 1024 * 1024
NN = (((1,), (0,)), ((), ()))
NT = (((1,), (1,)), ((), ()))
TN = (((0,), (0,)), ((), ()))


def mm(left, right, dims=NN):
    return lax.dot_general(left, right, dims, preferred_element_type=jnp.float32)


def level_scale(levels):
    return jnp.exp2(-0.5 * jnp.maximum(levels - 1, 0).astype(jnp.float32))


def joined(parts, axis):
    return parts[0] if len(parts) == 1 else jnp.concatenate(parts, axis)


def state_kernel(heads, k_ref, v_ref, out_ref):
    for h in range(heads):
        cols = slice(h * HEAD_DIM, (h + 1) * HEAD_DIM)
        out_ref[h] = mm(k_ref[:, cols], v_ref[:, cols], TN).astype(jnp.bfloat16)


def block_states(k, v):
    rows, width = k.shape
    heads = width // HEAD_DIM
    step = 4 if heads % 4 == 0 else 1
    block = pl.BlockSpec((rows, step * HEAD_DIM), lambda g: (0, g))
    return pl.pallas_call(
        functools.partial(state_kernel, step),
        grid=(heads // step,),
        in_specs=[block, block],
        out_specs=pl.BlockSpec((step, HEAD_DIM, HEAD_DIM), lambda g: (g, 0, 0)),
        out_shape=jax.ShapeDtypeStruct((heads, HEAD_DIM, HEAD_DIM), jnp.bfloat16),
        name="block_states",
    )(k, v)


def attend_kernel(qb, first_ref, q_ref, k_ref, v_ref, kp_ref, vp_ref, lw_ref, table_ref, out_ref):
    rows = q_ref.shape[0]
    lane = HEAD_DIM
    scale = HEAD_DIM**-0.5 * LOG2E
    bias = jnp.where(first_ref[0] == 0, -1e30, 0.0).astype(jnp.float32)
    table = table_ref[...]
    causal = lax.broadcasted_iota(jnp.int32, (qb, qb), 0) >= lax.broadcasted_iota(
        jnp.int32, (qb, qb), 1
    )
    lane_bits = lane.bit_length() - 1
    lw = lw_ref[0]
    for low in range(0, rows, qb):
        high = low + qb
        q = q_ref[low:high, :]
        own = mm(q, k_ref[:high, :], NT)
        past = mm(q, kp_ref[low:, :], NT)
        edge = jnp.where(causal, own[:, low:], past[:, :qb] + bias)
        top = jnp.max(edge, axis=1, keepdims=True)
        if low:
            top = jnp.maximum(top, jnp.max(own[:, :low], axis=1, keepdims=True))
        if high < rows:
            top = jnp.maximum(top, jnp.max(past[:, qb:], axis=1, keepdims=True) + bias)
        edge = jnp.exp2((edge - top) * scale)
        total = jnp.sum(edge, axis=1, keepdims=True)
        own_weights = [jnp.where(causal, edge, 0.0).astype(jnp.bfloat16)]
        past_weights = [jnp.where(causal, 0.0, edge).astype(jnp.bfloat16)]
        if low:
            inner = jnp.exp2((own[:, :low] - top) * scale)
            total = total + jnp.sum(inner, axis=1, keepdims=True)
            own_weights.insert(0, inner.astype(jnp.bfloat16))
        if high < rows:
            outer = jnp.exp2((past[:, qb:] - (top - bias)) * scale)
            total = total + jnp.sum(outer, axis=1, keepdims=True)
            past_weights.append(outer.astype(jnp.bfloat16))
        windowed = mm(joined(own_weights, 1), v_ref[:high, :])
        windowed = windowed + mm(joined(past_weights, 1), vp_ref[low:, :])
        near_rows = []
        for a in range(low // lane, high // lane):
            inside = slice(a * lane - low, (a + 1) * lane - low)
            mix = lw[:, a * lane : (a + 1) * lane]
            mix = joined([mix, jnp.zeros((lane - mix.shape[0], lane), jnp.float32)], 0).T
            parts = []
            for b in range(high // lane):
                scores = own[inside, b * lane : (b + 1) * lane]
                if b < a:
                    level = lane_bits + (a ^ b).bit_length()
                    parts.append((scores * mix[:, level : level + 1]).astype(jnp.bfloat16))
                elif b == a:
                    picked = jnp.take_along_axis(mix, table, axis=1)
                    parts.append((scores * picked).astype(jnp.bfloat16))
                else:
                    parts.append(jnp.zeros((lane, lane), jnp.bfloat16))
            near_rows.append(joined(parts, 1))
        near = mm(joined(near_rows, 0), v_ref[:high, :])
        out_ref[low:high, :] = windowed * (1.0 / total) + near


def attend(first, q, k, v, past_k, past_v, lw, table, head):
    rows, width = past_k.shape
    whole = pl.BlockSpec((rows, HEAD_DIM), lambda g, *_: (0, head + g))
    part = pl.BlockSpec((rows, HEAD_DIM), lambda g, *_: (0, g))
    qb = min(rows, 256)
    return pl.pallas_call(
        functools.partial(attend_kernel, qb),
        grid_spec=pltpu.PrefetchScalarGridSpec(
            num_scalar_prefetch=1,
            grid=(width // HEAD_DIM,),
            in_specs=[
                whole,
                whole,
                whole,
                part,
                part,
                pl.BlockSpec((1,) + lw.shape[1:], lambda g, *_: (head + g, 0, 0)),
                pl.BlockSpec(table.shape, lambda g, *_: (0, 0)),
            ],
            out_specs=part,
        ),
        out_shape=jax.ShapeDtypeStruct((rows, width), jnp.float32),
        compiler_params=pltpu.CompilerParams(vmem_limit_bytes=VMEM),
        name="attend",
    )(first, q, k, v, past_k, past_v, lw, table)


def far_kernel(near_n, slots, place_ref, q_ref, lw_ref, bucket_ref, part_ref, *rest):
    out_refs, scratch = rest[:slots], rest[slots]
    rows = q_ref.shape[0]
    lane = HEAD_DIM
    far_n = bucket_ref.shape[0]
    lw = lw_ref[0]
    proj = mm(q_ref[...], joined([bucket_ref[j, 0] for j in range(far_n)], 1))
    for a in range(rows // lane):
        inside = slice(a * lane, (a + 1) * lane)
        mix = lw[:, inside]
        mix = joined([mix, jnp.zeros((lane - mix.shape[0], lane), jnp.float32)], 0).T
        total = part_ref[inside, :]
        for j in range(far_n):
            total = total + proj[inside, j * lane : (j + 1) * lane] * mix[:, near_n + j : near_n + j + 1]
        scratch[inside, :] = total
    count = rows // slots
    for s in range(slots):
        start = pl.multiple_of(lax.rem(place_ref[0] + s, slots) * count, count)
        out_refs[s][...] = scratch[pl.ds(start, count), :].astype(jnp.bfloat16)


def far(place, q, lw, buckets, part, head, near_n, slots):
    rows, width = part.shape
    far_n = buckets.shape[0]
    count = rows // slots
    return pl.pallas_call(
        functools.partial(far_kernel, near_n, slots),
        grid_spec=pltpu.PrefetchScalarGridSpec(
            num_scalar_prefetch=1,
            grid=(width // HEAD_DIM,),
            in_specs=[
                pl.BlockSpec((rows, HEAD_DIM), lambda g, *_: (0, head + g)),
                pl.BlockSpec((1,) + lw.shape[1:], lambda g, *_: (head + g, 0, 0)),
                pl.BlockSpec((far_n, 1, HEAD_DIM, HEAD_DIM), lambda g, *_: (0, head + g, 0, 0)),
                pl.BlockSpec((rows, HEAD_DIM), lambda g, *_: (0, g)),
            ],
            out_specs=[pl.BlockSpec((count, HEAD_DIM), lambda g, *_: (0, g))] * slots,
            scratch_shapes=[pltpu.VMEM((rows, HEAD_DIM), jnp.float32)],
        ),
        out_shape=[jax.ShapeDtypeStruct((count, width), jnp.bfloat16)] * slots,
        name="far",
    )(place, q, lw, buckets, part)


def norm_kernel(slots, offsets, local_width, place_ref, gate_ref, gain_ref, *rest):
    pieces, (out_ref, gated) = rest[:-2], rest[-2:]
    square = None
    index = 0
    for s in range(slots):
        base = lax.rem(place_ref[0] + slots - s, slots) * local_width
        for offset in offsets:
            piece = pieces[index]
            index += 1
            cols = pl.ds(pl.multiple_of(base + offset, HEAD_DIM), piece.shape[1])
            gate = gate_ref[:, cols].astype(jnp.float32)
            value = piece[...].astype(jnp.float32) * (gate / (1.0 + jnp.exp(-gate)))
            gated[:, cols] = value
            here = jnp.sum(value * value, axis=1, keepdims=True)
            square = here if square is None else square + here
    factor = lax.rsqrt(square / gated.shape[1] + EPSILON)
    out_ref[...] = (gain_ref[...] * gated[...] * factor).astype(jnp.bfloat16)


def norm(place, gate, gain, pieces, slots, offsets, local_width):
    rows, width = gate.shape
    tile = min(rows, 64)
    return pl.pallas_call(
        functools.partial(norm_kernel, slots, offsets, local_width),
        grid_spec=pltpu.PrefetchScalarGridSpec(
            num_scalar_prefetch=1,
            grid=(rows // tile,),
            in_specs=[
                pl.BlockSpec((tile, width), lambda g, *_: (g, 0)),
                pl.BlockSpec((1, width), lambda g, *_: (0, 0)),
            ]
            + [pl.BlockSpec((tile, p.shape[1]), lambda g, *_: (g, 0)) for p in pieces],
            out_specs=pl.BlockSpec((tile, width), lambda g, *_: (g, 0)),
            scratch_shapes=[pltpu.VMEM((tile, width), jnp.float32)],
        ),
        out_shape=jax.ShapeDtypeStruct((rows, width), jnp.bfloat16),
        compiler_params=pltpu.CompilerParams(vmem_limit_bytes=VMEM),
        name="norm",
    )(place, gate, gain.reshape(1, width), *pieces)


def shifted(value, axis, steps, wrap=False):
    count = lax.axis_size(axis)
    pairs = [(i, (i + steps) % count) for i in range(count) if wrap or i + steps < count]
    return lax.ppermute(value, axis, pairs)


def from_partner(value, axis, level, only_up=False):
    count = lax.axis_size(axis)
    pairs = [(i, i ^ 1 << level) for i in range(count) if not only_up or not i >> level & 1]
    return lax.ppermute(value, axis, pairs)


def added(left, right):
    return (left.astype(jnp.float32) + right.astype(jnp.float32)).astype(jnp.bfloat16)


def far_buckets(states, place, far_n):
    bit = [(place >> level & 1).astype(jnp.bfloat16) for level in range(far_n)]
    other = from_partner(states, "seq", 0)
    first = other * bit[0]
    if far_n == 1:
        return first[None]
    half = HEAD_DIM // 2
    running = added(states, other)
    running = lax.dynamic_slice_in_dim(running, (place & 1) * half, half, 1)
    halves = []
    for level in range(1, far_n):
        last = level == far_n - 1
        other = from_partner(running, "seq", level, last)
        halves.append(other * bit[level])
        if not last:
            running = added(running, other)
    mine = jnp.stack(halves, 0)
    theirs = from_partner(mine, "seq", 0)
    odd = place & 1 == 1
    rest = jnp.concatenate([jnp.where(odd, theirs, mine), jnp.where(odd, mine, theirs)], 2)
    return jnp.concatenate([first[None], rest], 0)


def local(queries, key_vectors, values, level_weights, gate_branch, norm_gain):
    rows, local_width = queries.shape
    heads = local_width // HEAD_DIM
    near_n = rows.bit_length()
    levels = level_weights.shape[0]
    far_n = levels - near_n
    slots = lax.axis_size("heads")
    seq_place = lax.axis_index("seq")
    first = seq_place.reshape(1)
    heads_place = lax.axis_index("heads").reshape(1)
    chunk = max(1, heads // 4)
    starts = list(range(0, heads, chunk))

    states = block_states(key_vectors, values)
    past = []
    for start in starts:
        cols = slice(start * HEAD_DIM, (start + chunk) * HEAD_DIM)
        past.append(shifted((key_vectors[:, cols], values[:, cols]), "seq", 1))
    buckets = far_buckets(states, seq_place, far_n)

    coef = level_scale(jnp.arange(levels, dtype=jnp.int32)) * HEAD_DIM**-0.5
    lw = jnp.transpose(level_weights, (1, 0, 2)) * coef[None, :, None]
    pos = jnp.arange(HEAD_DIM, dtype=jnp.int32)
    differ = pos[:, None] ^ pos[None, :]
    table = sum((differ >> b > 0).astype(jnp.int32) for b in range(HEAD_DIM.bit_length()))
    table = jnp.where(pos[:, None] >= pos[None, :], table, HEAD_DIM - 1)

    kept = [[] for _ in range(slots)]
    for start, (past_k, past_v) in zip(starts, past):
        part = attend(first, queries, key_vectors, values, past_k, past_v, lw, table, start)
        pieces = far(heads_place, queries, lw, buckets, part, start, near_n, slots)
        for s in range(slots):
            kept[s].append(pieces[s] if s == 0 else shifted(pieces[s], "heads", s, True))
    pieces = [piece for group in kept for piece in group]
    offsets = tuple(start * HEAD_DIM for start in starts)
    return norm(heads_place, gate_branch, norm_gain, pieces, slots, offsets, local_width)


def solution(mesh):
    return jax.shard_map(
        local,
        mesh=mesh,
        in_specs=(
            P("seq", "heads"),
            P("seq", "heads"),
            P("seq", "heads"),
            P(None, "heads", "seq"),
            P(("seq", "heads"), None),
            P(),
        ),
        out_specs=P(("seq", "heads"), None),
        check_vma=False,
    )
```

time: 227 us -> 132 us (0.58)
  other arithmetic: 82.4 us -> 8.8 us
  matrix products: 70.1 us -> 0 us
  Pallas kernels: 0 us -> 54.8 us
  blocking collectives: 27.8 us -> 0 us
  starting transfers between devices: 20.5 us -> 47 us
  local copies, waits for them, and re-layouts: 22.4 us -> 6.34 us
  waiting for transfers between devices: 3.03 us -> 12.7 us
    dot_general x5 -> x0, matrix products: 70.1 us -> none  [the longest x1 24.7 us: local(): jnp.einsum('hqk,khd->qhd', near_weights, context_values[WINDOW:WINDOW + q...]
    pallas_call x0 -> x10, Pallas kernels: none -> 54.8 us  [the longest x4 26.7 us: attend(): pl.pallas_call(functools.partial(attend_kernel, qb), grid_spec=pltpu.Pref...]
    sub x1 -> x0, other arithmetic: 34.6 us -> none  [local(): exp_scores = jnp.where(in_window[None], jnp.exp(scores - row_max), 0.0)]
    all_to_all x1 -> x0, blocking collectives: 27.8 us -> none  [local(): lax.all_to_all(mixed, 'heads', split_axis=0, concat_axis=1, tiled=True)]
    ppermute x6 -> x17, starting transfers between devices: 20.5 us -> 47 us  [the longest x12 37.9 us: shifted(): return lax.ppermute(value, axis, pairs)]
    eq x5 -> x0, other arithmetic: 11.1 us -> none  [local(): level_table[None] == level_id]
    ppermute x6 -> x17, waiting for transfers between devices: 3.03 us -> 12.7 us  [the longest x5 6.82 us: from_partner(): return lax.ppermute(value, axis, pairs)]
    convert_element_type x3 -> x0, local copies, waits for them, and re-layouts: 8.61 us -> none  [the longest x1 5.79 us: local(): token_rows.astype(jnp.float32)]
  transfers between devices with their start and end apart: 6 -> 17, of which waited for: 2 -> 5; matrix products, arithmetic and copies ran while one was open for 57% -> 6% of each run, Pallas kernels for 0% -> 32%
where the time goes in v1:
time: 132 us; the launch traced here: 130 us
  Pallas kernels  54.8 us (42%)
  starting transfers between devices  47 us (36%)
  waiting for transfers between devices  12.7 us (10%)
  other arithmetic  8.8 us (7%)
  local copies, waits for them, and re-layouts  6.34 us (5%)
    ppermute x12, starting transfers between devices, shifted(): return lax.ppermute(value, axis, pairs)  37.9 us
    pallas_call x4, Pallas kernels, attend(): pl.pallas_call(functools.partial(attend_kernel, qb), grid_spec=pltpu.Pref...  26.7 us
    pallas_call x4, Pallas kernels, far(): pl.pallas_call(functools.partial(far_kernel, near_n, slots), grid_spec=pl...  19.1 us
    ppermute x5, starting transfers between devices, from_partner(): return lax.ppermute(value, axis, pairs)  9.09 us
    ppermute x5, waiting for transfers between devices, from_partner(): return lax.ppermute(value, axis, pairs)  6.82 us
    ppermute x12, waiting for transfers between devices, shifted(): return lax.ppermute(value, axis, pairs)  5.84 us
    pallas_call x1, Pallas kernels, block_states(): pl.pallas_call(functools.partial(state_kernel, step), grid=(heads // step...  4.64 us
    pallas_call x1, Pallas kernels, norm(): pl.pallas_call(functools.partial(norm_kernel, slots, offsets, local_width...  4.34 us
  transfers between devices with their start and end apart: 17, of which 5 were waited for; matrix products, arithmetic and copies ran while one was open for 6% of the time, Pallas kernels for 32%

profile of v1, /device:TPU:0, one launch (start us, length us, event | category | flops | bytes accessed | tf_op | source)
XLA Modules:
  0.0 129.9 jit_solution(4105284181862048382)
XLA Ops:
  0.0 4.6 %block_states.1 = bf16[16,128,128]{2,1,0:T(8,128)(2,1)} custom-call(bf16[512,2048]{1,0:T(8,128)(2,1)} %k_ref.9, bf16[512,2048]{1,0:T(8,128)(2,1)} %v_ref.9), custom_call_target="tpu_custom_call" | custom-call | tf_op jit(solution)/shard_map/block_states/pallas_call | solution.py:43
  4.6 0.5 collective-permute-start
  5.1 1.7 %collective-permute-done = bf16[16,128,128]{2,1,0:T(8,128)(2,1)S(1)} collective-permute-done((bf16[16,128,128]{2,1,0:T(8,128)(2,1)}, bf16[16,128,128]{2,1,0:T(8,128)(2,1)S(1)}, u32[]{:S(2)}, u32[]{:S(2)}) %collective-permute-start) | collective-permute-done | bytes 524320 | tf_op jit(solution)/shard_map/ppermute | solution.py:231
  6.9 1.2 add_convert_fusion.2
  8.1 3.0 %collective-permute-start.1 = (bf16[16,64,128]{2,1,0:T(8,128)(2,1)S(1)}, bf16[16,64,128]{2,1,0:T(8,128)(2,1)S(1)}, u32[]{:S(2)}, u32[]{:S(2)}) collective-permute-start(bf16[16,64,128]{2,1,0:T(8,128)(2,1)S(1)} %add_convert_fusion.2), channel_id=1, source_target_pairs={{0,2},{1,3},{2,0},{3,1},{4,6},{5,7},{6,4},{7,5},{8,10},{9,11},{10,... | collective-permute-start | bytes 786440 | tf_op jit(solution)/shard_map/ppermute | solution.py:231
  11.0 1.4 %fusion.18 = (bf16[512,512]{1,0:T(8,128)(2,1)}, bf16[512,512]{1,0:T(8,128)(2,1)}, bf16[512,512]{1,0:T(8,128)(2,1)}, bf16[512,512]{1,0:T(8,128)(2,1)}) fusion(bf16[512,2048]{1,0:T(8,128)(2,1)S(1)} %copy-done.14), kind=kLoop, calls=%fused_computation.34 | loop fusion | bytes 4194304 | tf_op jit(solution)/shard_map/slice | solution.py:278
  12.4 1.8 %collective-permute-start.11 = (bf16[512,512]{1,0:T(8,128)(2,1)}, bf16[512,512]{1,0:T(8,128)(2,1)S(1)}, u32[]{:S(2)}, u32[]{:S(2)}) collective-permute-start(bf16[512,512]{1,0:T(8,128)(2,1)} %get-tuple-element.25), channel_id=1, source_target_pairs={{0,1},{1,2},{2,3},{3,4},{4,5},{5,6},{6,7},{7,8},{8,9},{9,10},{10,1... | collective-permute-start | bytes 1572872 | tf_op jit(solution)/shard_map/ppermute | solution.py:225
  14.2 2.2 %collective-permute-start.9 = (bf16[512,512]{1,0:T(8,128)(2,1)}, bf16[512,512]{1,0:T(8,128)(2,1)S(1)}, u32[]{:S(2)}, u32[]{:S(2)}) collective-permute-start(bf16[512,512]{1,0:T(8,128)(2,1)} %get-tuple-element.26), channel_id=1, source_target_pairs={{0,1},{1,2},{2,3},{3,4},{4,5},{5,6},{6,7},{7,8},{8,9},{9,10},{10,1... | collective-permute-start | bytes 1572872 | tf_op jit(solution)/shard_map/ppermute | solution.py:225
  16.4 1.3 collective-permute-done.1
  17.7 0.1 add_convert_fusion.1
  17.8 1.8 %collective-permute-start.2 = (bf16[16,64,128]{2,1,0:T(8,128)(2,1)S(1)}, bf16[16,64,128]{2,1,0:T(8,128)(2,1)S(1)}, u32[]{:S(2)}, u32[]{:S(2)}) collective-permute-start(bf16[16,64,128]{2,1,0:T(8,128)(2,1)S(1)} %add_convert_fusion.1), channel_id=1, source_target_pairs={{0,4},{1,5},{2,6},{3,7},{4,0},{5,1},{6,2},{7,3},{8,12},{9,13},{10,... | collective-permute-start | bytes 786440 | tf_op jit(solution)/shard_map/ppermute | solution.py:231
  19.6 1.4 %fusion.17 = (bf16[512,512]{1,0:T(8,128)(2,1)}, bf16[512,512]{1,0:T(8,128)(2,1)}, bf16[512,512]{1,0:T(8,128)(2,1)}, bf16[512,512]{1,0:T(8,128)(2,1)}) fusion(bf16[512,2048]{1,0:T(8,128)(2,1)S(1)} %copy-done.15), kind=kLoop, calls=%fused_computation.33 | loop fusion | bytes 4194304 | tf_op jit(solution)/shard_map/slice | solution.py:278
  20.9 2.1 %collective-permute-start.12 = (bf16[512,512]{1,0:T(8,128)(2,1)}, bf16[512,512]{1,0:T(8,128)(2,1)}, u32[]{:S(2)}, u32[]{:S(2)}) collective-permute-start(bf16[512,512]{1,0:T(8,128)(2,1)} %get-tuple-element.21), channel_id=1, source_target_pairs={{0,1},{1,2},{2,3},{3,4},{4,5},{5,6},{6,7},{7,8},{8,9},{9,10},{10,1... | collective-permute-start | bytes 1572872 | tf_op jit(solution)/shard_map/ppermute | solution.py:225
  23.0 4.9 %collective-permute-start.10 = (bf16[512,512]{1,0:T(8,128)(2,1)}, bf16[512,512]{1,0:T(8,128)(2,1)}, u32[]{:S(2)}, u32[]{:S(2)}) collective-permute-start(bf16[512,512]{1,0:T(8,128)(2,1)} %get-tuple-element.22), channel_id=1, source_target_pairs={{0,1},{1,2},{2,3},{3,4},{4,5},{5,6},{6,7},{7,8},{8,9},{9,10},{10,1... | collective-permute-start | bytes 1572872 | tf_op jit(solution)/shard_map/ppermute | solution.py:225
  28.0 0.7 copy-done.23
  28.7 0.1 add_convert_fusion
  28.8 3.9 %collective-permute-start.3 = (bf16[16,64,128]{2,1,0:T(8,128)(2,1)S(1)}, bf16[16,64,128]{2,1,0:T(8,128)(2,1)S(1)}, u32[]{:S(2)}, u32[]{:S(2)}) collective-permute-start(bf16[16,64,128]{2,1,0:T(8,128)(2,1)S(1)} %add_convert_fusion), channel_id=1, source_target_pairs={{0,8},{1,9},{2,10},{3,11},{4,12},{5,13},{6,14},{7,15},{16,24},{17,... | collective-permute-start | bytes 786440 | tf_op jit(solution)/shard_map/ppermute | solution.py:231
  32.7 1.0 multiply_bitcast_fusion.3
  33.6 1.0 multiply_bitcast_fusion.2
  34.6 3.8 %collective-permute-done.3 = bf16[16,64,128]{2,1,0:T(8,128)(2,1)S(1)} collective-permute-done((bf16[16,64,128]{2,1,0:T(8,128)(2,1)S(1)}, bf16[16,64,128]{2,1,0:T(8,128)(2,1)S(1)}, u32[]{:S(2)}, u32[]{:S(2)}) %collective-permute-start.3) | collective-permute-done | bytes 262176 | tf_op jit(solution)/shard_map/ppermute | solution.py:231
  38.4 1.0 pad_maximum_fusion
  39.4 3.2 %collective-permute-start.7 = (bf16[512,512]{1,0:T(8,128)(2,1)}, bf16[512,512]{1,0:T(8,128)(2,1)}, u32[]{:S(2)}, u32[]{:S(2)}) collective-permute-start(bf16[512,512]{1,0:T(8,128)(2,1)} %get-tuple-element.27), channel_id=1, source_target_pairs={{0,1},{1,2},{2,3},{3,4},{4,5},{5,6},{6,7},{7,8},{8,9},{9,10},{10,1... | collective-permute-start | bytes 1572872 | tf_op jit(solution)/shard_map/ppermute | solution.py:225
  42.7 0.9 copy-done.7
  43.5 15.0 %collective-permute-start.5 = (bf16[512,512]{1,0:T(8,128)(2,1)}, bf16[512,512]{1,0:T(8,128)(2,1)}, u32[]{:S(2)}, u32[]{:S(2)}) collective-permute-start(bf16[512,512]{1,0:T(8,128)(2,1)} %get-tuple-element.28), channel_id=1, source_target_pairs={{0,1},{1,2},{2,3},{3,4},{4,5},{5,6},{6,7},{7,8},{8,9},{9,10},{10,1... | collective-permute-start | bytes 1572872 | tf_op jit(solution)/shard_map/ppermute | solution.py:225
  58.6 2.1 %collective-permute-start.8 = (bf16[512,512]{1,0:T(8,128)(2,1)}, bf16[512,512]{1,0:T(8,128)(2,1)}, u32[]{:S(2)}, u32[]{:S(2)}) collective-permute-start(bf16[512,512]{1,0:T(8,128)(2,1)} %get-tuple-element.23), channel_id=1, source_target_pairs={{0,1},{1,2},{2,3},{3,4},{4,5},{5,6},{6,7},{7,8},{8,9},{9,10},{10,1... | collective-permute-start | bytes 1572872 | tf_op jit(solution)/shard_map/ppermute | solution.py:225
  60.7 2.1 %collective-permute-start.6 = (bf16[512,512]{1,0:T(8,128)(2,1)}, bf16[512,512]{1,0:T(8,128)(2,1)}, u32[]{:S(2)}, u32[]{:S(2)}) collective-permute-start(bf16[512,512]{1,0:T(8,128)(2,1)} %get-tuple-element.24), channel_id=1, source_target_pairs={{0,1},{1,2},{2,3},{3,4},{4,5},{5,6},{6,7},{7,8},{8,9},{9,10},{10,1... | collective-permute-start | bytes 1572872 | tf_op jit(solution)/shard_map/ppermute | solution.py:225
  62.8 0.1 add_select_fusion.table_ref
  62.9 1.3 fusion.lw_ref
  64.2 6.7 %attend.7.part_ref = f32[512,512]{1,0:T(8,128)S(1)} custom-call(s32[1]{0:T(128)} %bitcast.7.first_ref, bf16[512,2048]{1,0:T(8,128)(2,1)S(1)} %copy-done, bf16[512,2048]{1,0:T(8,128)(2,1)} %k_ref.9, bf16[512,2048]{1,0:T(8,128)(2,1)} %v_ref.9, bf16[512,512]{1,0:T(8,128)(2,1)S(1)} %collective-permute-done.11.kp_ref, ...), custom_call_target="tpu_custom_call" | custom-call | tf_op jit(solution)/shard_map/attend/pallas_call | solution.py:115
  70.9 1.0 copy-done.4
  71.9 6.4 %attend.6.part_ref = f32[512,512]{1,0:T(8,128)S(1)} custom-call(s32[1]{0:T(128)} %bitcast.7.first_ref, bf16[512,2048]{1,0:T(8,128)(2,1)S(1)} %copy-done, bf16[512,2048]{1,0:T(8,128)(2,1)} %k_ref.9, bf16[512,2048]{1,0:T(8,128)(2,1)} %v_ref.9, bf16[512,512]{1,0:T(8,128)(2,1)S(1)} %copy-done.8, bf16[512,512]{1,0:T(8,128)(2,1)} %collective-permute-done.10.vp_ref, ...), custom_call_target="tpu_custom_call" | custom-call | tf_op jit(solution)/shard_map/attend/pallas_call | solution.py:115
  78.3 6.8 %attend.5.part_ref = f32[512,512]{1,0:T(8,128)S(1)} custom-call(s32[1]{0:T(128)} %bitcast.7.first_ref, bf16[512,2048]{1,0:T(8,128)(2,1)S(1)} %copy-done, bf16[512,2048]{1,0:T(8,128)(2,1)} %k_ref.9, bf16[512,2048]{1,0:T(8,128)(2,1)} %v_ref.9, bf16[512,512]{1,0:T(8,128)(2,1)} %collective-permute-done.7.kp_ref, bf16[512,512]{1,0:T(8,128)(2,1)} %collective-permute-done.8.vp_ref, ...), custom_call_target="tpu_custom_call" | custom-call | tf_op jit(solution)/shard_map/attend/pallas_call | solution.py:115
  85.2 6.9 %attend.4.part_ref = f32[512,512]{1,0:T(8,128)S(1)} custom-call(s32[1]{0:T(128)} %bitcast.7.first_ref, bf16[512,2048]{1,0:T(8,128)(2,1)S(1)} %copy-done, bf16[512,2048]{1,0:T(8,128)(2,1)} %k_ref.9, bf16[512,2048]{1,0:T(8,128)(2,1)} %v_ref.9, bf16[512,512]{1,0:T(8,128)(2,1)} %collective-permute-done.5.kp_ref, bf16[512,512]{1,0:T(8,128)(2,1)} %collective-permute-done.6.vp_ref, ...), custom_call_target="tpu_custom_call" | custom-call | tf_op jit(solution)/shard_map/attend/pallas_call | solution.py:115
  92.2 1.6 %broadcast_select_fusion.1 = (bf16[3,16,64,128]{3,2,1,0:T(8,128)(2,1)S(1)}, bf16[3,16,64,128]{3,2,1,0:T(8,128)(2,1)S(1)}) fusion(bf16[3,16,64,128]{3,2,1,0:T(8,128)(2,1)} %collective-permute-done.4, pred[]{:T(512)S(6)} %eq.3, bf16[1,16,64,128]{3,2,1,0:T(8,128)(2,1)S(1)} %copy-done.19, bf16[1,16,64,128]{3,2,1,0:T(8,128)(2,1)S(1)} %copy-done.17, ...), kind=kLoop, calls=%fused_computation.3 | loop fusion | flops 1572864 | bytes 3145729 | tf_op jit(solution)/shard_map/jit(_where)/select_n | solution.py:257
  93.7 1.5 %maximum_maximum_fusion.bucket_ref = bf16[4,16,128,128]{3,2,1,0:T(8,128)(2,1)} fusion(bf16[3,16,64,128]{3,2,1,0:T(8,128)(2,1)S(1)} %get-tuple-element.30, bf16[3,16,64,128]{3,2,1,0:T(8,128)(2,1)S(1)} %get-tuple-element.29, bf16[1,16,128,128]{3,2,1,0:T(8,128)(2,1)S(1)} %multiply_bitcast_fusion), kind=kLoop, calls=%fused_computation | loop fusion | flops 6291456 | bytes 4194304 | tf_op jit(solution)/shard_map/concatenate | solution.py:258
  95.3 4.8 %far.7 = (bf16[256,512]{1,0:T(8,128)(2,1)}, bf16[256,512]{1,0:T(8,128)(2,1)}) custom-call(s32[1]{0:T(128)} %bitcast.place_ref, bf16[512,2048]{1,0:T(8,128)(2,1)} %q_ref.15, f32[16,14,512]{2,1,0:T(8,128)} %copy-done.1, bf16[4,16,128,128]{3,2,1,0:T(8,128)(2,1)} %maximum_maximum_fusion.bucket_ref, f32[512,512]{1,0:T(8,128)} %copy-done.4), custom_call_target="tpu_custom_call" | custom-call | tf_op jit(solution)/shard_map/far/pallas_call | solution.py:162
  100.0 1.5 %collective-permute-start.16 = (bf16[256,512]{1,0:T(8,128)(2,1)}, bf16[256,512]{1,0:T(8,128)(2,1)S(1)}, u32[]{:S(2)}, u32[]{:S(2)}) collective-permute-start(bf16[256,512]{1,0:T(8,128)(2,1)} %get-tuple-element.20), channel_id=1, source_target_pairs={{0,16},{16,0},{1,17},{17,1},{2,18},{18,2},{3,19},{19,3},{4,20},{20... | collective-permute-start | bytes 786440 | tf_op jit(solution)/shard_map/ppermute | solution.py:225
  101.6 4.8 %far.6 = (bf16[256,512]{1,0:T(8,128)(2,1)}, bf16[256,512]{1,0:T(8,128)(2,1)}) custom-call(s32[1]{0:T(128)} %bitcast.place_ref, bf16[512,2048]{1,0:T(8,128)(2,1)} %q_ref.15, f32[16,14,512]{2,1,0:T(8,128)} %copy-done.1, bf16[4,16,128,128]{3,2,1,0:T(8,128)(2,1)} %maximum_maximum_fusion.bucket_ref, f32[512,512]{1,0:T(8,128)} %copy-done.2), custom_call_target="tpu_custom_call" | custom-call | tf_op jit(solution)/shard_map/far/pallas_call | solution.py:162
  106.3 0.5 collective-permute-start.15
  106.9 4.8 %far.5 = (bf16[256,512]{1,0:T(8,128)(2,1)}, bf16[256,512]{1,0:T(8,128)(2,1)}) custom-call(s32[1]{0:T(128)} %bitcast.place_ref, bf16[512,2048]{1,0:T(8,128)(2,1)} %q_ref.15, f32[16,14,512]{2,1,0:T(8,128)} %copy-done.1, bf16[4,16,128,128]{3,2,1,0:T(8,128)(2,1)} %maximum_maximum_fusion.bucket_ref, f32[512,512]{1,0:T(8,128)} %copy-done.3), custom_call_target="tpu_custom_call" | custom-call | tf_op jit(solution)/shard_map/far/pallas_call | solution.py:162
  111.7 0.0 copy-start.13
  111.7 1.6 %collective-permute-start.14 = (bf16[256,512]{1,0:T(8,128)(2,1)}, bf16[256,512]{1,0:T(8,128)(2,1)}, u32[]{:S(2)}, u32[]{:S(2)}) collective-permute-start(bf16[256,512]{1,0:T(8,128)(2,1)} %get-tuple-element.18), channel_id=1, source_target_pairs={{0,16},{16,0},{1,17},{17,1},{2,18},{18,2},{3,19},{19,3},{4,20},{20... | collective-permute-start | bytes 786440 | tf_op jit(solution)/shard_map/ppermute | solution.py:225
  113.2 4.8 %far.4 = (bf16[256,512]{1,0:T(8,128)(2,1)}, bf16[256,512]{1,0:T(8,128)(2,1)}) custom-call(s32[1]{0:T(128)} %bitcast.place_ref, bf16[512,2048]{1,0:T(8,128)(2,1)} %q_ref.15, f32[16,14,512]{2,1,0:T(8,128)} %copy-done.1, bf16[4,16,128,128]{3,2,1,0:T(8,128)(2,1)} %maximum_maximum_fusion.bucket_ref, f32[512,512]{1,0:T(8,128)} %copy-done.5), custom_call_target="tpu_custom_call" | custom-call | tf_op jit(solution)/shard_map/far/pallas_call | solution.py:162
  118.0 0.8 collective-permute-start.13
  118.8 0.3 collective-permute-done.14.rest_5_
  119.1 5.5 %collective-permute-done.13.rest_4_ = bf16[256,512]{1,0:T(8,128)(2,1)S(1)} collective-permute-done((bf16[256,512]{1,0:T(8,128)(2,1)}, bf16[256,512]{1,0:T(8,128)(2,1)S(1)}, u32[]{:S(2)}, u32[]{:S(2)}) %collective-permute-start.13) | collective-permute-done | bytes 262176 | tf_op jit(solution)/shard_map/ppermute | solution.py:225
  124.6 0.9 copy-done.12
  125.6 4.3 %norm.1 = bf16[256,4096]{1,0:T(8,128)(2,1)} custom-call(s32[1]{0:T(128)} %bitcast.place_ref, bf16[256,4096]{1,0:T(8,128)(2,1)S(1)} %copy-done.6, f32[1,4096]{1,0:T(1,128)S(1)} %bitcast.13, bf16[256,512]{1,0:T(8,128)(2,1)S(1)} %copy-done.12, bf16[256,512]{1,0:T(8,128)(2,1)S(1)} %copy-done.11, bf16[256,512]{1,0:T(8,128)(2,1)S(1)} %copy-done.10, ...), custom_call_target="tpu_custom_call" | custom-call | tf_op jit(solution)/shard_map/norm/pallas_call | solution.py:203
  (59 shorter events, 0.2 us)
Async XLA Ops:
  0.0 11.0 %copy-start.14 = (bf16[512,2048]{1,0:T(8,128)(2,1)S(1)}, bf16[512,2048]{1,0:T(8,128)(2,1)}, u32[]{:S(2)}) copy-start(bf16[512,2048]{1,0:T(8,128)(2,1)} %k_ref.9) | copy-start | bytes 6291460
  4.6 2.2 %collective-permute-start = (bf16[16,128,128]{2,1,0:T(8,128)(2,1)}, bf16[16,128,128]{2,1,0:T(8,128)(2,1)S(1)}, u32[]{:S(2)}, u32[]{:S(2)}) collective-permute-start(bf16[16,128,128]{2,1,0:T(8,128)(2,1)} %block_states.1), channel_id=1, source_target_pairs={{0,1},{1,0},{2,3},{3,2},{4,5},{5,4},{6,7},{7,6},{8,9},{9,8},{10,11... | collective-permute-start | bytes 1572872 | tf_op jit(solution)/shard_map/ppermute | solution.py:231
  6.9 5.6 %copy-start.20 = (bf16[16,128,128]{2,1,0:T(8,128)(2,1)}, bf16[16,128,128]{2,1,0:T(8,128)(2,1)S(1)}, u32[]{:S(2)}) copy-start(bf16[16,128,128]{2,1,0:T(8,128)(2,1)S(1)} %collective-permute-done) | copy-start | bytes 1572868
  8.0 11.5 %copy-start.15 = (bf16[512,2048]{1,0:T(8,128)(2,1)S(1)}, bf16[512,2048]{1,0:T(8,128)(2,1)}, u32[]{:S(2)}) copy-start(bf16[512,2048]{1,0:T(8,128)(2,1)} %v_ref.9) | copy-start | bytes 6291460
  8.1 9.6 %collective-permute-start.1 = (bf16[16,64,128]{2,1,0:T(8,128)(2,1)S(1)}, bf16[16,64,128]{2,1,0:T(8,128)(2,1)S(1)}, u32[]{:S(2)}, u32[]{:S(2)}) collective-permute-start(bf16[16,64,128]{2,1,0:T(8,128)(2,1)S(1)} %add_convert_fusion.2), channel_id=1, source_target_pairs={{0,2},{1,3},{2,0},{3,1},{4,6},{5,7},{6,4},{7,5},{8,10},{9,11},{10,... | collective-permute-start | bytes 786440 | tf_op jit(solution)/shard_map/ppermute | solution.py:231
  12.4 27.0 %collective-permute-start.11 = (bf16[512,512]{1,0:T(8,128)(2,1)}, bf16[512,512]{1,0:T(8,128)(2,1)S(1)}, u32[]{:S(2)}, u32[]{:S(2)}) collective-permute-start(bf16[512,512]{1,0:T(8,128)(2,1)} %get-tuple-element.25), channel_id=1, source_target_pairs={{0,1},{1,2},{2,3},{3,4},{4,5},{5,6},{6,7},{7,8},{8,9},{9,10},{10,1... | collective-permute-start | bytes 1572872 | tf_op jit(solution)/shard_map/ppermute | solution.py:225
  14.2 28.5 %collective-permute-start.9 = (bf16[512,512]{1,0:T(8,128)(2,1)}, bf16[512,512]{1,0:T(8,128)(2,1)S(1)}, u32[]{:S(2)}, u32[]{:S(2)}) collective-permute-start(bf16[512,512]{1,0:T(8,128)(2,1)} %get-tuple-element.26), channel_id=1, source_target_pairs={{0,1},{1,2},{2,3},{3,4},{4,5},{5,6},{6,7},{7,8},{8,9},{9,10},{10,1... | collective-permute-start | bytes 1572872 | tf_op jit(solution)/shard_map/ppermute | solution.py:225
  17.7 3.2 %copy-start.22 = (bf16[16,64,128]{2,1,0:T(8,128)(2,1)}, bf16[16,64,128]{2,1,0:T(8,128)(2,1)S(1)}, u32[]{:S(2)}) copy-start(bf16[16,64,128]{2,1,0:T(8,128)(2,1)S(1)} %collective-permute-done.1) | copy-start | bytes 786436
  17.8 10.2 %collective-permute-start.2 = (bf16[16,64,128]{2,1,0:T(8,128)(2,1)S(1)}, bf16[16,64,128]{2,1,0:T(8,128)(2,1)S(1)}, u32[]{:S(2)}, u32[]{:S(2)}) collective-permute-start(bf16[16,64,128]{2,1,0:T(8,128)(2,1)S(1)} %add_convert_fusion.1), channel_id=1, source_target_pairs={{0,4},{1,5},{2,6},{3,7},{4,0},{5,1},{6,2},{7,3},{8,12},{9,13},{10,... | collective-permute-start | bytes 786440 | tf_op jit(solution)/shard_map/ppermute | solution.py:231
  20.9 37.7 %collective-permute-start.12 = (bf16[512,512]{1,0:T(8,128)(2,1)}, bf16[512,512]{1,0:T(8,128)(2,1)}, u32[]{:S(2)}, u32[]{:S(2)}) collective-permute-start(bf16[512,512]{1,0:T(8,128)(2,1)} %get-tuple-element.21), channel_id=1, source_target_pairs={{0,1},{1,2},{2,3},{3,4},{4,5},{5,6},{6,7},{7,8},{8,9},{9,10},{10,1... | collective-permute-start | bytes 1572872 | tf_op jit(solution)/shard_map/ppermute | solution.py:225
  23.0 37.7 %collective-permute-start.10 = (bf16[512,512]{1,0:T(8,128)(2,1)}, bf16[512,512]{1,0:T(8,128)(2,1)}, u32[]{:S(2)}, u32[]{:S(2)}) collective-permute-start(bf16[512,512]{1,0:T(8,128)(2,1)} %get-tuple-element.22), channel_id=1, source_target_pairs={{0,1},{1,2},{2,3},{3,4},{4,5},{5,6},{6,7},{7,8},{8,9},{9,10},{10,1... | collective-permute-start | bytes 1572872 | tf_op jit(solution)/shard_map/ppermute | solution.py:225
  28.0 0.7 copy-start.23
  28.8 35.4 %copy-start = (bf16[512,2048]{1,0:T(8,128)(2,1)S(1)}, bf16[512,2048]{1,0:T(8,128)(2,1)}, u32[]{:S(2)}) copy-start(bf16[512,2048]{1,0:T(8,128)(2,1)} %q_ref.15) | copy-start | bytes 6291460
  28.8 9.6 %collective-permute-start.3 = (bf16[16,64,128]{2,1,0:T(8,128)(2,1)S(1)}, bf16[16,64,128]{2,1,0:T(8,128)(2,1)S(1)}, u32[]{:S(2)}, u32[]{:S(2)}) collective-permute-start(bf16[16,64,128]{2,1,0:T(8,128)(2,1)S(1)} %add_convert_fusion), channel_id=1, source_target_pairs={{0,8},{1,9},{2,10},{3,11},{4,12},{5,13},{6,14},{7,15},{16,24},{17,... | collective-permute-start | bytes 786440 | tf_op jit(solution)/shard_map/ppermute | solution.py:231
  34.6 8.0 %copy-start.16 = (bf16[1,16,64,128]{3,2,1,0:T(8,128)(2,1)}, bf16[1,16,64,128]{3,2,1,0:T(8,128)(2,1)S(1)}, u32[]{:S(2)}) copy-start(bf16[1,16,64,128]{3,2,1,0:T(8,128)(2,1)S(1)} %multiply_bitcast_fusion.2) | copy-start | bytes 786436
  38.4 5.1 %copy-start.18 = (bf16[1,16,64,128]{3,2,1,0:T(8,128)(2,1)}, bf16[1,16,64,128]{3,2,1,0:T(8,128)(2,1)S(1)}, u32[]{:S(2)}) copy-start(bf16[1,16,64,128]{3,2,1,0:T(8,128)(2,1)S(1)} %multiply_bitcast_fusion.1) | copy-start | bytes 786436
  39.4 52.7 %collective-permute-start.4 = (bf16[3,16,64,128]{3,2,1,0:T(8,128)(2,1)}, bf16[3,16,64,128]{3,2,1,0:T(8,128)(2,1)}, u32[]{:S(2)}, u32[]{:S(2)}) collective-permute-start(bf16[3,16,64,128]{3,2,1,0:T(8,128)(2,1)} %pad_maximum_fusion), channel_id=1, source_target_pairs={{0,1},{1,0},{2,3},{3,2},{4,5},{5,4},{6,7},{7,6},{8,9},{9,8},{10,11... | collective-permute-start | bytes 2359304 | tf_op jit(solution)/shard_map/ppermute | solution.py:231
  39.4 38.9 %collective-permute-start.7 = (bf16[512,512]{1,0:T(8,128)(2,1)}, bf16[512,512]{1,0:T(8,128)(2,1)}, u32[]{:S(2)}, u32[]{:S(2)}) collective-permute-start(bf16[512,512]{1,0:T(8,128)(2,1)} %get-tuple-element.27), channel_id=1, source_target_pairs={{0,1},{1,2},{2,3},{3,4},{4,5},{5,6},{6,7},{7,8},{8,9},{9,10},{10,1... | collective-permute-start | bytes 1572872 | tf_op jit(solution)/shard_map/ppermute | solution.py:225
  42.7 0.9 copy-start.7
  43.5 41.6 %collective-permute-start.5 = (bf16[512,512]{1,0:T(8,128)(2,1)}, bf16[512,512]{1,0:T(8,128)(2,1)}, u32[]{:S(2)}, u32[]{:S(2)}) collective-permute-start(bf16[512,512]{1,0:T(8,128)(2,1)} %get-tuple-element.28), channel_id=1, source_target_pairs={{0,1},{1,2},{2,3},{3,4},{4,5},{5,6},{6,7},{7,8},{8,9},{9,10},{10,1... | collective-permute-start | bytes 1572872 | tf_op jit(solution)/shard_map/ppermute | solution.py:225
  58.6 19.7 %collective-permute-start.8 = (bf16[512,512]{1,0:T(8,128)(2,1)}, bf16[512,512]{1,0:T(8,128)(2,1)}, u32[]{:S(2)}, u32[]{:S(2)}) collective-permute-start(bf16[512,512]{1,0:T(8,128)(2,1)} %get-tuple-element.23), channel_id=1, source_target_pairs={{0,1},{1,2},{2,3},{3,4},{4,5},{5,6},{6,7},{7,8},{8,9},{9,10},{10,1... | collective-permute-start | bytes 1572872 | tf_op jit(solution)/shard_map/ppermute | solution.py:225
  60.7 24.4 %collective-permute-start.6 = (bf16[512,512]{1,0:T(8,128)(2,1)}, bf16[512,512]{1,0:T(8,128)(2,1)}, u32[]{:S(2)}, u32[]{:S(2)}) collective-permute-start(bf16[512,512]{1,0:T(8,128)(2,1)} %get-tuple-element.24), channel_id=1, source_target_pairs={{0,1},{1,2},{2,3},{3,4},{4,5},{5,6},{6,7},{7,8},{8,9},{9,10},{10,1... | collective-permute-start | bytes 1572872 | tf_op jit(solution)/shard_map/ppermute | solution.py:225
  64.2 21.0 %copy-start.1 = (f32[16,14,512]{2,1,0:T(8,128)}, f32[16,14,512]{2,1,0:T(8,128)S(1)}, u32[]{:S(2)}) copy-start(f32[16,14,512]{2,1,0:T(8,128)S(1)} %fusion.lw_ref) | copy-start | bytes 1376260
  64.2 7.7 %copy-start.8 = (bf16[512,512]{1,0:T(8,128)(2,1)S(1)}, bf16[512,512]{1,0:T(8,128)(2,1)}, u32[]{:S(2)}) copy-start(bf16[512,512]{1,0:T(8,128)(2,1)} %copy-done.7) | copy-start | bytes 1572868
  70.9 1.0 copy-start.4
  78.3 6.8 %copy-start.2 = (f32[512,512]{1,0:T(8,128)}, f32[512,512]{1,0:T(8,128)S(1)}, u32[]{:S(2)}) copy-start(f32[512,512]{1,0:T(8,128)S(1)} %attend.6.part_ref) | copy-start | bytes 3145732
  85.1 7.0 %copy-start.3 = (f32[512,512]{1,0:T(8,128)}, f32[512,512]{1,0:T(8,128)S(1)}, u32[]{:S(2)}) copy-start(f32[512,512]{1,0:T(8,128)S(1)} %attend.5.part_ref) | copy-start | bytes 3145732
  85.1 7.0 %copy-start.21 = (bf16[16,128,128]{2,1,0:T(8,128)(2,1)S(1)}, bf16[16,128,128]{2,1,0:T(8,128)(2,1)}, u32[]{:S(2)}) copy-start(bf16[16,128,128]{2,1,0:T(8,128)(2,1)} %copy-done.20) | copy-start | bytes 1572868
  85.1 7.0 %copy-start.17 = (bf16[1,16,64,128]{3,2,1,0:T(8,128)(2,1)S(1)}, bf16[1,16,64,128]{3,2,1,0:T(8,128)(2,1)}, u32[]{:S(2)}) copy-start(bf16[1,16,64,128]{3,2,1,0:T(8,128)(2,1)} %copy-done.16) | copy-start | bytes 786436
  85.1 7.0 %copy-start.19 = (bf16[1,16,64,128]{3,2,1,0:T(8,128)(2,1)S(1)}, bf16[1,16,64,128]{3,2,1,0:T(8,128)(2,1)}, u32[]{:S(2)}) copy-start(bf16[1,16,64,128]{3,2,1,0:T(8,128)(2,1)} %copy-done.18) | copy-start | bytes 786436
  92.1 1.7 %copy-start.5 = (f32[512,512]{1,0:T(8,128)}, f32[512,512]{1,0:T(8,128)S(1)}, u32[]{:S(2)}) copy-start(f32[512,512]{1,0:T(8,128)S(1)} %attend.4.part_ref) | copy-start | bytes 3145732
  100.0 18.7 %collective-permute-start.16 = (bf16[256,512]{1,0:T(8,128)(2,1)}, bf16[256,512]{1,0:T(8,128)(2,1)S(1)}, u32[]{:S(2)}, u32[]{:S(2)}) collective-permute-start(bf16[256,512]{1,0:T(8,128)(2,1)} %get-tuple-element.20), channel_id=1, source_target_pairs={{0,16},{16,0},{1,17},{17,1},{2,18},{18,2},{3,19},{19,3},{4,20},{20... | collective-permute-start | bytes 786440 | tf_op jit(solution)/shard_map/ppermute | solution.py:225
  106.3 12.5 %collective-permute-start.15 = (bf16[256,512]{1,0:T(8,128)(2,1)}, bf16[256,512]{1,0:T(8,128)(2,1)S(1)}, u32[]{:S(2)}, u32[]{:S(2)}) collective-permute-start(bf16[256,512]{1,0:T(8,128)(2,1)} %get-tuple-element.19), channel_id=1, source_target_pairs={{0,16},{16,0},{1,17},{17,1},{2,18},{18,2},{3,19},{19,3},{4,20},{20... | collective-permute-start | bytes 786440 | tf_op jit(solution)/shard_map/ppermute | solution.py:225
  111.6 13.0 %copy-start.6 = (bf16[256,4096]{1,0:T(8,128)(2,1)S(1)}, bf16[256,4096]{1,0:T(8,128)(2,1)}, u32[]{:S(2)}) copy-start(bf16[256,4096]{1,0:T(8,128)(2,1)} %gate_ref.1) | copy-start | bytes 6291460
  111.6 13.0 %copy-start.9 = (bf16[256,512]{1,0:T(8,128)(2,1)S(1)}, bf16[256,512]{1,0:T(8,128)(2,1)}, u32[]{:S(2)}) copy-start(bf16[256,512]{1,0:T(8,128)(2,1)} %get-tuple-element.16.rest_3_) | copy-start | bytes 786436
  111.6 13.0 %copy-start.10 = (bf16[256,512]{1,0:T(8,128)(2,1)S(1)}, bf16[256,512]{1,0:T(8,128)(2,1)}, u32[]{:S(2)}) copy-start(bf16[256,512]{1,0:T(8,128)(2,1)} %get-tuple-element.15.rest_2_) | copy-start | bytes 786436
  111.7 13.0 %copy-start.11 = (bf16[256,512]{1,0:T(8,128)(2,1)S(1)}, bf16[256,512]{1,0:T(8,128)(2,1)}, u32[]{:S(2)}) copy-start(bf16[256,512]{1,0:T(8,128)(2,1)} %get-tuple-element.14.rest_1_) | copy-start | bytes 786436
  111.7 13.0 %copy-start.13 = (f32[4096]{0:T(1024)S(1)}, f32[4096]{0:T(1024)}, u32[]{:S(2)}) copy-start(f32[4096]{0:T(1024)} %param.11) | copy-start | bytes 49156
  111.7 7.4 %collective-permute-start.14 = (bf16[256,512]{1,0:T(8,128)(2,1)}, bf16[256,512]{1,0:T(8,128)(2,1)}, u32[]{:S(2)}, u32[]{:S(2)}) collective-permute-start(bf16[256,512]{1,0:T(8,128)(2,1)} %get-tuple-element.18), channel_id=1, source_target_pairs={{0,16},{16,0},{1,17},{17,1},{2,18},{18,2},{3,19},{19,3},{4,20},{20... | collective-permute-start | bytes 786440 | tf_op jit(solution)/shard_map/ppermute | solution.py:225
  118.0 6.6 %collective-permute-start.13 = (bf16[256,512]{1,0:T(8,128)(2,1)}, bf16[256,512]{1,0:T(8,128)(2,1)S(1)}, u32[]{:S(2)}, u32[]{:S(2)}) collective-permute-start(bf16[256,512]{1,0:T(8,128)(2,1)} %get-tuple-element.17), channel_id=1, source_target_pairs={{0,16},{16,0},{1,17},{17,1},{2,18},{18,2},{3,19},{19,3},{4,20},{20... | collective-permute-start | bytes 786440 | tf_op jit(solution)/shard_map/ppermute | solution.py:225
  124.6 1.0 copy-start.12

commit v2 on v1

--- a/solution.py
+++ b/solution.py
@@ -11,7 +11,7 @@
 WINDOW = 512
 EPSILON = 1e-06
 LOG2E = 1.4426950408889634
-VMEM = 48 * 1024 * 1024
+VMEM = 24 * 1024 * 1024
 NN = (((1,), (0,)), ((), ()))
 NT = (((1,), (1,)), ((), ()))
 TN = (((0,), (0,)), ((), ()))
@@ -50,7 +50,14 @@
     )(k, v)
 
 
-def attend_kernel(qb, first_ref, q_ref, k_ref, v_ref, kp_ref, vp_ref, lw_ref, table_ref, out_ref):
+def attend_kernel(qb, heads, first_ref, q_ref, k_ref, v_ref, kp_ref, vp_ref, lw_ref, table_ref, out_ref):
+    for h in range(heads):
+        cols = slice(h * HEAD_DIM, (h + 1) * HEAD_DIM)
+        tensors = [ref.at[:, cols] for ref in (q_ref, k_ref, v_ref, kp_ref, vp_ref)]
+        attend_head(qb, first_ref, *tensors, lw_ref.at[h], table_ref, out_ref.at[:, cols])
+
+
+def attend_head(qb, first_ref, q_ref, k_ref, v_ref, kp_ref, vp_ref, lw_ref, table_ref, out_ref):
     rows = q_ref.shape[0]
     lane = HEAD_DIM
     scale = HEAD_DIM**-0.5 * LOG2E
@@ -60,7 +67,7 @@
         jnp.int32, (qb, qb), 1
     )
     lane_bits = lane.bit_length() - 1
-    lw = lw_ref[0]
+    lw = lw_ref[...]
     for low in range(0, rows, qb):
         high = low + qb
         q = q_ref[low:high, :]
@@ -107,23 +114,28 @@
         out_ref[low:high, :] = windowed * (1.0 / total) + near
 
 
-def attend(first, q, k, v, past_k, past_v, lw, table, head):
+def heads_a_step(heads, most):
+    return max(n for n in range(1, most + 1) if heads % n == 0)
+
+
+def attend(first, q, k, v, past_k, past_v, lw, table, head, step):
     rows, width = past_k.shape
-    whole = pl.BlockSpec((rows, HEAD_DIM), lambda g, *_: (0, head + g))
-    part = pl.BlockSpec((rows, HEAD_DIM), lambda g, *_: (0, g))
+    cols = step * HEAD_DIM
+    whole = pl.BlockSpec((rows, cols), lambda g, *_: (0, head // step + g))
+    part = pl.BlockSpec((rows, cols), lambda g, *_: (0, g))
     qb = min(rows, 256)
     return pl.pallas_call(
-        functools.partial(attend_kernel, qb),
+        functools.partial(attend_kernel, qb, step),
         grid_spec=pltpu.PrefetchScalarGridSpec(
             num_scalar_prefetch=1,
-            grid=(width // HEAD_DIM,),
+            grid=(width // cols,),
             in_specs=[
                 whole,
                 whole,
                 whole,
                 part,
                 part,
-                pl.BlockSpec((1,) + lw.shape[1:], lambda g, *_: (head + g, 0, 0)),
+                pl.BlockSpec((step,) + lw.shape[1:], lambda g, *_: (head // step + g, 0, 0)),
                 pl.BlockSpec(table.shape, lambda g, *_: (0, 0)),
             ],
             out_specs=part,
@@ -134,48 +146,58 @@
     )(first, q, k, v, past_k, past_v, lw, table)
 
 
-def far_kernel(near_n, slots, place_ref, q_ref, lw_ref, bucket_ref, part_ref, *rest):
-    out_refs, scratch = rest[:slots], rest[slots]
+def far_kernel(near_n, slots, heads, far_n, place_ref, q_ref, lw_ref, part_ref, *rest):
+    bucket_refs = rest[: 2 * far_n - 1]
+    out_refs, scratch = rest[2 * far_n - 1 : -1], rest[-1]
     rows = q_ref.shape[0]
     lane = HEAD_DIM
-    far_n = bucket_ref.shape[0]
-    lw = lw_ref[0]
-    proj = mm(q_ref[...], joined([bucket_ref[j, 0] for j in range(far_n)], 1))
-    for a in range(rows // lane):
-        inside = slice(a * lane, (a + 1) * lane)
-        mix = lw[:, inside]
-        mix = joined([mix, jnp.zeros((lane - mix.shape[0], lane), jnp.float32)], 0).T
-        total = part_ref[inside, :]
-        for j in range(far_n):
-            total = total + proj[inside, j * lane : (j + 1) * lane] * mix[:, near_n + j : near_n + j + 1]
-        scratch[inside, :] = total
+    odd = place_ref[1] == 1
+    for h in range(heads):
+        cols = slice(h * lane, (h + 1) * lane)
+        buckets = [bucket_refs[0][h]]
+        for j in range(1, far_n):
+            mine, theirs = bucket_refs[2 * j - 1][h], bucket_refs[2 * j][h]
+            buckets += [jnp.where(odd, theirs, mine), jnp.where(odd, mine, theirs)]
+        bucket = joined(buckets, 0)
+        for a in range(rows // lane):
+            inside = slice(a * lane, (a + 1) * lane)
+            mix = lw_ref[h, :, inside]
+            mix = joined([mix, jnp.zeros((lane - mix.shape[0], lane), jnp.float32)], 0).T
+            q = q_ref[inside, cols].astype(jnp.float32)
+            scaled = [
+                (q * mix[:, near_n + j : near_n + j + 1]).astype(jnp.bfloat16) for j in range(far_n)
+            ]
+            scratch[inside, cols] = part_ref[inside, cols] + mm(joined(scaled, 1), bucket)
     count = rows // slots
     for s in range(slots):
         start = pl.multiple_of(lax.rem(place_ref[0] + s, slots) * count, count)
         out_refs[s][...] = scratch[pl.ds(start, count), :].astype(jnp.bfloat16)
 
 
-def far(place, q, lw, buckets, part, head, near_n, slots):
+def far(place, q, lw, buckets, part, head, near_n, slots, step):
     rows, width = part.shape
-    far_n = buckets.shape[0]
+    far_n = (len(buckets) + 1) // 2
     count = rows // slots
+    cols = step * HEAD_DIM
+    group = lambda g, *_: (head // step + g, 0, 0)
     return pl.pallas_call(
-        functools.partial(far_kernel, near_n, slots),
+        functools.partial(far_kernel, near_n, slots, step, far_n),
         grid_spec=pltpu.PrefetchScalarGridSpec(
             num_scalar_prefetch=1,
-            grid=(width // HEAD_DIM,),
+            grid=(width // cols,),
             in_specs=[
-                pl.BlockSpec((rows, HEAD_DIM), lambda g, *_: (0, head + g)),
-                pl.BlockSpec((1,) + lw.shape[1:], lambda g, *_: (head + g, 0, 0)),
-                pl.BlockSpec((far_n, 1, HEAD_DIM, HEAD_DIM), lambda g, *_: (0, head + g, 0, 0)),
-                pl.BlockSpec((rows, HEAD_DIM), lambda g, *_: (0, g)),
-            ],
-            out_specs=[pl.BlockSpec((count, HEAD_DIM), lambda g, *_: (0, g))] * slots,
-            scratch_shapes=[pltpu.VMEM((rows, HEAD_DIM), jnp.float32)],
+                pl.BlockSpec((rows, cols), lambda g, *_: (0, head // step + g)),
+                pl.BlockSpec((step,) + lw.shape[1:], group),
+                pl.BlockSpec((rows, cols), lambda g, *_: (0, g)),
+            ]
+            + [pl.BlockSpec((step,) + b.shape[1:], group) for b in buckets],
+            out_specs=[pl.BlockSpec((count, cols), lambda g, *_: (0, g))] * slots,
+            scratch_shapes=[pltpu.VMEM((rows, cols), jnp.float32)],
         ),
         out_shape=[jax.ShapeDtypeStruct((count, width), jnp.bfloat16)] * slots,
+        compiler_params=pltpu.CompilerParams(vmem_limit_bytes=VMEM),
         name="far",
-    )(place, q, lw, buckets, part)
+    )(place, q, lw, part, *buckets)
 
 
 def norm_kernel(slots, offsets, local_width, place_ref, gate_ref, gain_ref, *rest):
@@ -219,43 +241,21 @@
     )(place, gate, gain.reshape(1, width), *pieces)
 
 
-def shifted(value, axis, steps, wrap=False):
+def shifted(value, axis, steps):
     count = lax.axis_size(axis)
-    pairs = [(i, (i + steps) % count) for i in range(count) if wrap or i + steps < count]
-    return lax.ppermute(value, axis, pairs)
-
-
-def from_partner(value, axis, level, only_up=False):
-    count = lax.axis_size(axis)
-    pairs = [(i, i ^ 1 << level) for i in range(count) if not only_up or not i >> level & 1]
-    return lax.ppermute(value, axis, pairs)
+    return lax.ppermute(value, axis, [(i, (i + steps) % count) for i in range(count)])
+
+
+def from_partner(value, axis, level):
+    return lax.ppermute(value, axis, [(i, i ^ 1 << level) for i in range(lax.axis_size(axis))])
 
 
 def added(left, right):
     return (left.astype(jnp.float32) + right.astype(jnp.float32)).astype(jnp.bfloat16)
 
 
-def far_buckets(states, place, far_n):
-    bit = [(place >> level & 1).astype(jnp.bfloat16) for level in range(far_n)]
-    other = from_partner(states, "seq", 0)
-    first = other * bit[0]
-    if far_n == 1:
-        return first[None]
-    half = HEAD_DIM // 2
-    running = added(states, other)
-    running = lax.dynamic_slice_in_dim(running, (place & 1) * half, half, 1)
-    halves = []
-    for level in range(1, far_n):
-        last = level == far_n - 1
-        other = from_partner(running, "seq", level, last)
-        halves.append(other * bit[level])
-        if not last:
-            running = added(running, other)
-    mine = jnp.stack(halves, 0)
-    theirs = from_partner(mine, "seq", 0)
-    odd = place & 1 == 1
-    rest = jnp.concatenate([jnp.where(odd, theirs, mine), jnp.where(odd, mine, theirs)], 2)
-    return jnp.concatenate([first[None], rest], 0)
+def after(value, *earlier):
+    return lax.optimization_barrier((value,) + earlier)[0]
 
 
 def local(queries, key_vectors, values, level_weights, gate_branch, norm_gain):
@@ -267,33 +267,53 @@
     slots = lax.axis_size("heads")
     seq_place = lax.axis_index("seq")
     first = seq_place.reshape(1)
-    heads_place = lax.axis_index("heads").reshape(1)
+    heads_place = lax.axis_index("heads")
+    place = jnp.stack([heads_place, seq_place & 1])
     chunk = max(1, heads // 4)
     starts = list(range(0, heads, chunk))
 
+    def halo(start, *earlier):
+        cols = slice(start * HEAD_DIM, (start + chunk) * HEAD_DIM)
+        pair = (key_vectors[:, cols], values[:, cols])
+        if earlier:
+            pair = lax.optimization_barrier(pair + earlier)[:2]
+        return shifted(pair, "seq", 1)
+
     states = block_states(key_vectors, values)
+    other = from_partner(states, "seq", 0)
+    buckets = [other]
+    half = HEAD_DIM // 2
+    running = lax.dynamic_slice_in_dim(added(states, other), (seq_place & 1) * half, half, 1)
     past = []
-    for start in starts:
-        cols = slice(start * HEAD_DIM, (start + chunk) * HEAD_DIM)
-        past.append(shifted((key_vectors[:, cols], values[:, cols]), "seq", 1))
-    buckets = far_buckets(states, seq_place, far_n)
+    for level in range(1, far_n):
+        other = from_partner(running, "seq", level)
+        if level == far_n - 1:
+            past += [halo(start, running) for start in starts[len(past) :]]
+        elif len(past) < len(starts):
+            past.append(halo(starts[len(past)], running))
+        buckets += [other, from_partner(other, "seq", 0)]
+        running = added(running, other)
 
     coef = level_scale(jnp.arange(levels, dtype=jnp.int32)) * HEAD_DIM**-0.5
+    far_id = jnp.arange(levels, dtype=jnp.int32) - near_n
+    present = jnp.where(far_id < 0, 1, seq_place >> jnp.maximum(far_id, 0) & 1)
+    coef = coef * present.astype(jnp.float32)
     lw = jnp.transpose(level_weights, (1, 0, 2)) * coef[None, :, None]
     pos = jnp.arange(HEAD_DIM, dtype=jnp.int32)
     differ = pos[:, None] ^ pos[None, :]
     table = sum((differ >> b > 0).astype(jnp.int32) for b in range(HEAD_DIM.bit_length()))
     table = jnp.where(pos[:, None] >= pos[None, :], table, HEAD_DIM - 1)
 
+    step = heads_a_step(chunk, 2)
     kept = [[] for _ in range(slots)]
     for start, (past_k, past_v) in zip(starts, past):
-        part = attend(first, queries, key_vectors, values, past_k, past_v, lw, table, start)
-        pieces = far(heads_place, queries, lw, buckets, part, start, near_n, slots)
+        part = attend(first, queries, key_vectors, values, past_k, past_v, lw, table, start, step)
+        pieces = far(place, queries, lw, buckets, part, start, near_n, slots, step)
         for s in range(slots):
-            kept[s].append(pieces[s] if s == 0 else shifted(pieces[s], "heads", s, True))
+            kept[s].append(pieces[s] if s == 0 else shifted(pieces[s], "heads", s))
     pieces = [piece for group in kept for piece in group]
     offsets = tuple(start * HEAD_DIM for start in starts)
-    return norm(heads_place, gate_branch, norm_gain, pieces, slots, offsets, local_width)
+    return norm(heads_place.reshape(1), gate_branch, norm_gain, pieces, slots, offsets, local_width)
 
 
 def solution(mesh):

time: 132 us -> 148 us (1.12)
  waiting for transfers between devices: 12.7 us -> 35.4 us
  Pallas kernels: 54.8 us -> 44.8 us
  starting transfers between devices: 47 us -> 53.5 us
  other arithmetic: 8.8 us -> 2.63 us
  local copies, waits for them, and re-layouts: 6.34 us -> 10.7 us
    ppermute x17 -> x19, waiting for transfers between devices: 12.7 us -> 35.4 us  [the longest x7 19 us: from_partner(): lax.ppermute(value, axis, [(i, i ^ 1 << level) for i in range(lax.axis_si...]
    pallas_call x8, Pallas kernels: 45.8 us -> 36.9 us  [the longest x4 25.3 us: attend(): pl.pallas_call(functools.partial(attend_kernel, qb, step), grid_spec=pltp...]
    ppermute x17 -> x19, starting transfers between devices: 47 us -> 53.5 us  [the longest x12 47.6 us: shifted(): lax.ppermute(value, axis, [(i, (i + steps) % count) for i in range(count)])]
    unnamed x48 -> x24, local copies, waits for them, and re-layouts: 3.59 us -> 7.67 us
    another operation x4 -> x1, other arithmetic: 2.95 us -> 0.07 us  [local(): place = jnp.stack([heads_place, seq_place & 1])]
    select_n x1 -> x0, other arithmetic: 1.57 us -> none  [far_buckets(): jnp.where(odd, theirs, mine)]
    concatenate x1 -> x0, other arithmetic: 1.52 us -> none  [far_buckets(): return jnp.concatenate([first[None], rest], 0)]
    slice x2 -> x1, local copies, waits for them, and re-layouts: 2.75 us -> 3.04 us  [halo(): pair = (key_vectors[:, cols], values[:, cols])]
  transfers between devices with their start and end apart: 17 -> 19, of which waited for: 5 -> 8; matrix products, arithmetic and copies ran while one was open for 6% -> 3% of each run, Pallas kernels for 32% -> 23%
where the time goes in v2:
time: 148 us; the launch traced here: 147 us
  starting transfers between devices  53.5 us (36%)
  Pallas kernels  44.8 us (30%)
  waiting for transfers between devices  35.4 us (24%)
  local copies, waits for them, and re-layouts  10.7 us (7%)
  other arithmetic  2.63 us (2%)
    ppermute x12, starting transfers between devices, shifted(): lax.ppermute(value, axis, [(i, (i + steps) % count) for i in range(count)])  47.6 us
    pallas_call x4, Pallas kernels, attend(): pl.pallas_call(functools.partial(attend_kernel, qb, step), grid_spec=pltp...  25.3 us
    ppermute x7, waiting for transfers between devices, from_partner(): lax.ppermute(value, axis, [(i, i ^ 1 << level) for i in range(lax.axis_si...  19 us
    ppermute x12, waiting for transfers between devices, shifted(): lax.ppermute(value, axis, [(i, (i + steps) % count) for i in range(count)])  16.4 us
    pallas_call x4, Pallas kernels, far(): pl.pallas_call(functools.partial(far_kernel, near_n, slots, step, far_n),...  11.6 us
    unnamed x24, local copies, waits for them, and re-layouts  7.67 us
    ppermute x7, starting transfers between devices, from_partner(): lax.ppermute(value, axis, [(i, i ^ 1 << level) for i in range(lax.axis_si...  5.91 us
    pallas_call x1, Pallas kernels, block_states(): pl.pallas_call(functools.partial(state_kernel, step), grid=(heads // step...  4.64 us
  transfers between devices with their start and end apart: 19, of which 8 were waited for; matrix products, arithmetic and copies ran while one was open for 3% of the time, Pallas kernels for 23%

profile of v2, /device:TPU:0, one launch (start us, length us, event | category | flops | bytes accessed | tf_op | source)
XLA Modules:
  0.0 147.3 jit_solution(4515357695314893658)
XLA Ops:
  0.0 4.6 %block_states.1 = bf16[16,128,128]{2,1,0:T(8,128)(2,1)} custom-call(bf16[512,2048]{1,0:T(8,128)(2,1)} %k_ref.9, bf16[512,2048]{1,0:T(8,128)(2,1)} %v_ref.9), custom_call_target="tpu_custom_call" | custom-call | tf_op jit(solution)/shard_map/block_states/pallas_call | solution.py:43
  4.6 0.5 collective-permute-start
  5.1 1.7 %collective-permute-done.rest_0_ = bf16[16,128,128]{2,1,0:T(8,128)(2,1)S(1)} collective-permute-done((bf16[16,128,128]{2,1,0:T(8,128)(2,1)}, bf16[16,128,128]{2,1,0:T(8,128)(2,1)S(1)}, u32[]{:S(2)}, u32[]{:S(2)}) %collective-permute-start) | collective-permute-done | bytes 524320 | tf_op jit(solution)/shard_map/ppermute | solution.py:250
  6.9 1.0 add_convert_fusion.2
  7.9 3.0 %collective-permute-start.3 = (bf16[16,64,128]{2,1,0:T(8,128)(2,1)S(1)}, bf16[16,64,128]{2,1,0:T(8,128)(2,1)S(1)}, u32[]{:S(2)}, u32[]{:S(2)}) collective-permute-start(bf16[16,64,128]{2,1,0:T(8,128)(2,1)S(1)} %add_convert_fusion.2), channel_id=1, source_target_pairs={{0,2},{1,3},{2,0},{3,1},{4,6},{5,7},{6,4},{7,5},{8,10},{9,11},{10,... | collective-permute-start | bytes 786440 | tf_op jit(solution)/shard_map/ppermute | solution.py:250
  10.8 3.0 %fusion.19 = (bf16[512,512]{1,0:T(8,128)(2,1)}, bf16[512,512]{1,0:T(8,128)(2,1)}, bf16[512,512]{1,0:T(8,128)(2,1)}, bf16[512,512]{1,0:T(8,128)(2,1)S(1)}, bf16[5...) fusion(bf16[512,2048]{1,0:T(8,128)(2,1)} %v_ref.9, ...), kind=kLoop, calls=%fused_computation.28 | loop fusion | bytes 8388608 | tf_op jit(solution)/shard_map/slice | solution.py:277
  13.9 3.6 %collective-permute-done.3.rest_1_ = bf16[16,64,128]{2,1,0:T(8,128)(2,1)S(1)} collective-permute-done((bf16[16,64,128]{2,1,0:T(8,128)(2,1)S(1)}, bf16[16,64,128]{2,1,0:T(8,128)(2,1)S(1)}, u32[]{:S(2)}, u32[]{:S(2)}) %collective-permute-start.3) | collective-permute-done | bytes 262176 | tf_op jit(solution)/shard_map/ppermute | solution.py:250
  17.5 0.1 add_convert_fusion.1
  17.6 1.8 %collective-permute-start.5 = (bf16[16,64,128]{2,1,0:T(8,128)(2,1)S(1)}, bf16[16,64,128]{2,1,0:T(8,128)(2,1)S(1)}, u32[]{:S(2)}, u32[]{:S(2)}) collective-permute-start(bf16[16,64,128]{2,1,0:T(8,128)(2,1)S(1)} %add_convert_fusion.1), channel_id=1, source_target_pairs={{0,4},{1,5},{2,6},{3,7},{4,0},{5,1},{6,2},{7,3},{8,12},{9,13},{10,... | collective-permute-start | bytes 786440 | tf_op jit(solution)/shard_map/ppermute | solution.py:250
  19.4 2.4 %collective-permute-start.9 = (bf16[512,512]{1,0:T(8,128)(2,1)S(1)}, bf16[512,512]{1,0:T(8,128)(2,1)S(1)}, u32[]{:S(2)}, u32[]{:S(2)}) collective-permute-start(bf16[512,512]{1,0:T(8,128)(2,1)S(1)} %get-tuple-element.24), channel_id=1, source_target_pairs={{0,1},{1,2},{2,3},{3,4},{4,5},{5,6},{6,7},{7,8},{8,9},{9,10},{10,1... | collective-permute-start | bytes 1572872 | tf_op jit(solution)/shard_map/ppermute | solution.py:246
  21.8 0.0 collective-permute-start.10
  21.9 3.6 %collective-permute-done.5.rest_3_ = bf16[16,64,128]{2,1,0:T(8,128)(2,1)S(1)} collective-permute-done((bf16[16,64,128]{2,1,0:T(8,128)(2,1)S(1)}, bf16[16,64,128]{2,1,0:T(8,128)(2,1)S(1)}, u32[]{:S(2)}, u32[]{:S(2)}) %collective-permute-start.5) | collective-permute-done | bytes 262176 | tf_op jit(solution)/shard_map/ppermute | solution.py:250
  25.4 0.1 add_convert_fusion
  25.5 0.1 collective-permute-start.11
  25.6 0.8 copy-done.5
  26.4 6.1 %collective-permute-start.12 = (bf16[512,512]{1,0:T(8,128)(2,1)}, bf16[512,512]{1,0:T(8,128)(2,1)}, u32[]{:S(2)}, u32[]{:S(2)}) collective-permute-start(bf16[512,512]{1,0:T(8,128)(2,1)} %get-tuple-element.28), channel_id=1, source_target_pairs={{0,1},{1,2},{2,3},{3,4},{4,5},{5,6},{6,7},{7,8},{8,9},{9,10},{10,1... | collective-permute-start | bytes 1572872 | tf_op jit(solution)/shard_map/ppermute | solution.py:246
  32.5 4.0 %collective-permute-done.2.vp_ref = bf16[512,512]{1,0:T(8,128)(2,1)S(1)} collective-permute-done((bf16[512,512]{1,0:T(8,128)(2,1)S(1)}, bf16[512,512]{1,0:T(8,128)(2,1)S(1)}, u32[]{:S(2)}, u32[]{:S(2)}) %collective-permute-start.2) | collective-permute-done | bytes 524320 | tf_op jit(solution)/shard_map/ppermute | solution.py:246
  36.4 0.8 copy-done.7
  37.2 10.1 %collective-permute-done.7.rest_5_ = bf16[16,64,128]{2,1,0:T(8,128)(2,1)S(1)} collective-permute-done((bf16[16,64,128]{2,1,0:T(8,128)(2,1)S(1)}, bf16[16,64,128]{2,1,0:T(8,128)(2,1)S(1)}, u32[]{:S(2)}, u32[]{:S(2)}) %collective-permute-start.7) | collective-permute-done | bytes 262176 | tf_op jit(solution)/shard_map/ppermute | solution.py:250
  47.3 0.8 copy-done.9
  48.1 34.7 %collective-permute-start.14 = (bf16[512,512]{1,0:T(8,128)(2,1)}, bf16[512,512]{1,0:T(8,128)(2,1)}, u32[]{:S(2)}, u32[]{:S(2)}) collective-permute-start(bf16[512,512]{1,0:T(8,128)(2,1)} %get-tuple-element.31), channel_id=1, source_target_pairs={{0,1},{1,2},{2,3},{3,4},{4,5},{5,6},{6,7},{7,8},{8,9},{9,10},{10,1... | collective-permute-start | bytes 1572872 | tf_op jit(solution)/shard_map/ppermute | solution.py:246
  82.8 0.1 add_select_fusion.table_ref
  82.9 0.2 collective-permute-start.4
  83.0 0.4 collective-permute-start.6
  83.4 0.1 collective-permute-start.8
  83.6 0.1 pad_add_fusion.place_ref
  83.6 1.3 fusion.lw_ref
  84.9 0.0 copy-start.2
  85.0 1.6 %copy-done.2 = bf16[512,2048]{1,0:T(8,128)(2,1)S(1)} copy-done((bf16[512,2048]{1,0:T(8,128)(2,1)S(1)}, bf16[512,2048]{1,0:T(8,128)(2,1)}, u32[]{:S(2)}) %copy-start.2) | copy-done | bytes 2097176
  86.5 1.6 %copy-done.3 = bf16[512,2048]{1,0:T(8,128)(2,1)S(1)} copy-done((bf16[512,2048]{1,0:T(8,128)(2,1)S(1)}, bf16[512,2048]{1,0:T(8,128)(2,1)}, u32[]{:S(2)}) %copy-start.3) | copy-done | bytes 2097176
  88.1 1.0 copy-done.6
  89.2 1.0 copy-done.8
  90.2 5.7 %attend.4.part_ref = f32[512,512]{1,0:T(8,128)S(1)} custom-call(s32[1]{0:T(128)} %bitcast.4.first_ref, bf16[512,2048]{1,0:T(8,128)(2,1)S(1)} %copy-done, bf16[512,2048]{1,0:T(8,128)(2,1)S(1)} %copy-done.2, bf16[512,2048]{1,0:T(8,128)(2,1)S(1)} %copy-done.3, bf16[512,512]{1,0:T(8,128)(2,1)S(1)} %copy-done.6, bf16[512,512]{1,0:T(8,128)(2,1)S(1)} %copy-done.8, ...), custom_call_target="tpu_custom_call" | custom-call | tf_op jit(solution)/shard_map/attend/pallas_call | solution.py:127
  95.9 6.5 %attend.5.part_ref = f32[512,512]{1,0:T(8,128)S(1)} custom-call(s32[1]{0:T(128)} %bitcast.4.first_ref, bf16[512,2048]{1,0:T(8,128)(2,1)S(1)} %copy-done, bf16[512,2048]{1,0:T(8,128)(2,1)S(1)} %copy-done.2, bf16[512,2048]{1,0:T(8,128)(2,1)S(1)} %copy-done.3, bf16[512,512]{1,0:T(8,128)(2,1)S(1)} %copy-done.10, ...), custom_call_target="tpu_custom_call" | custom-call | tf_op jit(solution)/shard_map/attend/pallas_call | solution.py:127
  102.4 6.6 %attend.6.part_ref = f32[512,512]{1,0:T(8,128)S(1)} custom-call(s32[1]{0:T(128)} %bitcast.4.first_ref, bf16[512,2048]{1,0:T(8,128)(2,1)S(1)} %copy-done, bf16[512,2048]{1,0:T(8,128)(2,1)S(1)} %copy-done.2, bf16[512,2048]{1,0:T(8,128)(2,1)S(1)} %copy-done.3, bf16[512,512]{1,0:T(8,128)(2,1)} %collective-permute-done.11.kp_ref, ...), custom_call_target="tpu_custom_call" | custom-call | tf_op jit(solution)/shard_map/attend/pallas_call | solution.py:127
  109.0 6.6 %attend.7.part_ref = f32[512,512]{1,0:T(8,128)S(1)} custom-call(s32[1]{0:T(128)} %bitcast.4.first_ref, bf16[512,2048]{1,0:T(8,128)(2,1)S(1)} %copy-done, bf16[512,2048]{1,0:T(8,128)(2,1)S(1)} %copy-done.2, bf16[512,2048]{1,0:T(8,128)(2,1)S(1)} %copy-done.3, bf16[512,512]{1,0:T(8,128)(2,1)} %collective-permute-done.13.kp_ref, ...), custom_call_target="tpu_custom_call" | custom-call | tf_op jit(solution)/shard_map/attend/pallas_call | solution.py:127
  115.6 2.8 %far.4 = (bf16[256,512]{1,0:T(8,128)(2,1)S(1)}, bf16[256,512]{1,0:T(8,128)(2,1)S(1)}) custom-call(s32[2]{0:T(128)S(1)} %pad_add_fusion.place_ref, bf16[512,2048]{1,0:T(8,128)(2,1)S(1)} %copy-done, f32[16,14,512]{2,1,0:T(8,128)S(1)} %fusion.lw_ref, f32[512,512]{1,0:T(8,128)S(1)} %attend.4.part_ref, bf16[16,128,128]{2,1,0:T(8,128)(2,1)S(1)} %collective-permute-done.rest_0_, ...), custom_call_target="tpu_custom_call" | custom-call | tf_op jit(solution)/shard_map/far/pallas_call | solution.py:183
  118.5 1.6 %collective-permute-start.15 = (bf16[256,512]{1,0:T(8,128)(2,1)S(1)}, bf16[256,512]{1,0:T(8,128)(2,1)S(1)}, u32[]{:S(2)}, u32[]{:S(2)}) collective-permute-start(bf16[256,512]{1,0:T(8,128)(2,1)S(1)} %get-tuple-element.33), channel_id=1, source_target_pairs={{0,16},{16,0},{1,17},{17,1},{2,18},{18,2},{3,19},{19,3},{4,20},{20... | collective-permute-start | bytes 786440 | tf_op jit(solution)/shard_map/ppermute | solution.py:246
  120.0 2.9 %far.5 = (bf16[256,512]{1,0:T(8,128)(2,1)S(1)}, bf16[256,512]{1,0:T(8,128)(2,1)S(1)}) custom-call(s32[2]{0:T(128)S(1)} %pad_add_fusion.place_ref, bf16[512,2048]{1,0:T(8,128)(2,1)S(1)} %copy-done, f32[16,14,512]{2,1,0:T(8,128)S(1)} %fusion.lw_ref, f32[512,512]{1,0:T(8,128)S(1)} %attend.5.part_ref, bf16[16,128,128]{2,1,0:T(8,128)(2,1)S(1)} %collective-permute-done.rest_0_, ...), custom_call_target="tpu_custom_call" | custom-call | tf_op jit(solution)/shard_map/far/pallas_call | solution.py:183
  122.9 0.6 collective-permute-start.16
  123.5 3.1 %far.6 = (bf16[256,512]{1,0:T(8,128)(2,1)S(1)}, bf16[256,512]{1,0:T(8,128)(2,1)S(1)}) custom-call(s32[2]{0:T(128)S(1)} %pad_add_fusion.place_ref, bf16[512,2048]{1,0:T(8,128)(2,1)S(1)} %copy-done, f32[16,14,512]{2,1,0:T(8,128)S(1)} %fusion.lw_ref, f32[512,512]{1,0:T(8,128)S(1)} %attend.6.part_ref, bf16[16,128,128]{2,1,0:T(8,128)(2,1)S(1)} %collective-permute-done.rest_0_, ...), custom_call_target="tpu_custom_call" | custom-call | tf_op jit(solution)/shard_map/far/pallas_call | solution.py:183
  126.6 1.6 %collective-permute-start.17 = (bf16[256,512]{1,0:T(8,128)(2,1)S(1)}, bf16[256,512]{1,0:T(8,128)(2,1)S(1)}, u32[]{:S(2)}, u32[]{:S(2)}) collective-permute-start(bf16[256,512]{1,0:T(8,128)(2,1)S(1)} %get-tuple-element.35), channel_id=1, source_target_pairs={{0,16},{16,0},{1,17},{17,1},{2,18},{18,2},{3,19},{19,3},{4,20},{20... | collective-permute-start | bytes 786440 | tf_op jit(solution)/shard_map/ppermute | solution.py:246
  128.2 2.9 %far.7 = (bf16[256,512]{1,0:T(8,128)(2,1)S(1)}, bf16[256,512]{1,0:T(8,128)(2,1)S(1)}) custom-call(s32[2]{0:T(128)S(1)} %pad_add_fusion.place_ref, bf16[512,2048]{1,0:T(8,128)(2,1)S(1)} %copy-done, f32[16,14,512]{2,1,0:T(8,128)S(1)} %fusion.lw_ref, f32[512,512]{1,0:T(8,128)S(1)} %attend.7.part_ref, bf16[16,128,128]{2,1,0:T(8,128)(2,1)S(1)} %collective-permute-done.rest_0_, ...), custom_call_target="tpu_custom_call" | custom-call | tf_op jit(solution)/shard_map/far/pallas_call | solution.py:183
  131.0 0.6 collective-permute-start.18
  131.6 1.6 %collective-permute-done.16.rest_5_ = bf16[256,512]{1,0:T(8,128)(2,1)S(1)} collective-permute-done((bf16[256,512]{1,0:T(8,128)(2,1)S(1)}, bf16[256,512]{1,0:T(8,128)(2,1)S(1)}, u32[]{:S(2)}, u32[]{:S(2)}) %collective-permute-start.16) | collective-permute-done | bytes 262176 | tf_op jit(solution)/shard_map/ppermute | solution.py:246
  133.2 5.6 %collective-permute-done.17.rest_6_ = bf16[256,512]{1,0:T(8,128)(2,1)S(1)} collective-permute-done((bf16[256,512]{1,0:T(8,128)(2,1)S(1)}, bf16[256,512]{1,0:T(8,128)(2,1)S(1)}, u32[]{:S(2)}, u32[]{:S(2)}) %collective-permute-start.17) | collective-permute-done | bytes 262176 | tf_op jit(solution)/shard_map/ppermute | solution.py:246
  138.9 5.1 %collective-permute-done.18.rest_7_ = bf16[256,512]{1,0:T(8,128)(2,1)S(1)} collective-permute-done((bf16[256,512]{1,0:T(8,128)(2,1)S(1)}, bf16[256,512]{1,0:T(8,128)(2,1)S(1)}, u32[]{:S(2)}, u32[]{:S(2)}) %collective-permute-start.18) | collective-permute-done | bytes 262176 | tf_op jit(solution)/shard_map/ppermute | solution.py:246
  144.0 3.2 %norm.1 = bf16[256,4096]{1,0:T(8,128)(2,1)} custom-call(s32[1]{0:T(128)} %bitcast.place_ref, bf16[256,4096]{1,0:T(8,128)(2,1)S(1)} %copy-done.4, f32[1,4096]{1,0:T(1,128)S(1)} %bitcast.6, bf16[256,512]{1,0:T(8,128)(2,1)S(1)} %get-tuple-element.23.rest_0_, bf16[256,512]{1,0:T(8,128)(2,1)S(1)} %get-tuple-element.26.rest_1_, ...), custom_call_target="tpu_custom_call" | custom-call | tf_op jit(solution)/shard_map/norm/pallas_call | solution.py:225
  (32 shorter events, 0.1 us)
Async XLA Ops:
  0.0 10.8 %copy-start.1 = (bf16[512,2048]{1,0:T(8,128)(2,1)S(1)}, bf16[512,2048]{1,0:T(8,128)(2,1)}, u32[]{:S(2)}) copy-start(bf16[512,2048]{1,0:T(8,128)(2,1)} %k_ref.9) | copy-start | bytes 6291460
  4.6 2.2 %collective-permute-start = (bf16[16,128,128]{2,1,0:T(8,128)(2,1)}, bf16[16,128,128]{2,1,0:T(8,128)(2,1)S(1)}, u32[]{:S(2)}, u32[]{:S(2)}) collective-permute-start(bf16[16,128,128]{2,1,0:T(8,128)(2,1)} %block_states.1), channel_id=1, source_target_pairs={{0,1},{1,0},{2,3},{3,2},{4,5},{5,4},{6,7},{7,6},{8,9},{9,8},{10,11... | collective-permute-start | bytes 1572872 | tf_op jit(solution)/shard_map/ppermute | solution.py:250
  7.9 9.6 %collective-permute-start.3 = (bf16[16,64,128]{2,1,0:T(8,128)(2,1)S(1)}, bf16[16,64,128]{2,1,0:T(8,128)(2,1)S(1)}, u32[]{:S(2)}, u32[]{:S(2)}) collective-permute-start(bf16[16,64,128]{2,1,0:T(8,128)(2,1)S(1)} %add_convert_fusion.2), channel_id=1, source_target_pairs={{0,2},{1,3},{2,0},{3,1},{4,6},{5,7},{6,4},{7,5},{8,10},{9,11},{10,... | collective-permute-start | bytes 786440 | tf_op jit(solution)/shard_map/ppermute | solution.py:250
  13.9 71.1 %copy-start = (bf16[512,2048]{1,0:T(8,128)(2,1)S(1)}, bf16[512,2048]{1,0:T(8,128)(2,1)}, u32[]{:S(2)}) copy-start(bf16[512,2048]{1,0:T(8,128)(2,1)} %q_ref.15) | copy-start | bytes 6291460
  13.9 11.7 %collective-permute-start.1 = (bf16[512,512]{1,0:T(8,128)(2,1)S(1)}, bf16[512,512]{1,0:T(8,128)(2,1)S(1)}, u32[]{:S(2)}, u32[]{:S(2)}) collective-permute-start(bf16[512,512]{1,0:T(8,128)(2,1)S(1)} %get-tuple-element.21), channel_id=1, source_target_pairs={{0,1},{1,2},{2,3},{3,4},{4,5},{5,6},{6,7},{7,8},{8,9},{9,10},{10,1... | collective-permute-start | bytes 1572872 | tf_op jit(solution)/shard_map/ppermute | solution.py:246
  17.6 7.8 %collective-permute-start.5 = (bf16[16,64,128]{2,1,0:T(8,128)(2,1)S(1)}, bf16[16,64,128]{2,1,0:T(8,128)(2,1)S(1)}, u32[]{:S(2)}, u32[]{:S(2)}) collective-permute-start(bf16[16,64,128]{2,1,0:T(8,128)(2,1)S(1)} %add_convert_fusion.1), channel_id=1, source_target_pairs={{0,4},{1,5},{2,6},{3,7},{4,0},{5,1},{6,2},{7,3},{8,12},{9,13},{10,... | collective-permute-start | bytes 786440 | tf_op jit(solution)/shard_map/ppermute | solution.py:250
  19.4 17.0 %collective-permute-start.2 = (bf16[512,512]{1,0:T(8,128)(2,1)S(1)}, bf16[512,512]{1,0:T(8,128)(2,1)S(1)}, u32[]{:S(2)}, u32[]{:S(2)}) collective-permute-start(bf16[512,512]{1,0:T(8,128)(2,1)S(1)} %get-tuple-element.22), channel_id=1, source_target_pairs={{0,1},{1,2},{2,3},{3,4},{4,5},{5,6},{6,7},{7,8},{8,9},{9,10},{10,1... | collective-permute-start | bytes 1572872 | tf_op jit(solution)/shard_map/ppermute | solution.py:246
  19.4 27.9 %collective-permute-start.9 = (bf16[512,512]{1,0:T(8,128)(2,1)S(1)}, bf16[512,512]{1,0:T(8,128)(2,1)S(1)}, u32[]{:S(2)}, u32[]{:S(2)}) collective-permute-start(bf16[512,512]{1,0:T(8,128)(2,1)S(1)} %get-tuple-element.24), channel_id=1, source_target_pairs={{0,1},{1,2},{2,3},{3,4},{4,5},{5,6},{6,7},{7,8},{8,9},{9,10},{10,1... | collective-permute-start | bytes 1572872 | tf_op jit(solution)/shard_map/ppermute | solution.py:246
  21.8 61.0 %collective-permute-start.10 = (bf16[512,512]{1,0:T(8,128)(2,1)}, bf16[512,512]{1,0:T(8,128)(2,1)}, u32[]{:S(2)}, u32[]{:S(2)}) collective-permute-start(bf16[512,512]{1,0:T(8,128)(2,1)} %get-tuple-element.25), channel_id=1, source_target_pairs={{0,1},{1,2},{2,3},{3,4},{4,5},{5,6},{6,7},{7,8},{8,9},{9,10},{10,1... | collective-permute-start | bytes 1572872 | tf_op jit(solution)/shard_map/ppermute | solution.py:246
  25.5 57.5 %collective-permute-start.11 = (bf16[512,512]{1,0:T(8,128)(2,1)}, bf16[512,512]{1,0:T(8,128)(2,1)}, u32[]{:S(2)}, u32[]{:S(2)}) collective-permute-start(bf16[512,512]{1,0:T(8,128)(2,1)} %get-tuple-element.27), channel_id=1, source_target_pairs={{0,1},{1,2},{2,3},{3,4},{4,5},{5,6},{6,7},{7,8},{8,9},{9,10},{10,1... | collective-permute-start | bytes 1572872 | tf_op jit(solution)/shard_map/ppermute | solution.py:246
  25.6 0.8 copy-start.5
  26.4 57.0 %collective-permute-start.12 = (bf16[512,512]{1,0:T(8,128)(2,1)}, bf16[512,512]{1,0:T(8,128)(2,1)}, u32[]{:S(2)}, u32[]{:S(2)}) collective-permute-start(bf16[512,512]{1,0:T(8,128)(2,1)} %get-tuple-element.28), channel_id=1, source_target_pairs={{0,1},{1,2},{2,3},{3,4},{4,5},{5,6},{6,7},{7,8},{8,9},{9,10},{10,1... | collective-permute-start | bytes 1572872 | tf_op jit(solution)/shard_map/ppermute | solution.py:246
  36.4 0.8 copy-start.7
  37.2 10.1 %collective-permute-start.7 = (bf16[16,64,128]{2,1,0:T(8,128)(2,1)S(1)}, bf16[16,64,128]{2,1,0:T(8,128)(2,1)S(1)}, u32[]{:S(2)}, u32[]{:S(2)}) collective-permute-start(bf16[16,64,128]{2,1,0:T(8,128)(2,1)S(1)} %add_convert_fusion), channel_id=1, source_target_pairs={{0,8},{1,9},{2,10},{3,11},{4,12},{5,13},{6,14},{7,15},{8,0},{9,1},... | collective-permute-start | bytes 786440 | tf_op jit(solution)/shard_map/ppermute | solution.py:250
  47.3 61.7 %collective-permute-start.13 = (bf16[512,512]{1,0:T(8,128)(2,1)}, bf16[512,512]{1,0:T(8,128)(2,1)}, u32[]{:S(2)}, u32[]{:S(2)}) collective-permute-start(bf16[512,512]{1,0:T(8,128)(2,1)} %get-tuple-element.30), channel_id=1, source_target_pairs={{0,1},{1,2},{2,3},{3,4},{4,5},{5,6},{6,7},{7,8},{8,9},{9,10},{10,1... | collective-permute-start | bytes 1572872 | tf_op jit(solution)/shard_map/ppermute | solution.py:246
  47.3 0.8 copy-start.9
  48.1 60.9 %collective-permute-start.14 = (bf16[512,512]{1,0:T(8,128)(2,1)}, bf16[512,512]{1,0:T(8,128)(2,1)}, u32[]{:S(2)}, u32[]{:S(2)}) collective-permute-start(bf16[512,512]{1,0:T(8,128)(2,1)} %get-tuple-element.31), channel_id=1, source_target_pairs={{0,1},{1,2},{2,3},{3,4},{4,5},{5,6},{6,7},{7,8},{8,9},{9,10},{10,1... | collective-permute-start | bytes 1572872 | tf_op jit(solution)/shard_map/ppermute | solution.py:246
  82.9 32.7 %collective-permute-start.4 = (bf16[16,64,128]{2,1,0:T(8,128)(2,1)S(1)}, bf16[16,64,128]{2,1,0:T(8,128)(2,1)S(1)}, u32[]{:S(2)}, u32[]{:S(2)}) collective-permute-start(bf16[16,64,128]{2,1,0:T(8,128)(2,1)S(1)} %collective-permute-done.3.rest_1_), channel_id=1, source_target_pairs={{0,1},{1,0},{2,3},{3,2},{4,5},{5,4},{6,7},{7,6},{8,9},{9,8},{10,11... | collective-permute-start | bytes 786440 | tf_op jit(solution)/shard_map/ppermute | solution.py:250
  83.0 32.5 %collective-permute-start.6 = (bf16[16,64,128]{2,1,0:T(8,128)(2,1)S(1)}, bf16[16,64,128]{2,1,0:T(8,128)(2,1)S(1)}, u32[]{:S(2)}, u32[]{:S(2)}) collective-permute-start(bf16[16,64,128]{2,1,0:T(8,128)(2,1)S(1)} %collective-permute-done.5.rest_3_), channel_id=1, source_target_pairs={{0,1},{1,0},{2,3},{3,2},{4,5},{5,4},{6,7},{7,6},{8,9},{9,8},{10,11... | collective-permute-start | bytes 786440 | tf_op jit(solution)/shard_map/ppermute | solution.py:250
  83.4 32.2 %collective-permute-start.8 = (bf16[16,64,128]{2,1,0:T(8,128)(2,1)S(1)}, bf16[16,64,128]{2,1,0:T(8,128)(2,1)S(1)}, u32[]{:S(2)}, u32[]{:S(2)}) collective-permute-start(bf16[16,64,128]{2,1,0:T(8,128)(2,1)S(1)} %collective-permute-done.7.rest_5_), channel_id=1, source_target_pairs={{0,1},{1,0},{2,3},{3,2},{4,5},{5,4},{6,7},{7,6},{8,9},{9,8},{10,11... | collective-permute-start | bytes 786440 | tf_op jit(solution)/shard_map/ppermute | solution.py:250
  84.9 1.6 %copy-start.2 = (bf16[512,2048]{1,0:T(8,128)(2,1)S(1)}, bf16[512,2048]{1,0:T(8,128)(2,1)}, u32[]{:S(2)}) copy-start(bf16[512,2048]{1,0:T(8,128)(2,1)} %k_ref.9) | copy-start | bytes 6291460
  86.5 1.6 %copy-start.3 = (bf16[512,2048]{1,0:T(8,128)(2,1)S(1)}, bf16[512,2048]{1,0:T(8,128)(2,1)}, u32[]{:S(2)}) copy-start(bf16[512,2048]{1,0:T(8,128)(2,1)} %v_ref.9) | copy-start | bytes 6291460
  88.1 1.0 copy-start.6
  89.2 1.0 copy-start.8
  90.2 5.7 %copy-start.10 = (bf16[512,512]{1,0:T(8,128)(2,1)S(1)}, bf16[512,512]{1,0:T(8,128)(2,1)}, u32[]{:S(2)}) copy-start(bf16[512,512]{1,0:T(8,128)(2,1)} %copy-done.9) | copy-start | bytes 1572868
  118.5 13.2 %collective-permute-start.15 = (bf16[256,512]{1,0:T(8,128)(2,1)S(1)}, bf16[256,512]{1,0:T(8,128)(2,1)S(1)}, u32[]{:S(2)}, u32[]{:S(2)}) collective-permute-start(bf16[256,512]{1,0:T(8,128)(2,1)S(1)} %get-tuple-element.33), channel_id=1, source_target_pairs={{0,16},{16,0},{1,17},{17,1},{2,18},{18,2},{3,19},{19,3},{4,20},{20... | collective-permute-start | bytes 786440 | tf_op jit(solution)/shard_map/ppermute | solution.py:246
  122.9 10.3 %collective-permute-start.16 = (bf16[256,512]{1,0:T(8,128)(2,1)S(1)}, bf16[256,512]{1,0:T(8,128)(2,1)S(1)}, u32[]{:S(2)}, u32[]{:S(2)}) collective-permute-start(bf16[256,512]{1,0:T(8,128)(2,1)S(1)} %get-tuple-element.34), channel_id=1, source_target_pairs={{0,16},{16,0},{1,17},{17,1},{2,18},{18,2},{3,19},{19,3},{4,20},{20... | collective-permute-start | bytes 786440 | tf_op jit(solution)/shard_map/ppermute | solution.py:246
  126.6 17.5 %copy-start.4 = (bf16[256,4096]{1,0:T(8,128)(2,1)S(1)}, bf16[256,4096]{1,0:T(8,128)(2,1)}, u32[]{:S(2)}) copy-start(bf16[256,4096]{1,0:T(8,128)(2,1)} %gate_ref.1) | copy-start | bytes 6291460
  126.6 17.4 %copy-start.11 = (f32[4096]{0:T(1024)S(1)}, f32[4096]{0:T(1024)}, u32[]{:S(2)}) copy-start(f32[4096]{0:T(1024)} %param.11) | copy-start | bytes 49156
  126.6 12.3 %collective-permute-start.17 = (bf16[256,512]{1,0:T(8,128)(2,1)S(1)}, bf16[256,512]{1,0:T(8,128)(2,1)S(1)}, u32[]{:S(2)}, u32[]{:S(2)}) collective-permute-start(bf16[256,512]{1,0:T(8,128)(2,1)S(1)} %get-tuple-element.35), channel_id=1, source_target_pairs={{0,16},{16,0},{1,17},{17,1},{2,18},{18,2},{3,19},{19,3},{4,20},{20... | collective-permute-start | bytes 786440 | tf_op jit(solution)/shard_map/ppermute | solution.py:246
  131.0 13.0 %collective-permute-start.18 = (bf16[256,512]{1,0:T(8,128)(2,1)S(1)}, bf16[256,512]{1,0:T(8,128)(2,1)S(1)}, u32[]{:S(2)}, u32[]{:S(2)}) collective-permute-start(bf16[256,512]{1,0:T(8,128)(2,1)S(1)} %get-tuple-element.36), channel_id=1, source_target_pairs={{0,16},{16,0},{1,17},{17,1},{2,18},{18,2},{3,19},{19,3},{4,20},{20... | collective-permute-start | bytes 786440 | tf_op jit(solution)/shard_map/ppermute | solution.py:246

commit v3 on v2

v3 whole, which is shorter than its diff:
```python
import functools

import jax
import jax.numpy as jnp
from jax import lax
from jax.experimental import pallas as pl
from jax.experimental.pallas import tpu as pltpu
from jax.sharding import PartitionSpec as P

HEAD_DIM = 128
WINDOW = 512
EPSILON = 1e-06
LOG2E = 1.4426950408889634
LEVEL_LANES = 16
SIZES = (1, 2, 1, 2, 1, 1)
VMEM = 24 * 1024 * 1024
NN = (((1,), (0,)), ((), ()))
NT = (((1,), (1,)), ((), ()))
TN = (((0,), (0,)), ((), ()))


def mm(left, right, dims=NN):
    return lax.dot_general(left, right, dims, preferred_element_type=jnp.float32)


def level_scale(levels):
    return jnp.exp2(-0.5 * jnp.maximum(levels - 1, 0).astype(jnp.float32))


def joined(parts, axis):
    return parts[0] if len(parts) == 1 else jnp.concatenate(parts, axis)


def cost(micros):
    return pl.CostEstimate(
        flops=int(micros * 1.1e9), bytes_accessed=int(micros * 3.6e6), transcendentals=0
    )


def state_kernel(heads, k_ref, v_ref, out_ref, copy_ref):
    for h in range(heads):
        cols = slice(h * HEAD_DIM, (h + 1) * HEAD_DIM)
        out_ref[h] = mm(k_ref[:, cols], v_ref[:, cols], TN).astype(jnp.bfloat16)

    @pl.when(pl.program_id(0) == 0)
    def _():
        copy_ref[0] = k_ref[:, : copy_ref.shape[2]]
        copy_ref[1] = v_ref[:, : copy_ref.shape[2]]


def block_states(k, v, copied):
    rows, width = k.shape
    heads = width // HEAD_DIM
    step = 4 if heads % 4 == 0 else 1
    block = pl.BlockSpec((rows, step * HEAD_DIM), lambda g: (0, g))
    copy_shape = (2, rows, copied * HEAD_DIM)
    return pl.pallas_call(
        functools.partial(state_kernel, step),
        grid=(heads // step,),
        in_specs=[block, block],
        out_specs=[pl.BlockSpec((step, HEAD_DIM, HEAD_DIM), lambda g: (g, 0, 0)), pl.BlockSpec(copy_shape, lambda g: (0, 0, 0))],
        out_shape=[
            jax.ShapeDtypeStruct((heads, HEAD_DIM, HEAD_DIM), jnp.bfloat16),
            jax.ShapeDtypeStruct(copy_shape, k.dtype),
        ],
        cost_estimate=cost(0.3 * heads),
        name="block_states",
    )(k, v)


def attend_kernel(qb, heads, near_n, slots, place_ref, q_ref, k_ref, v_ref, past_ref, lw_ref, table_ref, *rest):
    bucket_refs, out_refs, mixed = rest[: -1 - slots], rest[-1 - slots : -1], rest[-1]
    rows = q_ref.shape[0]
    odd = place_ref[1] == 1
    for h in range(heads):
        cols = slice(h * HEAD_DIM, (h + 1) * HEAD_DIM)
        buckets = [bucket_refs[0][h]]
        for mine_ref, theirs_ref in zip(bucket_refs[1::2], bucket_refs[2::2]):
            mine, theirs = mine_ref[h], theirs_ref[h]
            buckets += [jnp.where(odd, theirs, mine), jnp.where(odd, mine, theirs)]
        tensors = [ref.at[:, cols] for ref in (q_ref, k_ref, v_ref, past_ref.at[0], past_ref.at[1])]
        attend_head(qb, place_ref, *tensors, lw_ref, table_ref, joined(buckets, 0), mixed.at[:, cols], h, near_n)
    count = rows // slots
    for s in range(slots):
        start = pl.multiple_of(lax.rem(place_ref[0] + s, slots) * count, count)
        out_refs[s][...] = mixed[pl.ds(start, count), :].astype(jnp.bfloat16)


def attend_head(qb, place_ref, q_ref, k_ref, v_ref, kp_ref, vp_ref, lw_ref, table_ref, bucket, out_ref, head, near_n):
    rows = q_ref.shape[0]
    lane = HEAD_DIM
    scale = HEAD_DIM**-0.5 * LOG2E
    bias = jnp.where(place_ref[2] == 0, -1e30, 0.0).astype(jnp.float32)
    table = table_ref[head]
    causal = lax.broadcasted_iota(jnp.int32, (qb, qb), 0) >= lax.broadcasted_iota(
        jnp.int32, (qb, qb), 1
    )
    lane_bits = lane.bit_length() - 1
    first_level = head * LEVEL_LANES
    for low in range(0, rows, qb):
        high = low + qb
        q = q_ref[low:high, :]
        own = mm(q, k_ref[:high, :], NT)
        past = mm(q, kp_ref[low:, :], NT)
        edge = jnp.where(causal, own[:, low:], past[:, :qb] + bias)
        top = jnp.max(edge, axis=1, keepdims=True)
        if low:
            top = jnp.maximum(top, jnp.max(own[:, :low], axis=1, keepdims=True))
        if high < rows:
            top = jnp.maximum(top, jnp.max(past[:, qb:], axis=1, keepdims=True) + bias)
        edge = jnp.exp2((edge - top) * scale)
        total = jnp.sum(edge, axis=1, keepdims=True)
        own_weights = [jnp.where(causal, edge, 0.0).astype(jnp.bfloat16)]
        past_weights = [jnp.where(causal, 0.0, edge).astype(jnp.bfloat16)]
        if low:
            inner = jnp.exp2((own[:, :low] - top) * scale)
            total = total + jnp.sum(inner, axis=1, keepdims=True)
            own_weights.insert(0, inner.astype(jnp.bfloat16))
        if high < rows:
            outer = jnp.exp2((past[:, qb:] - (top - bias)) * scale)
            total = total + jnp.sum(outer, axis=1, keepdims=True)
            past_weights.append(outer.astype(jnp.bfloat16))
        windowed = mm(joined(own_weights, 1), v_ref[:high, :])
        windowed = windowed + mm(joined(past_weights, 1), vp_ref[low:, :])
        near_rows, far_rows = [], []
        far_n = bucket.shape[0] // lane
        for a in range(low // lane, high // lane):
            inside = slice(a * lane - low, (a + 1) * lane - low)
            mix = lw_ref[0, a * lane : (a + 1) * lane, :]
            parts = []
            for b in range(high // lane):
                scores = own[inside, b * lane : (b + 1) * lane]
                if b < a:
                    level = first_level + lane_bits + (a ^ b).bit_length()
                    parts.append((scores * mix[:, level : level + 1]).astype(jnp.bfloat16))
                elif b == a:
                    picked = jnp.take_along_axis(mix, table, axis=1)
                    parts.append((scores * picked).astype(jnp.bfloat16))
                else:
                    parts.append(jnp.zeros((lane, lane), jnp.bfloat16))
            near_rows.append(joined(parts, 1))
            q_part = q[inside, :].astype(jnp.float32)
            level = first_level + near_n
            far_parts = [
                (q_part * mix[:, level + j : level + j + 1]).astype(jnp.bfloat16) for j in range(far_n)
            ]
            far_rows.append(joined(far_parts, 1))
        near = mm(joined(near_rows, 0), v_ref[:high, :])
        near = near + mm(joined(far_rows, 0), bucket)
        out_ref[low:high, :] = windowed * (1.0 / total) + near


def attend(place, q, k, v, past, lw, table, buckets, head, step, near_n, slots):
    rows, width = past.shape[1:]
    cols = step * HEAD_DIM
    count = rows // slots
    whole = pl.BlockSpec((rows, cols), lambda g, *_: (0, head // step + g))
    group = lambda g, *_: (head // step + g, 0, 0)
    qb = min(rows, 256)
    return pl.pallas_call(
        functools.partial(attend_kernel, qb, step, near_n, slots),
        grid_spec=pltpu.PrefetchScalarGridSpec(
            num_scalar_prefetch=1,
            grid=(width // cols,),
            in_specs=[
                whole,
                whole,
                whole,
                pl.BlockSpec((2, rows, cols), lambda g, *_: (0, 0, g)),
                pl.BlockSpec((1,) + lw.shape[1:], group),
                pl.BlockSpec(table.shape, lambda g, *_: (0, 0, 0)),
            ]
            + [pl.BlockSpec((step,) + b.shape[1:], group) for b in buckets],
            out_specs=[pl.BlockSpec((count, cols), lambda g, *_: (0, g))] * slots,
            scratch_shapes=[pltpu.VMEM((rows, cols), jnp.float32)],
        ),
        out_shape=[jax.ShapeDtypeStruct((count, width), jnp.bfloat16)] * slots,
        compiler_params=pltpu.CompilerParams(vmem_limit_bytes=VMEM),
        cost_estimate=cost(1.6 * width / HEAD_DIM),
        name="attend",
    )(place, q, k, v, past, lw, table, *buckets)


def norm_kernel(slots, offsets, local_width, place_ref, gate_ref, gain_ref, *rest):
    pieces, (out_ref, gated) = rest[:-2], rest[-2:]
    square = None
    index = 0
    for s in range(slots):
        base = lax.rem(place_ref[0] + slots - s, slots) * local_width
        for offset in offsets:
            piece = pieces[index]
            index += 1
            cols = pl.ds(pl.multiple_of(base + offset, HEAD_DIM), piece.shape[1])
            gate = gate_ref[:, cols].astype(jnp.float32)
            value = piece[...].astype(jnp.float32) * (gate / (1.0 + jnp.exp(-gate)))
            gated[:, cols] = value
            here = jnp.sum(value * value, axis=1, keepdims=True)
            square = here if square is None else square + here
    factor = lax.rsqrt(square / gated.shape[1] + EPSILON)
    out_ref[...] = (gain_ref[...] * gated[...] * factor).astype(jnp.bfloat16)


def norm(place, gate, gain, pieces, slots, offsets, local_width):
    rows, width = gate.shape
    tile = min(rows, 64)
    return pl.pallas_call(
        functools.partial(norm_kernel, slots, offsets, local_width),
        grid_spec=pltpu.PrefetchScalarGridSpec(
            num_scalar_prefetch=1,
            grid=(rows // tile,),
            in_specs=[
                pl.BlockSpec((tile, width), lambda g, *_: (g, 0)),
                pl.BlockSpec((1, width), lambda g, *_: (0, 0)),
            ]
            + [pl.BlockSpec((tile, p.shape[1]), lambda g, *_: (g, 0)) for p in pieces],
            out_specs=pl.BlockSpec((tile, width), lambda g, *_: (g, 0)),
            scratch_shapes=[pltpu.VMEM((tile, width), jnp.float32)],
        ),
        out_shape=jax.ShapeDtypeStruct((rows, width), jnp.bfloat16),
        compiler_params=pltpu.CompilerParams(vmem_limit_bytes=VMEM),
        cost_estimate=cost(3.2),
        name="norm",
    )(place, gate, gain.reshape(1, width), *pieces)


def shifted(value, axis, steps):
    count = lax.axis_size(axis)
    return lax.ppermute(value, axis, [(i, (i + steps) % count) for i in range(count)])


def from_partner(value, axis, level):
    return lax.ppermute(value, axis, [(i, i ^ 1 << level) for i in range(lax.axis_size(axis))])


def added(left, right):
    return (left.astype(jnp.float32) + right.astype(jnp.float32)).astype(jnp.bfloat16)


def after(value, *earlier):
    return lax.optimization_barrier((value,) + earlier)[0]


def local(queries, key_vectors, values, level_weights, gate_branch, norm_gain):
    rows, local_width = queries.shape
    heads = local_width // HEAD_DIM
    near_n = rows.bit_length()
    levels = level_weights.shape[0]
    far_n = levels - near_n
    slots = lax.axis_size("heads")
    seq_place = lax.axis_index("seq")
    heads_place = lax.axis_index("heads")
    place = jnp.stack([heads_place, seq_place & 1, seq_place])
    unit = heads // 8
    sizes = [n * unit for n in SIZES] if heads % 8 == 0 else [1] * heads
    starts = [sum(sizes[:i]) for i in range(len(sizes))]
    step = min(sizes)

    coef = level_scale(jnp.arange(levels, dtype=jnp.int32)) * HEAD_DIM**-0.5
    far_id = jnp.arange(levels, dtype=jnp.int32) - near_n
    present = jnp.where(far_id < 0, 1, seq_place >> jnp.maximum(far_id, 0) & 1)
    coef = coef * present.astype(jnp.float32)
    lw = (level_weights * coef[:, None, None]).reshape(levels, heads // step, step, rows)
    lw = jnp.pad(jnp.transpose(lw, (1, 3, 2, 0)), ((0, 0), (0, 0), (0, 0), (0, LEVEL_LANES - levels)))
    lw = lw.reshape(heads // step, rows, step * LEVEL_LANES)
    lw = jnp.pad(lw, ((0, 0), (0, 0), (0, HEAD_DIM - step * LEVEL_LANES)))
    pos = jnp.arange(HEAD_DIM, dtype=jnp.int32)
    differ = pos[:, None] ^ pos[None, :]
    table = sum((differ >> b > 0).astype(jnp.int32) for b in range(HEAD_DIM.bit_length()))
    table = table + LEVEL_LANES * jnp.arange(step, dtype=jnp.int32)[:, None, None]
    table = jnp.where(pos[:, None] >= pos[None, :], table, HEAD_DIM - 1)

    past = []

    def send_until(count, *earlier):
        for index in range(len(past), min(count, len(sizes))):
            past.append(shifted(after(cuts[index], *earlier), "seq", 1))

    half = HEAD_DIM // 2
    states, cut = block_states(key_vectors, values, sizes[0])
    cuts = [cut]
    send_until(1)
    other = from_partner(states, "seq", 0)
    buckets = [other]
    running = lax.dynamic_slice_in_dim(added(states, other), (seq_place & 1) * half, half, 1)
    whole = lax.optimization_barrier((key_vectors, values, running))[:2]
    for start, size in zip(starts[1:], sizes[1:]):
        cols = slice(start * HEAD_DIM, (start + size) * HEAD_DIM)
        cuts.append(jnp.stack([w[:, cols] for w in whole]))
    for level in range(1, far_n):
        other = from_partner(running, "seq", level)
        if level < far_n - 1:
            send_until(1 + level, running)
            running = added(running, other)
        buckets += [other, from_partner(other, "seq", 0)]
    send_until(len(sizes), other)

    kept = [[] for _ in range(slots)]
    latest = ()
    for index in range(len(sizes)):
        pieces = attend(
            place, queries, key_vectors, values, after(past[index], *latest), lw, table, buckets,
            starts[index], step, near_n, slots,
        )
        latest = (pieces[-1],)
        for s in range(slots):
            kept[s].append(pieces[s] if s == 0 else shifted(pieces[s], "heads", s))
    pieces = [piece for group in kept for piece in group]
    offsets = tuple(start * HEAD_DIM for start in starts)
    return norm(heads_place.reshape(1), gate_branch, norm_gain, pieces, slots, offsets, local_width)


def solution(mesh):
    return jax.shard_map(
        local,
        mesh=mesh,
        in_specs=(
            P("seq", "heads"),
            P("seq", "heads"),
            P("seq", "heads"),
            P(None, "heads", "seq"),
            P(("seq", "heads"), None),
            P(),
        ),
        out_specs=P(("seq", "heads"), None),
        check_vma=False,
    )
```

time: 148 us -> 99.3 us (0.67)
  starting transfers between devices: 53.5 us -> 24 us
  Pallas kernels: 44.8 us -> 35.4 us
  local copies, waits for them, and re-layouts: 10.7 us -> 3.29 us
  waiting for transfers between devices: 35.4 us -> 32.5 us
    ppermute x12, starting transfers between devices: 47.6 us -> 17.7 us  [shifted(): lax.ppermute(value, axis, [(i, (i + steps) % count) for i in range(count)])]
    ppermute x12, waiting for transfers between devices: 16.4 us -> 4.81 us  [shifted(): lax.ppermute(value, axis, [(i, (i + steps) % count) for i in range(count)])]
    pallas_call x8 -> x6, Pallas kernels: 36.9 us -> 27.3 us  [attend(): pl.pallas_call(functools.partial(attend_kernel, qb, step, near_n, slots),...]
    ppermute x7, waiting for transfers between devices: 19 us -> 27.7 us  [from_partner(): lax.ppermute(value, axis, [(i, i ^ 1 << level) for i in range(lax.axis_si...]
    unnamed x24 -> x12, local copies, waits for them, and re-layouts: 7.67 us -> 0.04 us
    slice x1 -> x0, local copies, waits for them, and re-layouts: 3.04 us -> none  [halo(): pair = (key_vectors[:, cols], values[:, cols])]
    convert_element_type x3, other arithmetic: 1.17 us -> 2.85 us  [added(): (left.astype(jnp.float32) + right.astype(jnp.float32)).astype(jnp.bfloat16)]
    reshape x0 -> x1, local copies, waits for them, and re-layouts: none -> 1.64 us  [local(): lw = lw.reshape(heads // step, rows, step * LEVEL_LANES)]
  transfers between devices with their start and end apart: 19 -> 19, of which waited for: 8 -> 6; matrix products, arithmetic and copies ran while one was open for 3% -> 7% of each run, Pallas kernels for 23% -> 28%
where the time goes in v3:
time: 99.3 us; the launch traced here: 99.1 us
  Pallas kernels  35.4 us (36%)
  waiting for transfers between devices  32.5 us (33%)
  starting transfers between devices  24 us (24%)
  other arithmetic  3.55 us (4%)
  local copies, waits for them, and re-layouts  3.29 us (3%)
    ppermute x7, waiting for transfers between devices, from_partner(): lax.ppermute(value, axis, [(i, i ^ 1 << level) for i in range(lax.axis_si...  27.7 us
    pallas_call x6, Pallas kernels, attend(): pl.pallas_call(functools.partial(attend_kernel, qb, step, near_n, slots),...  27.3 us
    ppermute x12, starting transfers between devices, shifted(): lax.ppermute(value, axis, [(i, (i + steps) % count) for i in range(count)])  17.7 us
    ppermute x7, starting transfers between devices, from_partner(): lax.ppermute(value, axis, [(i, i ^ 1 << level) for i in range(lax.axis_si...  6.33 us
    ppermute x12, waiting for transfers between devices, shifted(): lax.ppermute(value, axis, [(i, (i + steps) % count) for i in range(count)])  4.81 us
    pallas_call x1, Pallas kernels, block_states(): pl.pallas_call(functools.partial(state_kernel, step), grid=(heads // step...  4.74 us
    pallas_call x1, Pallas kernels, norm(): pl.pallas_call(functools.partial(norm_kernel, slots, offsets, local_width...  3.3 us
    convert_element_type x3, other arithmetic, added(): (left.astype(jnp.float32) + right.astype(jnp.float32)).astype(jnp.bfloat16)  2.85 us
  transfers between devices with their start and end apart: 19, of which 6 were waited for; matrix products, arithmetic and copies ran while one was open for 7% of the time, Pallas kernels for 28%

profile of v3, /device:TPU:0, one launch (start us, length us, event | category | flops | bytes accessed | tf_op | source)
XLA Modules:
  0.0 99.1 jit_solution(18102524469558918523)
XLA Ops:
  0.0 4.7 %block_states.1 = (bf16[16,128,128]{2,1,0:T(8,128)(2,1)}, bf16[2,512,256]{2,1,0:T(8,128)(2,1)}) custom-call(bf16[512,2048]{1,0:T(8,128)(2,1)} %k_ref.13, bf16[512,2048]{1,0:T(8,128)(2,1)} %v_ref.13), custom_call_target="tpu_custom_call" | custom-call | flops 5280000000 | bytes 17280000 | tf_op jit(solution)/shard_map/block_states/pallas_call | solution.py:57
  4.7 0.5 collective-permute-start
  5.2 2.6 %collective-permute-start.1 = (bf16[16,128,128]{2,1,0:T(8,128)(2,1)}, bf16[16,128,128]{2,1,0:T(8,128)(2,1)S(1)}, u32[]{:S(2)}, u32[]{:S(2)}) collective-permute-start(bf16[16,128,128]{2,1,0:T(8,128)(2,1)} %get-tuple-element.32), channel_id=1, source_target_pairs={{0,1},{1,0},{2,3},{3,2},{4,5},{5,4},{6,7},{7,6},{8,9},{9,8},{10,11... | collective-permute-start | bytes 1572872 | tf_op jit(solution)/shard_map/ppermute | solution.py:232
  7.9 0.1 convert_add_fusion
  8.0 0.1 broadcast_multiply_fusion
  8.1 1.5 %collective-permute-done.1.rest_0_ = bf16[16,128,128]{2,1,0:T(8,128)(2,1)S(1)} collective-permute-done((bf16[16,128,128]{2,1,0:T(8,128)(2,1)}, bf16[16,128,128]{2,1,0:T(8,128)(2,1)S(1)}, u32[]{:S(2)}, u32[]{:S(2)}) %collective-permute-start.1) | collective-permute-done | bytes 524320 | tf_op jit(solution)/shard_map/ppermute | solution.py:232
  9.6 1.8 %add_convert_fusion.2 = bf16[16,64,128]{2,1,0:T(8,128)(2,1)} fusion(bf16[16,128,128]{2,1,0:T(8,128)(2,1)S(1)} %collective-permute-done.1.rest_0_, s32[]{:T(128)S(6)} %select_n.27, bf16[16,128,128]{2,1,0:T(8,128)(2,1)} %get-tuple-element.32), kind=kLoop, calls=%fused_computation.11 | loop fusion | flops 524288 | bytes 786436 | tf_op jit(solution)/shard_map/convert_element_type | solution.py:236
  11.3 1.5 %collective-permute-start.2 = (bf16[16,64,128]{2,1,0:T(8,128)(2,1)}, bf16[16,64,128]{2,1,0:T(8,128)(2,1)S(1)}, u32[]{:S(2)}, u32[]{:S(2)}) collective-permute-start(bf16[16,64,128]{2,1,0:T(8,128)(2,1)} %add_convert_fusion.2), channel_id=1, source_target_pairs={{0,2},{1,3},{2,0},{3,1},{4,6},{5,7},{6,4},{7,5},{8,10},{9,11},{10,... | collective-permute-start | bytes 786440 | tf_op jit(solution)/shard_map/ppermute | solution.py:232
  12.9 0.1 pad_add_fusion.place_ref
  12.9 0.3 copy.8
  13.2 0.8 pad.8
  14.1 1.6 %copy.9 = f32[8,512,32]{2,1,0:T(8,128)S(1)} copy(f32[8,512,32]{1,2,0:T(8,128)} %bitcast.29) | data formatting | bytes 1048576 | tf_op jit(solution)/shard_map/reshape | solution.py:264
  15.7 0.2 pad.9.lw_ref
  15.9 0.1 add_select_fusion.table_ref
  16.0 6.9 %collective-permute-done.2.rest_1_ = bf16[16,64,128]{2,1,0:T(8,128)(2,1)S(1)} collective-permute-done((bf16[16,64,128]{2,1,0:T(8,128)(2,1)}, bf16[16,64,128]{2,1,0:T(8,128)(2,1)S(1)}, u32[]{:S(2)}, u32[]{:S(2)}) %collective-permute-start.2) | collective-permute-done | bytes 262176 | tf_op jit(solution)/shard_map/ppermute | solution.py:232
  22.9 1.0 %add_convert_fusion.1 = bf16[16,64,128]{2,1,0:T(8,128)(2,1)S(1)} fusion(bf16[16,64,128]{2,1,0:T(8,128)(2,1)S(1)} %collective-permute-done.2.rest_1_, bf16[16,64,128]{2,1,0:T(8,128)(2,1)} %add_convert_fusion.2), kind=kLoop, calls=%fused_computation.10 | loop fusion | flops 524288 | bytes 786432 | tf_op jit(solution)/shard_map/convert_element_type | solution.py:236
  23.9 0.3 collective-permute-start.4
  24.2 0.2 slice_bitcast_fusion
  24.4 0.1 pad_maximum_fusion
  24.5 0.1 collective-permute-start.8
  24.6 7.7 %collective-permute-done.4.rest_3_ = bf16[16,64,128]{2,1,0:T(8,128)(2,1)S(1)} collective-permute-done((bf16[16,64,128]{2,1,0:T(8,128)(2,1)S(1)}, bf16[16,64,128]{2,1,0:T(8,128)(2,1)S(1)}, u32[]{:S(2)}, u32[]{:S(2)}) %collective-permute-start.4) | collective-permute-done | bytes 262176 | tf_op jit(solution)/shard_map/ppermute | solution.py:232
  32.3 0.1 add_convert_fusion
  32.3 1.3 %collective-permute-start.6 = (bf16[16,64,128]{2,1,0:T(8,128)(2,1)S(1)}, bf16[16,64,128]{2,1,0:T(8,128)(2,1)S(1)}, u32[]{:S(2)}, u32[]{:S(2)}) collective-permute-start(bf16[16,64,128]{2,1,0:T(8,128)(2,1)S(1)} %add_convert_fusion), channel_id=1, source_target_pairs={{0,8},{1,9},{2,10},{3,11},{4,12},{5,13},{6,14},{7,15},{8,0},{9,1},... | collective-permute-start | bytes 786440 | tf_op jit(solution)/shard_map/ppermute | solution.py:232
  33.6 0.1 slice_bitcast_fusion.4
  33.8 0.1 pad_maximum_fusion.2
  33.9 0.1 collective-permute-start.3
  34.0 0.5 collective-permute-start.5
  34.5 11.6 %collective-permute-done.6.rest_5_ = bf16[16,64,128]{2,1,0:T(8,128)(2,1)S(1)} collective-permute-done((bf16[16,64,128]{2,1,0:T(8,128)(2,1)S(1)}, bf16[16,64,128]{2,1,0:T(8,128)(2,1)S(1)}, u32[]{:S(2)}, u32[]{:S(2)}) %collective-permute-start.6) | collective-permute-done | bytes 262176 | tf_op jit(solution)/shard_map/ppermute | solution.py:232
  46.2 0.1 pad_maximum_fusion.1
  46.3 0.5 collective-permute-start.9
  46.9 9.4 %collective-permute-start.10 = (bf16[2,512,512]{2,1,0:T(8,128)(2,1)S(1)}, bf16[2,512,512]{2,1,0:T(8,128)(2,1)S(1)}, u32[]{:S(2)}, u32[]{:S(2)}) collective-permute-start(bf16[2,512,512]{2,1,0:T(8,128)(2,1)S(1)} %pad_maximum_fusion.1), channel_id=1, source_target_pairs={{0,1},{1,2},{2,3},{3,4},{4,5},{5,6},{6,7},{7,8},{8,9},{9,10},{10,1... | collective-permute-start | bytes 3145736 | tf_op jit(solution)/shard_map/ppermute | solution.py:228
  56.2 0.5 collective-permute-start.11
  56.8 0.2 collective-permute-start.12
  57.0 3.4 %attend.6 = (bf16[256,256]{1,0:T(8,128)(2,1)S(1)}, bf16[256,256]{1,0:T(8,128)(2,1)S(1)}) custom-call(s32[3]{0:T(128)S(1)} %pad_add_fusion.place_ref, bf16[512,2048]{1,0:T(8,128)(2,1)S(1)} %copy-done.2, bf16[512,2048]{1,0:T(8,128)(2,1)S(1)} %copy-done, bf16[512,2048]{1,0:T(8,128)(2,1)S(1)} %copy-done.1, ...), custom_call_target="tpu_custom_call" | custom-call | flops 3520000000 | bytes 11520000 | tf_op jit(solution)/shard_map/attend/pallas_call | solution.py:160
  60.4 1.6 %collective-permute-start.13 = (bf16[256,256]{1,0:T(8,128)(2,1)S(1)}, bf16[256,256]{1,0:T(8,128)(2,1)S(1)}, u32[]{:S(2)}, u32[]{:S(2)}) collective-permute-start(bf16[256,256]{1,0:T(8,128)(2,1)S(1)} %get-tuple-element.37), channel_id=1, source_target_pairs={{0,16},{16,0},{1,17},{17,1},{2,18},{18,2},{3,19},{19,3},{4,20},{20... | collective-permute-start | bytes 393224 | tf_op jit(solution)/shard_map/ppermute | solution.py:228
  62.0 6.7 %attend.7 = (bf16[256,512]{1,0:T(8,128)(2,1)S(1)}, bf16[256,512]{1,0:T(8,128)(2,1)S(1)}) custom-call(s32[3]{0:T(128)S(1)} %pad_add_fusion.place_ref, bf16[512,2048]{1,0:T(8,128)(2,1)S(1)} %copy-done.2, bf16[512,2048]{1,0:T(8,128)(2,1)S(1)} %copy-done, bf16[512,2048]{1,0:T(8,128)(2,1)S(1)} %copy-done.1, ...), custom_call_target="tpu_custom_call" | custom-call | flops 7040000000 | bytes 23040000 | tf_op jit(solution)/shard_map/attend/pallas_call | solution.py:160
  68.7 0.6 collective-permute-start.14
  69.3 3.4 %attend.8 = (bf16[256,256]{1,0:T(8,128)(2,1)S(1)}, bf16[256,256]{1,0:T(8,128)(2,1)S(1)}) custom-call(s32[3]{0:T(128)S(1)} %pad_add_fusion.place_ref, bf16[512,2048]{1,0:T(8,128)(2,1)S(1)} %copy-done.2, bf16[512,2048]{1,0:T(8,128)(2,1)S(1)} %copy-done, bf16[512,2048]{1,0:T(8,128)(2,1)S(1)} %copy-done.1, ...), custom_call_target="tpu_custom_call" | custom-call | flops 3520000000 | bytes 11520000 | tf_op jit(solution)/shard_map/attend/pallas_call | solution.py:160
  72.8 1.6 %collective-permute-start.15 = (bf16[256,256]{1,0:T(8,128)(2,1)S(1)}, bf16[256,256]{1,0:T(8,128)(2,1)S(1)}, u32[]{:S(2)}, u32[]{:S(2)}) collective-permute-start(bf16[256,256]{1,0:T(8,128)(2,1)S(1)} %get-tuple-element.45), channel_id=1, source_target_pairs={{0,16},{16,0},{1,17},{17,1},{2,18},{18,2},{3,19},{19,3},{4,20},{20... | collective-permute-start | bytes 393224 | tf_op jit(solution)/shard_map/ppermute | solution.py:228
  74.3 6.9 %attend.9 = (bf16[256,512]{1,0:T(8,128)(2,1)S(1)}, bf16[256,512]{1,0:T(8,128)(2,1)S(1)}) custom-call(s32[3]{0:T(128)S(1)} %pad_add_fusion.place_ref, bf16[512,2048]{1,0:T(8,128)(2,1)S(1)} %copy-done.2, bf16[512,2048]{1,0:T(8,128)(2,1)S(1)} %copy-done, bf16[512,2048]{1,0:T(8,128)(2,1)S(1)} %copy-done.1, ...), custom_call_target="tpu_custom_call" | custom-call | flops 7040000000 | bytes 23040000 | tf_op jit(solution)/shard_map/attend/pallas_call | solution.py:160
  81.3 0.6 collective-permute-start.16
  81.9 3.4 %attend.10 = (bf16[256,256]{1,0:T(8,128)(2,1)S(1)}, bf16[256,256]{1,0:T(8,128)(2,1)S(1)}) custom-call(s32[3]{0:T(128)S(1)} %pad_add_fusion.place_ref, bf16[512,2048]{1,0:T(8,128)(2,1)S(1)} %copy-done.2, bf16[512,2048]{1,0:T(8,128)(2,1)S(1)} %copy-done, bf16[512,2048]{1,0:T(8,128)(2,1)S(1)} %copy-done.1, ...), custom_call_target="tpu_custom_call" | custom-call | flops 3520000000 | bytes 11520000 | tf_op jit(solution)/shard_map/attend/pallas_call | solution.py:160
  85.4 1.5 %collective-permute-start.17 = (bf16[256,256]{1,0:T(8,128)(2,1)S(1)}, bf16[256,256]{1,0:T(8,128)(2,1)S(1)}, u32[]{:S(2)}, u32[]{:S(2)}) collective-permute-start(bf16[256,256]{1,0:T(8,128)(2,1)S(1)} %get-tuple-element.53), channel_id=1, source_target_pairs={{0,16},{16,0},{1,17},{17,1},{2,18},{18,2},{3,19},{19,3},{4,20},{20... | collective-permute-start | bytes 393224 | tf_op jit(solution)/shard_map/ppermute | solution.py:228
  86.9 3.4 %attend.11 = (bf16[256,256]{1,0:T(8,128)(2,1)S(1)}, bf16[256,256]{1,0:T(8,128)(2,1)S(1)}) custom-call(s32[3]{0:T(128)S(1)} %pad_add_fusion.place_ref, bf16[512,2048]{1,0:T(8,128)(2,1)S(1)} %copy-done.2, bf16[512,2048]{1,0:T(8,128)(2,1)S(1)} %copy-done, bf16[512,2048]{1,0:T(8,128)(2,1)S(1)} %copy-done.1, ...), custom_call_target="tpu_custom_call" | custom-call | flops 3520000000 | bytes 11520000 | tf_op jit(solution)/shard_map/attend/pallas_call | solution.py:160
  90.3 0.6 collective-permute-start.18
  91.0 1.9 %collective-permute-done.17.rest_10_ = bf16[256,256]{1,0:T(8,128)(2,1)S(1)} collective-permute-done((bf16[256,256]{1,0:T(8,128)(2,1)S(1)}, bf16[256,256]{1,0:T(8,128)(2,1)S(1)}, u32[]{:S(2)}, u32[]{:S(2)}) %collective-permute-start.17) | collective-permute-done | bytes 131104 | tf_op jit(solution)/shard_map/ppermute | solution.py:228
  92.9 2.9 %collective-permute-done.18.rest_11_ = bf16[256,256]{1,0:T(8,128)(2,1)S(1)} collective-permute-done((bf16[256,256]{1,0:T(8,128)(2,1)S(1)}, bf16[256,256]{1,0:T(8,128)(2,1)S(1)}, u32[]{:S(2)}, u32[]{:S(2)}) %collective-permute-start.18) | collective-permute-done | bytes 131104 | tf_op jit(solution)/shard_map/ppermute | solution.py:228
  95.8 3.3 %norm.1 = bf16[256,4096]{1,0:T(8,128)(2,1)} custom-call(s32[1]{0:T(128)} %bitcast.place_ref, bf16[256,4096]{1,0:T(8,128)(2,1)S(1)} %copy-done.3, f32[1,4096]{1,0:T(1,128)S(1)} %bitcast.28, bf16[256,256]{1,0:T(8,128)(2,1)S(1)} %get-tuple-element.33.rest_0_, bf16[256,512]{1,0:T(8,128)(2,1)S(1)} %get-tuple-element.39.rest_1_, ...), custom_call_target="tpu_custom_call" | custom-call | flops 3520000000 | bytes 11520000 | tf_op jit(solution)/shard_map/norm/pallas_call | solution.py:206
  (31 shorter events, 0.2 us)
Async XLA Ops:
  0.0 8.0 %copy-start.5 = (f32[14,16,512]{2,1,0:T(8,128)S(1)}, f32[14,16,512]{2,1,0:T(8,128)}, u32[]{:S(2)}) copy-start(f32[14,16,512]{2,1,0:T(8,128)} %param.9) | copy-start | bytes 1376260
  4.7 29.0 %collective-permute-start = (bf16[2,512,256]{2,1,0:T(8,128)(2,1)}, bf16[2,512,256]{2,1,0:T(8,128)(2,1)S(1)}, u32[]{:S(2)}, u32[]{:S(2)}) collective-permute-start(bf16[2,512,256]{2,1,0:T(8,128)(2,1)} %get-tuple-element.31), channel_id=1, source_target_pairs={{0,1},{1,2},{2,3},{3,4},{4,5},{5,6},{6,7},{7,8},{8,9},{9,10},{10,1... | collective-permute-start | bytes 1572872 | tf_op jit(solution)/shard_map/ppermute | solution.py:228
  5.2 4.4 %collective-permute-start.1 = (bf16[16,128,128]{2,1,0:T(8,128)(2,1)}, bf16[16,128,128]{2,1,0:T(8,128)(2,1)S(1)}, u32[]{:S(2)}, u32[]{:S(2)}) collective-permute-start(bf16[16,128,128]{2,1,0:T(8,128)(2,1)} %get-tuple-element.32), channel_id=1, source_target_pairs={{0,1},{1,0},{2,3},{3,2},{4,5},{5,4},{6,7},{7,6},{8,9},{9,8},{10,11... | collective-permute-start | bytes 1572872 | tf_op jit(solution)/shard_map/ppermute | solution.py:232
  11.3 11.6 %collective-permute-start.2 = (bf16[16,64,128]{2,1,0:T(8,128)(2,1)}, bf16[16,64,128]{2,1,0:T(8,128)(2,1)S(1)}, u32[]{:S(2)}, u32[]{:S(2)}) collective-permute-start(bf16[16,64,128]{2,1,0:T(8,128)(2,1)} %add_convert_fusion.2), channel_id=1, source_target_pairs={{0,2},{1,3},{2,0},{3,1},{4,6},{5,7},{6,4},{7,5},{8,10},{9,11},{10,... | collective-permute-start | bytes 786440 | tf_op jit(solution)/shard_map/ppermute | solution.py:232
  15.7 8.5 %copy-start = (bf16[512,2048]{1,0:T(8,128)(2,1)S(1)}, bf16[512,2048]{1,0:T(8,128)(2,1)}, u32[]{:S(2)}) copy-start(bf16[512,2048]{1,0:T(8,128)(2,1)} %k_ref.13) | copy-start | bytes 6291460
  15.7 8.5 %copy-start.1 = (bf16[512,2048]{1,0:T(8,128)(2,1)S(1)}, bf16[512,2048]{1,0:T(8,128)(2,1)}, u32[]{:S(2)}) copy-start(bf16[512,2048]{1,0:T(8,128)(2,1)} %v_ref.13) | copy-start | bytes 6291460
  23.9 8.3 %collective-permute-start.4 = (bf16[16,64,128]{2,1,0:T(8,128)(2,1)S(1)}, bf16[16,64,128]{2,1,0:T(8,128)(2,1)S(1)}, u32[]{:S(2)}, u32[]{:S(2)}) collective-permute-start(bf16[16,64,128]{2,1,0:T(8,128)(2,1)S(1)} %add_convert_fusion.1), channel_id=1, source_target_pairs={{0,4},{1,5},{2,6},{3,7},{4,0},{5,1},{6,2},{7,3},{8,12},{9,13},{10,... | collective-permute-start | bytes 786440 | tf_op jit(solution)/shard_map/ppermute | solution.py:232
  24.5 35.9 %collective-permute-start.8 = (bf16[2,512,512]{2,1,0:T(8,128)(2,1)S(1)}, bf16[2,512,512]{2,1,0:T(8,128)(2,1)S(1)}, u32[]{:S(2)}, u32[]{:S(2)}) collective-permute-start(bf16[2,512,512]{2,1,0:T(8,128)(2,1)S(1)} %pad_maximum_fusion), channel_id=1, source_target_pairs={{0,1},{1,2},{2,3},{3,4},{4,5},{5,6},{6,7},{7,8},{8,9},{9,10},{10,1... | collective-permute-start | bytes 3145736 | tf_op jit(solution)/shard_map/ppermute | solution.py:228
  32.3 13.8 %collective-permute-start.6 = (bf16[16,64,128]{2,1,0:T(8,128)(2,1)S(1)}, bf16[16,64,128]{2,1,0:T(8,128)(2,1)S(1)}, u32[]{:S(2)}, u32[]{:S(2)}) collective-permute-start(bf16[16,64,128]{2,1,0:T(8,128)(2,1)S(1)} %add_convert_fusion), channel_id=1, source_target_pairs={{0,8},{1,9},{2,10},{3,11},{4,12},{5,13},{6,14},{7,15},{8,0},{9,1},... | collective-permute-start | bytes 786440 | tf_op jit(solution)/shard_map/ppermute | solution.py:232
  33.8 23.2 %copy-start.2 = (bf16[512,2048]{1,0:T(8,128)(2,1)S(1)}, bf16[512,2048]{1,0:T(8,128)(2,1)}, u32[]{:S(2)}) copy-start(bf16[512,2048]{1,0:T(8,128)(2,1)} %q_ref.11) | copy-start | bytes 6291460
  33.9 12.9 %collective-permute-start.3 = (bf16[16,64,128]{2,1,0:T(8,128)(2,1)S(1)}, bf16[16,64,128]{2,1,0:T(8,128)(2,1)S(1)}, u32[]{:S(2)}, u32[]{:S(2)}) collective-permute-start(bf16[16,64,128]{2,1,0:T(8,128)(2,1)S(1)} %collective-permute-done.2.rest_1_), channel_id=1, source_target_pairs={{0,1},{1,0},{2,3},{3,2},{4,5},{5,4},{6,7},{7,6},{8,9},{9,8},{10,11... | collective-permute-start | bytes 786440 | tf_op jit(solution)/shard_map/ppermute | solution.py:232
  34.0 22.3 %collective-permute-start.5 = (bf16[16,64,128]{2,1,0:T(8,128)(2,1)S(1)}, bf16[16,64,128]{2,1,0:T(8,128)(2,1)S(1)}, u32[]{:S(2)}, u32[]{:S(2)}) collective-permute-start(bf16[16,64,128]{2,1,0:T(8,128)(2,1)S(1)} %collective-permute-done.4.rest_3_), channel_id=1, source_target_pairs={{0,1},{1,0},{2,3},{3,2},{4,5},{5,4},{6,7},{7,6},{8,9},{9,8},{10,11... | collective-permute-start | bytes 786440 | tf_op jit(solution)/shard_map/ppermute | solution.py:232
  46.1 10.6 %collective-permute-start.7 = (bf16[16,64,128]{2,1,0:T(8,128)(2,1)S(1)}, bf16[16,64,128]{2,1,0:T(8,128)(2,1)S(1)}, u32[]{:S(2)}, u32[]{:S(2)}) collective-permute-start(bf16[16,64,128]{2,1,0:T(8,128)(2,1)S(1)} %collective-permute-done.6.rest_5_), channel_id=1, source_target_pairs={{0,1},{1,0},{2,3},{3,2},{4,5},{5,4},{6,7},{7,6},{8,9},{9,8},{10,11... | collective-permute-start | bytes 786440 | tf_op jit(solution)/shard_map/ppermute | solution.py:232
  46.3 22.4 %collective-permute-start.9 = (bf16[2,512,256]{2,1,0:T(8,128)(2,1)S(1)}, bf16[2,512,256]{2,1,0:T(8,128)(2,1)S(1)}, u32[]{:S(2)}, u32[]{:S(2)}) collective-permute-start(bf16[2,512,256]{2,1,0:T(8,128)(2,1)S(1)} %pad_maximum_fusion.2), channel_id=1, source_target_pairs={{0,1},{1,2},{2,3},{3,4},{4,5},{5,6},{6,7},{7,8},{8,9},{9,10},{10,1... | collective-permute-start | bytes 1572872 | tf_op jit(solution)/shard_map/ppermute | solution.py:228
  46.9 25.9 %collective-permute-start.10 = (bf16[2,512,512]{2,1,0:T(8,128)(2,1)S(1)}, bf16[2,512,512]{2,1,0:T(8,128)(2,1)S(1)}, u32[]{:S(2)}, u32[]{:S(2)}) collective-permute-start(bf16[2,512,512]{2,1,0:T(8,128)(2,1)S(1)} %pad_maximum_fusion.1), channel_id=1, source_target_pairs={{0,1},{1,2},{2,3},{3,4},{4,5},{5,6},{6,7},{7,8},{8,9},{9,10},{10,1... | collective-permute-start | bytes 3145736 | tf_op jit(solution)/shard_map/ppermute | solution.py:228
  56.2 25.0 %collective-permute-start.11 = (bf16[2,512,256]{2,1,0:T(8,128)(2,1)S(1)}, bf16[2,512,256]{2,1,0:T(8,128)(2,1)S(1)}, u32[]{:S(2)}, u32[]{:S(2)}) collective-permute-start(bf16[2,512,256]{2,1,0:T(8,128)(2,1)S(1)} %pad_maximum_fusion.3), channel_id=1, source_target_pairs={{0,1},{1,2},{2,3},{3,4},{4,5},{5,6},{6,7},{7,8},{8,9},{9,10},{10,1... | collective-permute-start | bytes 1572872 | tf_op jit(solution)/shard_map/ppermute | solution.py:228
  56.8 28.6 %collective-permute-start.12 = (bf16[2,512,256]{2,1,0:T(8,128)(2,1)S(1)}, bf16[2,512,256]{2,1,0:T(8,128)(2,1)S(1)}, u32[]{:S(2)}, u32[]{:S(2)}) collective-permute-start(bf16[2,512,256]{2,1,0:T(8,128)(2,1)S(1)} %pad_maximum_fusion.4), channel_id=1, source_target_pairs={{0,1},{1,2},{2,3},{3,4},{4,5},{5,6},{6,7},{7,8},{8,9},{9,10},{10,1... | collective-permute-start | bytes 1572872 | tf_op jit(solution)/shard_map/ppermute | solution.py:228
  60.4 29.9 %collective-permute-start.13 = (bf16[256,256]{1,0:T(8,128)(2,1)S(1)}, bf16[256,256]{1,0:T(8,128)(2,1)S(1)}, u32[]{:S(2)}, u32[]{:S(2)}) collective-permute-start(bf16[256,256]{1,0:T(8,128)(2,1)S(1)} %get-tuple-element.37), channel_id=1, source_target_pairs={{0,16},{16,0},{1,17},{17,1},{2,18},{18,2},{3,19},{19,3},{4,20},{20... | collective-permute-start | bytes 393224 | tf_op jit(solution)/shard_map/ppermute | solution.py:228
  68.7 22.2 %collective-permute-start.14 = (bf16[256,512]{1,0:T(8,128)(2,1)S(1)}, bf16[256,512]{1,0:T(8,128)(2,1)S(1)}, u32[]{:S(2)}, u32[]{:S(2)}) collective-permute-start(bf16[256,512]{1,0:T(8,128)(2,1)S(1)} %get-tuple-element.41), channel_id=1, source_target_pairs={{0,16},{16,0},{1,17},{17,1},{2,18},{18,2},{3,19},{19,3},{4,20},{20... | collective-permute-start | bytes 786440 | tf_op jit(solution)/shard_map/ppermute | solution.py:228
  72.8 18.2 %collective-permute-start.15 = (bf16[256,256]{1,0:T(8,128)(2,1)S(1)}, bf16[256,256]{1,0:T(8,128)(2,1)S(1)}, u32[]{:S(2)}, u32[]{:S(2)}) collective-permute-start(bf16[256,256]{1,0:T(8,128)(2,1)S(1)} %get-tuple-element.45), channel_id=1, source_target_pairs={{0,16},{16,0},{1,17},{17,1},{2,18},{18,2},{3,19},{19,3},{4,20},{20... | collective-permute-start | bytes 393224 | tf_op jit(solution)/shard_map/ppermute | solution.py:228
  81.3 14.5 %collective-permute-start.16 = (bf16[256,512]{1,0:T(8,128)(2,1)S(1)}, bf16[256,512]{1,0:T(8,128)(2,1)S(1)}, u32[]{:S(2)}, u32[]{:S(2)}) collective-permute-start(bf16[256,512]{1,0:T(8,128)(2,1)S(1)} %get-tuple-element.49), channel_id=1, source_target_pairs={{0,16},{16,0},{1,17},{17,1},{2,18},{18,2},{3,19},{19,3},{4,20},{20... | collective-permute-start | bytes 786440 | tf_op jit(solution)/shard_map/ppermute | solution.py:228
  85.3 10.4 %copy-start.3 = (bf16[256,4096]{1,0:T(8,128)(2,1)S(1)}, bf16[256,4096]{1,0:T(8,128)(2,1)}, u32[]{:S(2)}) copy-start(bf16[256,4096]{1,0:T(8,128)(2,1)} %gate_ref.1) | copy-start | bytes 6291460
  85.3 10.4 %copy-start.4 = (f32[4096]{0:T(1024)S(1)}, f32[4096]{0:T(1024)}, u32[]{:S(2)}) copy-start(f32[4096]{0:T(1024)} %param.11) | copy-start | bytes 49156
  85.4 7.5 %collective-permute-start.17 = (bf16[256,256]{1,0:T(8,128)(2,1)S(1)}, bf16[256,256]{1,0:T(8,128)(2,1)S(1)}, u32[]{:S(2)}, u32[]{:S(2)}) collective-permute-start(bf16[256,256]{1,0:T(8,128)(2,1)S(1)} %get-tuple-element.53), channel_id=1, source_target_pairs={{0,16},{16,0},{1,17},{17,1},{2,18},{18,2},{3,19},{19,3},{4,20},{20... | collective-permute-start | bytes 393224 | tf_op jit(solution)/shard_map/ppermute | solution.py:228
  90.3 5.4 %collective-permute-start.18 = (bf16[256,256]{1,0:T(8,128)(2,1)S(1)}, bf16[256,256]{1,0:T(8,128)(2,1)S(1)}, u32[]{:S(2)}, u32[]{:S(2)}) collective-permute-start(bf16[256,256]{1,0:T(8,128)(2,1)S(1)} %get-tuple-element.56), channel_id=1, source_target_pairs={{0,16},{16,0},{1,17},{17,1},{2,18},{18,2},{3,19},{19,3},{4,20},{20... | collective-permute-start | bytes 393224 | tf_op jit(solution)/shard_map/ppermute | solution.py:228

commit v4 on v3

--- a/solution.py
+++ b/solution.py
@@ -12,8 +12,8 @@
 EPSILON = 1e-06
 LOG2E = 1.4426950408889634
 LEVEL_LANES = 16
-SIZES = (1, 2, 1, 2, 1, 1)
-VMEM = 24 * 1024 * 1024
+SIZES = (1, 2, 2, 1, 1, 1)
+VMEM = 16 * 1024 * 1024
 NN = (((1,), (0,)), ((), ()))
 NT = (((1,), (1,)), ((), ()))
 TN = (((0,), (0,)), ((), ()))
@@ -51,7 +51,7 @@
 def block_states(k, v, copied):
     rows, width = k.shape
     heads = width // HEAD_DIM
-    step = 4 if heads % 4 == 0 else 1
+    step = heads // 2 if heads % 2 == 0 else heads
     block = pl.BlockSpec((rows, step * HEAD_DIM), lambda g: (0, g))
     copy_shape = (2, rows, copied * HEAD_DIM)
     return pl.pallas_call(
@@ -87,7 +87,6 @@
 
 
 def attend_head(qb, place_ref, q_ref, k_ref, v_ref, kp_ref, vp_ref, lw_ref, table_ref, bucket, out_ref, head, near_n):
-    rows = q_ref.shape[0]
     lane = HEAD_DIM
     scale = HEAD_DIM**-0.5 * LOG2E
     bias = jnp.where(place_ref[2] == 0, -1e30, 0.0).astype(jnp.float32)
@@ -97,57 +96,71 @@
     )
     lane_bits = lane.bit_length() - 1
     first_level = head * LEVEL_LANES
-    for low in range(0, rows, qb):
-        high = low + qb
-        q = q_ref[low:high, :]
-        own = mm(q, k_ref[:high, :], NT)
-        past = mm(q, kp_ref[low:, :], NT)
-        edge = jnp.where(causal, own[:, low:], past[:, :qb] + bias)
-        top = jnp.max(edge, axis=1, keepdims=True)
-        if low:
-            top = jnp.maximum(top, jnp.max(own[:, :low], axis=1, keepdims=True))
-        if high < rows:
-            top = jnp.maximum(top, jnp.max(past[:, qb:], axis=1, keepdims=True) + bias)
+    far_n = bucket.shape[0] // lane
+    bf = jnp.bfloat16
+    q = q_ref[...]
+    own_low = mm(q, k_ref[:qb, :], NT)
+    own_high = mm(q[qb:], k_ref[qb:, :], NT)
+    past_low = mm(q[:qb], kp_ref[:qb, :], NT) + bias
+    past_high = mm(q, kp_ref[qb:, :], NT) + bias
+
+    def softmax(edge_own, edge_past, full):
+        edge = jnp.where(causal, edge_own, edge_past)
+        top = jnp.max(jnp.maximum(edge, full), axis=1, keepdims=True)
         edge = jnp.exp2((edge - top) * scale)
-        total = jnp.sum(edge, axis=1, keepdims=True)
-        own_weights = [jnp.where(causal, edge, 0.0).astype(jnp.bfloat16)]
-        past_weights = [jnp.where(causal, 0.0, edge).astype(jnp.bfloat16)]
-        if low:
-            inner = jnp.exp2((own[:, :low] - top) * scale)
-            total = total + jnp.sum(inner, axis=1, keepdims=True)
-            own_weights.insert(0, inner.astype(jnp.bfloat16))
-        if high < rows:
-            outer = jnp.exp2((past[:, qb:] - (top - bias)) * scale)
-            total = total + jnp.sum(outer, axis=1, keepdims=True)
-            past_weights.append(outer.astype(jnp.bfloat16))
-        windowed = mm(joined(own_weights, 1), v_ref[:high, :])
-        windowed = windowed + mm(joined(past_weights, 1), vp_ref[low:, :])
-        near_rows, far_rows = [], []
-        far_n = bucket.shape[0] // lane
-        for a in range(low // lane, high // lane):
-            inside = slice(a * lane - low, (a + 1) * lane - low)
+        full = jnp.exp2((full - top) * scale)
+        total = jnp.sum(edge + full, axis=1, keepdims=True)
+        own = jnp.where(causal, edge, 0.0).astype(bf)
+        return own, jnp.where(causal, 0.0, edge).astype(bf), full.astype(bf), 1.0 / total
+
+    low_own, low_past, low_full, low_factor = softmax(own_low[:qb], past_low, past_high[:qb])
+    high_own, high_past, high_full, high_factor = softmax(own_high, past_high[qb:], own_low[qb:])
+
+    def near_weights(scores, row, column):
+        out = []
+        for a in range(row // lane, row // lane + qb // lane):
             mix = lw_ref[0, a * lane : (a + 1) * lane, :]
             parts = []
-            for b in range(high // lane):
-                scores = own[inside, b * lane : (b + 1) * lane]
+            for b in range(column // lane, column // lane + qb // lane):
+                part = scores[a * lane - row : (a + 1) * lane - row, b * lane - column : (b + 1) * lane - column]
                 if b < a:
                     level = first_level + lane_bits + (a ^ b).bit_length()
-                    parts.append((scores * mix[:, level : level + 1]).astype(jnp.bfloat16))
+                    parts.append((part * mix[:, level : level + 1]).astype(bf))
                 elif b == a:
-                    picked = jnp.take_along_axis(mix, table, axis=1)
-                    parts.append((scores * picked).astype(jnp.bfloat16))
+                    parts.append((part * jnp.take_along_axis(mix, table, axis=1)).astype(bf))
                 else:
-                    parts.append(jnp.zeros((lane, lane), jnp.bfloat16))
-            near_rows.append(joined(parts, 1))
-            q_part = q[inside, :].astype(jnp.float32)
-            level = first_level + near_n
-            far_parts = [
-                (q_part * mix[:, level + j : level + j + 1]).astype(jnp.bfloat16) for j in range(far_n)
-            ]
-            far_rows.append(joined(far_parts, 1))
-        near = mm(joined(near_rows, 0), v_ref[:high, :])
-        near = near + mm(joined(far_rows, 0), bucket)
-        out_ref[low:high, :] = windowed * (1.0 / total) + near
+                    parts.append(jnp.zeros((lane, lane), bf))
+            out.append(joined(parts, 1))
+        return joined(out, 0)
+
+    first = mm(
+        joined(
+            [low_own, high_full, near_weights(own_low[:qb], 0, 0), near_weights(own_low[qb:], qb, 0)], 0
+        ),
+        v_ref[:qb, :],
+    )
+    second = mm(joined([high_own, near_weights(own_high, qb, qb)], 0), v_ref[qb:, :])
+    third = mm(low_past, vp_ref[:qb, :])
+    fourth = mm(joined([low_full, high_past], 0), vp_ref[qb:, :])
+    proj = mm(q, joined([bucket[j*lane:(j+1)*lane] for j in range(far_n)], 1))
+    far_rows = []
+    for a in range(2 * qb // lane):
+        inside = slice(a * lane, (a + 1) * lane)
+        mix = lw_ref[0, inside, :]
+        level = first_level + near_n
+        total = None
+        for j in range(far_n):
+            t = proj[inside, j*lane:(j+1)*lane] * mix[:, level + j : level + j + 1]
+            total = t if total is None else total + t
+        far_rows.append(total)
+    far = joined(far_rows, 0)
+    out_ref[:qb, :] = (first[:qb] + third + fourth[:qb]) * low_factor + first[2 * qb : 3 * qb] + far[:qb]
+    out_ref[qb:, :] = (
+        (first[qb : 2 * qb] + second[:qb] + fourth[qb:]) * high_factor
+        + first[3 * qb :]
+        + second[qb:]
+        + far[qb:]
+    )
 
 
 def attend(place, q, k, v, past, lw, table, buckets, head, step, near_n, slots):
@@ -156,7 +169,7 @@
     count = rows // slots
     whole = pl.BlockSpec((rows, cols), lambda g, *_: (0, head // step + g))
     group = lambda g, *_: (head // step + g, 0, 0)
-    qb = min(rows, 256)
+    qb = rows // 2
     return pl.pallas_call(
         functools.partial(attend_kernel, qb, step, near_n, slots),
         grid_spec=pltpu.PrefetchScalarGridSpec(
@@ -228,8 +241,9 @@
     return lax.ppermute(value, axis, [(i, (i + steps) % count) for i in range(count)])
 
 
-def from_partner(value, axis, level):
-    return lax.ppermute(value, axis, [(i, i ^ 1 << level) for i in range(lax.axis_size(axis))])
+def from_partner(value, axis, level, up=False):
+    count = lax.axis_size(axis)
+    return lax.ppermute(value, axis, [(i, i ^ 1 << level) for i in range(count) if not up or not i >> level & 1])
 
 
 def added(left, right):
@@ -287,7 +301,9 @@
         cols = slice(start * HEAD_DIM, (start + size) * HEAD_DIM)
         cuts.append(jnp.stack([w[:, cols] for w in whole]))
     for level in range(1, far_n):
-        other = from_partner(running, "seq", level)
+        if level == 2:
+            running = after(running, past[0])
+        other = from_partner(running, "seq", level, level == far_n - 1)
         if level < far_n - 1:
             send_until(1 + level, running)
             running = added(running, other)

time: 99.3 us -> 95.1 us (0.958)
  Pallas kernels: 35.4 us -> 29.7 us
    ppermute x12, waiting for transfers between devices: 4.81 us -> 13.2 us  [shifted(): lax.ppermute(value, axis, [(i, (i + steps) % count) for i in range(count)])]
    ppermute x7, waiting for transfers between devices: 27.7 us -> 20.3 us  [from_partner(): lax.ppermute(value, axis, [(i, i ^ 1 << level) for i in range(count) if n...]
    pallas_call x6, Pallas kernels: 27.3 us -> 22.8 us  [attend(): pl.pallas_call(functools.partial(attend_kernel, qb, step, near_n, slots),...]
    ppermute x7, starting transfers between devices: 6.33 us -> 8.17 us  [from_partner(): lax.ppermute(value, axis, [(i, i ^ 1 << level) for i in range(count) if n...]
    pallas_call x1, Pallas kernels: 4.74 us -> 3.62 us  [block_states(): pl.pallas_call(functools.partial(state_kernel, step), grid=(heads // step...]
    ppermute x12, starting transfers between devices: 17.7 us -> 16.6 us  [shifted(): lax.ppermute(value, axis, [(i, (i + steps) % count) for i in range(count)])]
  transfers between devices with their start and end apart: 19 -> 19, of which waited for: 6 -> 8; matrix products, arithmetic and copies ran while one was open for 7% -> 7% of each run, Pallas kernels for 28% -> 24%
where the time goes in v4:
time: 95.1 us; the launch traced here: 94.9 us
  waiting for transfers between devices  33.4 us (35%)
  Pallas kernels  29.7 us (31%)
  starting transfers between devices  24.8 us (26%)
  other arithmetic  3.55 us (4%)
  local copies, waits for them, and re-layouts  3.18 us (3%)
    pallas_call x6, Pallas kernels, attend(): pl.pallas_call(functools.partial(attend_kernel, qb, step, near_n, slots),...  22.8 us
    ppermute x7, waiting for transfers between devices, from_partner(): lax.ppermute(value, axis, [(i, i ^ 1 << level) for i in range(count) if n...  20.3 us
    ppermute x12, starting transfers between devices, shifted(): lax.ppermute(value, axis, [(i, (i + steps) % count) for i in range(count)])  16.6 us
    ppermute x12, waiting for transfers between devices, shifted(): lax.ppermute(value, axis, [(i, (i + steps) % count) for i in range(count)])  13.2 us
    ppermute x7, starting transfers between devices, from_partner(): lax.ppermute(value, axis, [(i, i ^ 1 << level) for i in range(count) if n...  8.17 us
    pallas_call x1, Pallas kernels, block_states(): pl.pallas_call(functools.partial(state_kernel, step), grid=(heads // step...  3.62 us
    pallas_call x1, Pallas kernels, norm(): pl.pallas_call(functools.partial(norm_kernel, slots, offsets, local_width...  3.29 us
    convert_element_type x3, other arithmetic, added(): (left.astype(jnp.float32) + right.astype(jnp.float32)).astype(jnp.bfloat16)  2.85 us
  transfers between devices with their start and end apart: 19, of which 8 were waited for; matrix products, arithmetic and copies ran while one was open for 7% of the time, Pallas kernels for 24%

profile of v4, /device:TPU:0, one launch (start us, length us, event | category | flops | bytes accessed | tf_op | source)
XLA Modules:
  0.0 94.9 jit_solution(2475077602513688480)
XLA Ops:
  0.0 3.6 %block_states.1 = (bf16[16,128,128]{2,1,0:T(8,128)(2,1)}, bf16[2,512,256]{2,1,0:T(8,128)(2,1)}) custom-call(bf16[512,2048]{1,0:T(8,128)(2,1)} %k_ref.13, bf16[512,2048]{1,0:T(8,128)(2,1)} %v_ref.13), custom_call_target="tpu_custom_call" | custom-call | flops 5280000000 | bytes 17280000 | tf_op jit(solution)/shard_map/block_states/pallas_call | solution.py:57
  3.6 0.5 collective-permute-start
  4.1 2.6 %collective-permute-start.1 = (bf16[16,128,128]{2,1,0:T(8,128)(2,1)}, bf16[16,128,128]{2,1,0:T(8,128)(2,1)S(1)}, u32[]{:S(2)}, u32[]{:S(2)}) collective-permute-start(bf16[16,128,128]{2,1,0:T(8,128)(2,1)} %get-tuple-element.33), channel_id=1, source_target_pairs={{0,1},{1,0},{2,3},{3,2},{4,5},{5,4},{6,7},{7,6},{8,9},{9,8},{10,11... | collective-permute-start | bytes 1572872 | tf_op jit(solution)/shard_map/ppermute | solution.py:246
  6.8 0.1 convert_add_fusion
  6.9 0.1 broadcast_multiply_fusion
  7.0 1.5 %collective-permute-done.1.rest_0_ = bf16[16,128,128]{2,1,0:T(8,128)(2,1)S(1)} collective-permute-done((bf16[16,128,128]{2,1,0:T(8,128)(2,1)}, bf16[16,128,128]{2,1,0:T(8,128)(2,1)S(1)}, u32[]{:S(2)}, u32[]{:S(2)}) %collective-permute-start.1) | collective-permute-done | bytes 524320 | tf_op jit(solution)/shard_map/ppermute | solution.py:246
  8.5 1.8 %add_convert_fusion.2 = bf16[16,64,128]{2,1,0:T(8,128)(2,1)} fusion(bf16[16,128,128]{2,1,0:T(8,128)(2,1)S(1)} %collective-permute-done.1.rest_0_, s32[]{:T(128)S(6)} %select_n.27, bf16[16,128,128]{2,1,0:T(8,128)(2,1)} %get-tuple-element.33), kind=kLoop, calls=%fused_computation.11 | loop fusion | flops 524288 | bytes 786436 | tf_op jit(solution)/shard_map/convert_element_type | solution.py:250
  10.2 1.5 %collective-permute-start.2 = (bf16[16,64,128]{2,1,0:T(8,128)(2,1)}, bf16[16,64,128]{2,1,0:T(8,128)(2,1)S(1)}, u32[]{:S(2)}, u32[]{:S(2)}) collective-permute-start(bf16[16,64,128]{2,1,0:T(8,128)(2,1)} %add_convert_fusion.2), channel_id=1, source_target_pairs={{0,2},{1,3},{2,0},{3,1},{4,6},{5,7},{6,4},{7,5},{8,10},{9,11},{10,... | collective-permute-start | bytes 786440 | tf_op jit(solution)/shard_map/ppermute | solution.py:246
  11.7 0.1 pad_add_fusion.place_ref
  11.8 0.3 copy.8
  12.1 0.8 pad.8
  12.9 1.6 %copy.9 = f32[8,512,32]{2,1,0:T(8,128)S(1)} copy(f32[8,512,32]{1,2,0:T(8,128)} %bitcast.29) | data formatting | bytes 1048576 | tf_op jit(solution)/shard_map/reshape | solution.py:278
  14.6 0.1 pad.9.lw_ref
  14.8 0.1 add_select_fusion.table_ref
  14.8 6.9 %collective-permute-done.2.rest_1_ = bf16[16,64,128]{2,1,0:T(8,128)(2,1)S(1)} collective-permute-done((bf16[16,64,128]{2,1,0:T(8,128)(2,1)}, bf16[16,64,128]{2,1,0:T(8,128)(2,1)S(1)}, u32[]{:S(2)}, u32[]{:S(2)}) %collective-permute-start.2) | collective-permute-done | bytes 262176 | tf_op jit(solution)/shard_map/ppermute | solution.py:246
  21.8 1.0 %add_convert_fusion.1 = bf16[16,64,128]{2,1,0:T(8,128)(2,1)S(1)} fusion(bf16[16,64,128]{2,1,0:T(8,128)(2,1)S(1)} %collective-permute-done.2.rest_1_, bf16[16,64,128]{2,1,0:T(8,128)(2,1)} %add_convert_fusion.2), kind=kLoop, calls=%fused_computation.10 | loop fusion | flops 524288 | bytes 786432 | tf_op jit(solution)/shard_map/convert_element_type | solution.py:250
  22.8 0.3 collective-permute-start.4
  23.1 0.2 slice_bitcast_fusion
  23.3 0.1 pad_maximum_fusion
  23.4 7.7 %collective-permute-done.4.rest_3_ = bf16[16,64,128]{2,1,0:T(8,128)(2,1)S(1)} collective-permute-done((bf16[16,64,128]{2,1,0:T(8,128)(2,1)S(1)}, bf16[16,64,128]{2,1,0:T(8,128)(2,1)S(1)}, u32[]{:S(2)}, u32[]{:S(2)}) %collective-permute-start.4) | collective-permute-done | bytes 262176 | tf_op jit(solution)/shard_map/ppermute | solution.py:246
  31.1 0.1 add_convert_fusion
  31.2 3.2 %collective-permute-start.6 = (bf16[16,64,128]{2,1,0:T(8,128)(2,1)S(1)}, bf16[16,64,128]{2,1,0:T(8,128)(2,1)S(1)}, u32[]{:S(2)}, u32[]{:S(2)}) collective-permute-start(bf16[16,64,128]{2,1,0:T(8,128)(2,1)S(1)} %add_convert_fusion), channel_id=1, source_target_pairs={{0,8},{1,9},{2,10},{3,11},{4,12},{5,13},{6,14},{7,15},{16,24},{17,... | collective-permute-start | bytes 786440 | tf_op jit(solution)/shard_map/ppermute | solution.py:246
  34.4 0.1 slice_bitcast_fusion.4
  34.6 0.1 collective-permute-start.3
  34.7 0.5 collective-permute-start.5
  35.2 4.1 %collective-permute-done.6.rest_5_ = bf16[16,64,128]{2,1,0:T(8,128)(2,1)S(1)} collective-permute-done((bf16[16,64,128]{2,1,0:T(8,128)(2,1)S(1)}, bf16[16,64,128]{2,1,0:T(8,128)(2,1)S(1)}, u32[]{:S(2)}, u32[]{:S(2)}) %collective-permute-start.6) | collective-permute-done | bytes 262176 | tf_op jit(solution)/shard_map/ppermute | solution.py:246
  39.3 0.1 pad_maximum_fusion.1
  39.4 0.6 collective-permute-start.9
  40.1 6.7 %collective-permute-start.10 = (bf16[2,512,256]{2,1,0:T(8,128)(2,1)S(1)}, bf16[2,512,256]{2,1,0:T(8,128)(2,1)S(1)}, u32[]{:S(2)}, u32[]{:S(2)}) collective-permute-start(bf16[2,512,256]{2,1,0:T(8,128)(2,1)S(1)} %pad_maximum_fusion.2), channel_id=1, source_target_pairs={{0,1},{1,2},{2,3},{3,4},{4,5},{5,6},{6,7},{7,8},{8,9},{9,10},{10,1... | collective-permute-start | bytes 1572872 | tf_op jit(solution)/shard_map/ppermute | solution.py:241
  46.8 0.1 collective-permute-start.11
  46.9 1.5 %collective-permute-start.12 = (bf16[2,512,256]{2,1,0:T(8,128)(2,1)S(1)}, bf16[2,512,256]{2,1,0:T(8,128)(2,1)S(1)}, u32[]{:S(2)}, u32[]{:S(2)}) collective-permute-start(bf16[2,512,256]{2,1,0:T(8,128)(2,1)S(1)} %pad_maximum_fusion.4), channel_id=1, source_target_pairs={{0,1},{1,2},{2,3},{3,4},{4,5},{5,6},{6,7},{7,8},{8,9},{9,10},{10,1... | collective-permute-start | bytes 1572872 | tf_op jit(solution)/shard_map/ppermute | solution.py:241
  48.4 2.9 %attend.6 = (bf16[256,256]{1,0:T(8,128)(2,1)S(1)}, bf16[256,256]{1,0:T(8,128)(2,1)S(1)}) custom-call(s32[3]{0:T(128)S(1)} %pad_add_fusion.place_ref, bf16[512,2048]{1,0:T(8,128)(2,1)S(1)} %copy-done.2, bf16[512,2048]{1,0:T(8,128)(2,1)S(1)} %copy-done, bf16[512,2048]{1,0:T(8,128)(2,1)S(1)} %copy-done.1, ...), custom_call_target="tpu_custom_call" | custom-call | flops 3520000000 | bytes 11520000 | tf_op jit(solution)/shard_map/attend/pallas_call | solution.py:173
  51.3 1.6 %collective-permute-start.13 = (bf16[256,256]{1,0:T(8,128)(2,1)S(1)}, bf16[256,256]{1,0:T(8,128)(2,1)S(1)}, u32[]{:S(2)}, u32[]{:S(2)}) collective-permute-start(bf16[256,256]{1,0:T(8,128)(2,1)S(1)} %get-tuple-element.39), channel_id=1, source_target_pairs={{0,16},{16,0},{1,17},{17,1},{2,18},{18,2},{3,19},{19,3},{4,20},{20... | collective-permute-start | bytes 393224 | tf_op jit(solution)/shard_map/ppermute | solution.py:241
  52.8 5.7 %attend.7 = (bf16[256,512]{1,0:T(8,128)(2,1)S(1)}, bf16[256,512]{1,0:T(8,128)(2,1)S(1)}) custom-call(s32[3]{0:T(128)S(1)} %pad_add_fusion.place_ref, bf16[512,2048]{1,0:T(8,128)(2,1)S(1)} %copy-done.2, bf16[512,2048]{1,0:T(8,128)(2,1)S(1)} %copy-done, bf16[512,2048]{1,0:T(8,128)(2,1)S(1)} %copy-done.1, ...), custom_call_target="tpu_custom_call" | custom-call | flops 7040000000 | bytes 23040000 | tf_op jit(solution)/shard_map/attend/pallas_call | solution.py:173
  58.5 6.8 %collective-permute-done.9.past_ref = bf16[2,512,512]{2,1,0:T(8,128)(2,1)S(1)} collective-permute-done((bf16[2,512,512]{2,1,0:T(8,128)(2,1)S(1)}, bf16[2,512,512]{2,1,0:T(8,128)(2,1)S(1)}, u32[]{:S(2)}, u32[]{:S(2)}) %collective-permute-start.9) | collective-permute-done | bytes 1048608 | tf_op jit(solution)/shard_map/ppermute | solution.py:241
  65.3 1.5 %collective-permute-start.14 = (bf16[256,512]{1,0:T(8,128)(2,1)S(1)}, bf16[256,512]{1,0:T(8,128)(2,1)S(1)}, u32[]{:S(2)}, u32[]{:S(2)}) collective-permute-start(bf16[256,512]{1,0:T(8,128)(2,1)S(1)} %get-tuple-element.43), channel_id=1, source_target_pairs={{0,16},{16,0},{1,17},{17,1},{2,18},{18,2},{3,19},{19,3},{4,20},{20... | collective-permute-start | bytes 786440 | tf_op jit(solution)/shard_map/ppermute | solution.py:241
  66.8 5.5 %attend.8 = (bf16[256,512]{1,0:T(8,128)(2,1)S(1)}, bf16[256,512]{1,0:T(8,128)(2,1)S(1)}) custom-call(s32[3]{0:T(128)S(1)} %pad_add_fusion.place_ref, bf16[512,2048]{1,0:T(8,128)(2,1)S(1)} %copy-done.2, bf16[512,2048]{1,0:T(8,128)(2,1)S(1)} %copy-done, bf16[512,2048]{1,0:T(8,128)(2,1)S(1)} %copy-done.1, ...), custom_call_target="tpu_custom_call" | custom-call | flops 7040000000 | bytes 23040000 | tf_op jit(solution)/shard_map/attend/pallas_call | solution.py:173
  72.4 0.6 collective-permute-start.15
  73.0 2.9 %attend.9 = (bf16[256,256]{1,0:T(8,128)(2,1)S(1)}, bf16[256,256]{1,0:T(8,128)(2,1)S(1)}) custom-call(s32[3]{0:T(128)S(1)} %pad_add_fusion.place_ref, bf16[512,2048]{1,0:T(8,128)(2,1)S(1)} %copy-done.2, bf16[512,2048]{1,0:T(8,128)(2,1)S(1)} %copy-done, bf16[512,2048]{1,0:T(8,128)(2,1)S(1)} %copy-done.1, ...), custom_call_target="tpu_custom_call" | custom-call | flops 3520000000 | bytes 11520000 | tf_op jit(solution)/shard_map/attend/pallas_call | solution.py:173
  75.9 0.7 collective-permute-done.11.past_ref
  76.6 1.5 %collective-permute-start.16 = (bf16[256,256]{1,0:T(8,128)(2,1)S(1)}, bf16[256,256]{1,0:T(8,128)(2,1)S(1)}, u32[]{:S(2)}, u32[]{:S(2)}) collective-permute-start(bf16[256,256]{1,0:T(8,128)(2,1)S(1)} %get-tuple-element.51), channel_id=1, source_target_pairs={{0,16},{16,0},{1,17},{17,1},{2,18},{18,2},{3,19},{19,3},{4,20},{20... | collective-permute-start | bytes 393224 | tf_op jit(solution)/shard_map/ppermute | solution.py:241
  78.1 2.9 %attend.10 = (bf16[256,256]{1,0:T(8,128)(2,1)S(1)}, bf16[256,256]{1,0:T(8,128)(2,1)S(1)}) custom-call(s32[3]{0:T(128)S(1)} %pad_add_fusion.place_ref, bf16[512,2048]{1,0:T(8,128)(2,1)S(1)} %copy-done.2, bf16[512,2048]{1,0:T(8,128)(2,1)S(1)} %copy-done, bf16[512,2048]{1,0:T(8,128)(2,1)S(1)} %copy-done.1, ...), custom_call_target="tpu_custom_call" | custom-call | flops 3520000000 | bytes 11520000 | tf_op jit(solution)/shard_map/attend/pallas_call | solution.py:173
  81.0 1.2 %collective-permute-done.12.past_ref = bf16[2,512,256]{2,1,0:T(8,128)(2,1)S(1)} collective-permute-done((bf16[2,512,256]{2,1,0:T(8,128)(2,1)S(1)}, bf16[2,512,256]{2,1,0:T(8,128)(2,1)S(1)}, u32[]{:S(2)}, u32[]{:S(2)}) %collective-permute-start.12) | collective-permute-done | bytes 524320 | tf_op jit(solution)/shard_map/ppermute | solution.py:241
  82.2 1.5 %collective-permute-start.17 = (bf16[256,256]{1,0:T(8,128)(2,1)S(1)}, bf16[256,256]{1,0:T(8,128)(2,1)S(1)}, u32[]{:S(2)}, u32[]{:S(2)}) collective-permute-start(bf16[256,256]{1,0:T(8,128)(2,1)S(1)} %get-tuple-element.55), channel_id=1, source_target_pairs={{0,16},{16,0},{1,17},{17,1},{2,18},{18,2},{3,19},{19,3},{4,20},{20... | collective-permute-start | bytes 393224 | tf_op jit(solution)/shard_map/ppermute | solution.py:241
  83.7 2.9 %attend.11 = (bf16[256,256]{1,0:T(8,128)(2,1)S(1)}, bf16[256,256]{1,0:T(8,128)(2,1)S(1)}) custom-call(s32[3]{0:T(128)S(1)} %pad_add_fusion.place_ref, bf16[512,2048]{1,0:T(8,128)(2,1)S(1)} %copy-done.2, bf16[512,2048]{1,0:T(8,128)(2,1)S(1)} %copy-done, bf16[512,2048]{1,0:T(8,128)(2,1)S(1)} %copy-done.1, ...), custom_call_target="tpu_custom_call" | custom-call | flops 3520000000 | bytes 11520000 | tf_op jit(solution)/shard_map/attend/pallas_call | solution.py:173
  86.6 0.6 collective-permute-start.18
  87.2 4.4 %collective-permute-done.18.rest_11_ = bf16[256,256]{1,0:T(8,128)(2,1)S(1)} collective-permute-done((bf16[256,256]{1,0:T(8,128)(2,1)S(1)}, bf16[256,256]{1,0:T(8,128)(2,1)S(1)}, u32[]{:S(2)}, u32[]{:S(2)}) %collective-permute-start.18) | collective-permute-done | bytes 131104 | tf_op jit(solution)/shard_map/ppermute | solution.py:241
  91.6 3.3 %norm.1 = bf16[256,4096]{1,0:T(8,128)(2,1)} custom-call(s32[1]{0:T(128)} %bitcast.place_ref, bf16[256,4096]{1,0:T(8,128)(2,1)S(1)} %copy-done.3, f32[1,4096]{1,0:T(1,128)S(1)} %bitcast.28, bf16[256,256]{1,0:T(8,128)(2,1)S(1)} %get-tuple-element.35.rest_0_, bf16[256,512]{1,0:T(8,128)(2,1)S(1)} %get-tuple-element.41.rest_1_, ...), custom_call_target="tpu_custom_call" | custom-call | flops 3520000000 | bytes 11520000 | tf_op jit(solution)/shard_map/norm/pallas_call | solution.py:219
  (31 shorter events, 0.3 us)
Async XLA Ops:
  0.0 6.8 %copy-start.5 = (f32[14,16,512]{2,1,0:T(8,128)S(1)}, f32[14,16,512]{2,1,0:T(8,128)}, u32[]{:S(2)}) copy-start(f32[14,16,512]{2,1,0:T(8,128)} %param.9) | copy-start | bytes 1376260
  3.6 19.2 %collective-permute-start = (bf16[2,512,256]{2,1,0:T(8,128)(2,1)}, bf16[2,512,256]{2,1,0:T(8,128)(2,1)S(1)}, u32[]{:S(2)}, u32[]{:S(2)}) collective-permute-start(bf16[2,512,256]{2,1,0:T(8,128)(2,1)} %get-tuple-element.32), channel_id=1, source_target_pairs={{0,1},{1,2},{2,3},{3,4},{4,5},{5,6},{6,7},{7,8},{8,9},{9,10},{10,1... | collective-permute-start | bytes 1572872 | tf_op jit(solution)/shard_map/ppermute | solution.py:241
  4.1 4.4 %collective-permute-start.1 = (bf16[16,128,128]{2,1,0:T(8,128)(2,1)}, bf16[16,128,128]{2,1,0:T(8,128)(2,1)S(1)}, u32[]{:S(2)}, u32[]{:S(2)}) collective-permute-start(bf16[16,128,128]{2,1,0:T(8,128)(2,1)} %get-tuple-element.33), channel_id=1, source_target_pairs={{0,1},{1,0},{2,3},{3,2},{4,5},{5,4},{6,7},{7,6},{8,9},{9,8},{10,11... | collective-permute-start | bytes 1572872 | tf_op jit(solution)/shard_map/ppermute | solution.py:246
  10.2 11.5 %collective-permute-start.2 = (bf16[16,64,128]{2,1,0:T(8,128)(2,1)}, bf16[16,64,128]{2,1,0:T(8,128)(2,1)S(1)}, u32[]{:S(2)}, u32[]{:S(2)}) collective-permute-start(bf16[16,64,128]{2,1,0:T(8,128)(2,1)} %add_convert_fusion.2), channel_id=1, source_target_pairs={{0,2},{1,3},{2,0},{3,1},{4,6},{5,7},{6,4},{7,5},{8,10},{9,11},{10,... | collective-permute-start | bytes 786440 | tf_op jit(solution)/shard_map/ppermute | solution.py:246
  14.6 8.5 %copy-start = (bf16[512,2048]{1,0:T(8,128)(2,1)S(1)}, bf16[512,2048]{1,0:T(8,128)(2,1)}, u32[]{:S(2)}) copy-start(bf16[512,2048]{1,0:T(8,128)(2,1)} %k_ref.13) | copy-start | bytes 6291460
  14.6 8.5 %copy-start.1 = (bf16[512,2048]{1,0:T(8,128)(2,1)S(1)}, bf16[512,2048]{1,0:T(8,128)(2,1)}, u32[]{:S(2)}) copy-start(bf16[512,2048]{1,0:T(8,128)(2,1)} %v_ref.13) | copy-start | bytes 6291460
  22.8 8.3 %collective-permute-start.4 = (bf16[16,64,128]{2,1,0:T(8,128)(2,1)S(1)}, bf16[16,64,128]{2,1,0:T(8,128)(2,1)S(1)}, u32[]{:S(2)}, u32[]{:S(2)}) collective-permute-start(bf16[16,64,128]{2,1,0:T(8,128)(2,1)S(1)} %add_convert_fusion.1), channel_id=1, source_target_pairs={{0,4},{1,5},{2,6},{3,7},{4,0},{5,1},{6,2},{7,3},{8,12},{9,13},{10,... | collective-permute-start | bytes 786440 | tf_op jit(solution)/shard_map/ppermute | solution.py:246
  23.4 27.9 %collective-permute-start.8 = (bf16[2,512,512]{2,1,0:T(8,128)(2,1)S(1)}, bf16[2,512,512]{2,1,0:T(8,128)(2,1)S(1)}, u32[]{:S(2)}, u32[]{:S(2)}) collective-permute-start(bf16[2,512,512]{2,1,0:T(8,128)(2,1)S(1)} %pad_maximum_fusion), channel_id=1, source_target_pairs={{0,1},{1,2},{2,3},{3,4},{4,5},{5,6},{6,7},{7,8},{8,9},{9,10},{10,1... | collective-permute-start | bytes 3145736 | tf_op jit(solution)/shard_map/ppermute | solution.py:241
  31.2 8.1 %collective-permute-start.6 = (bf16[16,64,128]{2,1,0:T(8,128)(2,1)S(1)}, bf16[16,64,128]{2,1,0:T(8,128)(2,1)S(1)}, u32[]{:S(2)}, u32[]{:S(2)}) collective-permute-start(bf16[16,64,128]{2,1,0:T(8,128)(2,1)S(1)} %add_convert_fusion), channel_id=1, source_target_pairs={{0,8},{1,9},{2,10},{3,11},{4,12},{5,13},{6,14},{7,15},{16,24},{17,... | collective-permute-start | bytes 786440 | tf_op jit(solution)/shard_map/ppermute | solution.py:246
  34.5 13.8 %copy-start.2 = (bf16[512,2048]{1,0:T(8,128)(2,1)S(1)}, bf16[512,2048]{1,0:T(8,128)(2,1)}, u32[]{:S(2)}) copy-start(bf16[512,2048]{1,0:T(8,128)(2,1)} %q_ref.11) | copy-start | bytes 6291460
  34.6 5.4 %collective-permute-start.3 = (bf16[16,64,128]{2,1,0:T(8,128)(2,1)S(1)}, bf16[16,64,128]{2,1,0:T(8,128)(2,1)S(1)}, u32[]{:S(2)}, u32[]{:S(2)}) collective-permute-start(bf16[16,64,128]{2,1,0:T(8,128)(2,1)S(1)} %collective-permute-done.2.rest_1_), channel_id=1, source_target_pairs={{0,1},{1,0},{2,3},{3,2},{4,5},{5,4},{6,7},{7,6},{8,9},{9,8},{10,11... | collective-permute-start | bytes 786440 | tf_op jit(solution)/shard_map/ppermute | solution.py:246
  34.7 12.1 %collective-permute-start.5 = (bf16[16,64,128]{2,1,0:T(8,128)(2,1)S(1)}, bf16[16,64,128]{2,1,0:T(8,128)(2,1)S(1)}, u32[]{:S(2)}, u32[]{:S(2)}) collective-permute-start(bf16[16,64,128]{2,1,0:T(8,128)(2,1)S(1)} %collective-permute-done.4.rest_3_), channel_id=1, source_target_pairs={{0,1},{1,0},{2,3},{3,2},{4,5},{5,4},{6,7},{7,6},{8,9},{9,8},{10,11... | collective-permute-start | bytes 786440 | tf_op jit(solution)/shard_map/ppermute | solution.py:246
  39.3 7.5 %collective-permute-start.7 = (bf16[16,64,128]{2,1,0:T(8,128)(2,1)S(1)}, bf16[16,64,128]{2,1,0:T(8,128)(2,1)S(1)}, u32[]{:S(2)}, u32[]{:S(2)}) collective-permute-start(bf16[16,64,128]{2,1,0:T(8,128)(2,1)S(1)} %collective-permute-done.6.rest_5_), channel_id=1, source_target_pairs={{0,1},{1,0},{2,3},{3,2},{4,5},{5,4},{6,7},{7,6},{8,9},{9,8},{10,11... | collective-permute-start | bytes 786440 | tf_op jit(solution)/shard_map/ppermute | solution.py:246
  39.4 25.9 %collective-permute-start.9 = (bf16[2,512,512]{2,1,0:T(8,128)(2,1)S(1)}, bf16[2,512,512]{2,1,0:T(8,128)(2,1)S(1)}, u32[]{:S(2)}, u32[]{:S(2)}) collective-permute-start(bf16[2,512,512]{2,1,0:T(8,128)(2,1)S(1)} %pad_maximum_fusion.1), channel_id=1, source_target_pairs={{0,1},{1,2},{2,3},{3,4},{4,5},{5,6},{6,7},{7,8},{8,9},{9,10},{10,1... | collective-permute-start | bytes 3145736 | tf_op jit(solution)/shard_map/ppermute | solution.py:241
  40.1 32.3 %collective-permute-start.10 = (bf16[2,512,256]{2,1,0:T(8,128)(2,1)S(1)}, bf16[2,512,256]{2,1,0:T(8,128)(2,1)S(1)}, u32[]{:S(2)}, u32[]{:S(2)}) collective-permute-start(bf16[2,512,256]{2,1,0:T(8,128)(2,1)S(1)} %pad_maximum_fusion.2), channel_id=1, source_target_pairs={{0,1},{1,2},{2,3},{3,4},{4,5},{5,6},{6,7},{7,8},{8,9},{9,10},{10,1... | collective-permute-start | bytes 1572872 | tf_op jit(solution)/shard_map/ppermute | solution.py:241
  46.8 29.8 %collective-permute-start.11 = (bf16[2,512,256]{2,1,0:T(8,128)(2,1)S(1)}, bf16[2,512,256]{2,1,0:T(8,128)(2,1)S(1)}, u32[]{:S(2)}, u32[]{:S(2)}) collective-permute-start(bf16[2,512,256]{2,1,0:T(8,128)(2,1)S(1)} %pad_maximum_fusion.3), channel_id=1, source_target_pairs={{0,1},{1,2},{2,3},{3,4},{4,5},{5,6},{6,7},{7,8},{8,9},{9,10},{10,1... | collective-permute-start | bytes 1572872 | tf_op jit(solution)/shard_map/ppermute | solution.py:241
  46.9 35.3 %collective-permute-start.12 = (bf16[2,512,256]{2,1,0:T(8,128)(2,1)S(1)}, bf16[2,512,256]{2,1,0:T(8,128)(2,1)S(1)}, u32[]{:S(2)}, u32[]{:S(2)}) collective-permute-start(bf16[2,512,256]{2,1,0:T(8,128)(2,1)S(1)} %pad_maximum_fusion.4), channel_id=1, source_target_pairs={{0,1},{1,2},{2,3},{3,4},{4,5},{5,6},{6,7},{7,8},{8,9},{9,10},{10,1... | collective-permute-start | bytes 1572872 | tf_op jit(solution)/shard_map/ppermute | solution.py:241
  51.3 35.3 %collective-permute-start.13 = (bf16[256,256]{1,0:T(8,128)(2,1)S(1)}, bf16[256,256]{1,0:T(8,128)(2,1)S(1)}, u32[]{:S(2)}, u32[]{:S(2)}) collective-permute-start(bf16[256,256]{1,0:T(8,128)(2,1)S(1)} %get-tuple-element.39), channel_id=1, source_target_pairs={{0,16},{16,0},{1,17},{17,1},{2,18},{18,2},{3,19},{19,3},{4,20},{20... | collective-permute-start | bytes 393224 | tf_op jit(solution)/shard_map/ppermute | solution.py:241
  65.3 21.8 %collective-permute-start.14 = (bf16[256,512]{1,0:T(8,128)(2,1)S(1)}, bf16[256,512]{1,0:T(8,128)(2,1)S(1)}, u32[]{:S(2)}, u32[]{:S(2)}) collective-permute-start(bf16[256,512]{1,0:T(8,128)(2,1)S(1)} %get-tuple-element.43), channel_id=1, source_target_pairs={{0,16},{16,0},{1,17},{17,1},{2,18},{18,2},{3,19},{19,3},{4,20},{20... | collective-permute-start | bytes 786440 | tf_op jit(solution)/shard_map/ppermute | solution.py:241
  72.4 19.2 %collective-permute-start.15 = (bf16[256,512]{1,0:T(8,128)(2,1)S(1)}, bf16[256,512]{1,0:T(8,128)(2,1)S(1)}, u32[]{:S(2)}, u32[]{:S(2)}) collective-permute-start(bf16[256,512]{1,0:T(8,128)(2,1)S(1)} %get-tuple-element.47), channel_id=1, source_target_pairs={{0,16},{16,0},{1,17},{17,1},{2,18},{18,2},{3,19},{19,3},{4,20},{20... | collective-permute-start | bytes 786440 | tf_op jit(solution)/shard_map/ppermute | solution.py:241
  76.6 10.6 %collective-permute-start.16 = (bf16[256,256]{1,0:T(8,128)(2,1)S(1)}, bf16[256,256]{1,0:T(8,128)(2,1)S(1)}, u32[]{:S(2)}, u32[]{:S(2)}) collective-permute-start(bf16[256,256]{1,0:T(8,128)(2,1)S(1)} %get-tuple-element.51), channel_id=1, source_target_pairs={{0,16},{16,0},{1,17},{17,1},{2,18},{18,2},{3,19},{19,3},{4,20},{20... | collective-permute-start | bytes 393224 | tf_op jit(solution)/shard_map/ppermute | solution.py:241
  82.2 9.4 %copy-start.3 = (bf16[256,4096]{1,0:T(8,128)(2,1)S(1)}, bf16[256,4096]{1,0:T(8,128)(2,1)}, u32[]{:S(2)}) copy-start(bf16[256,4096]{1,0:T(8,128)(2,1)} %gate_ref.1) | copy-start | bytes 6291460
  82.2 9.4 %copy-start.4 = (f32[4096]{0:T(1024)S(1)}, f32[4096]{0:T(1024)}, u32[]{:S(2)}) copy-start(f32[4096]{0:T(1024)} %param.11) | copy-start | bytes 49156
  82.2 5.0 %collective-permute-start.17 = (bf16[256,256]{1,0:T(8,128)(2,1)S(1)}, bf16[256,256]{1,0:T(8,128)(2,1)S(1)}, u32[]{:S(2)}, u32[]{:S(2)}) collective-permute-start(bf16[256,256]{1,0:T(8,128)(2,1)S(1)} %get-tuple-element.55), channel_id=1, source_target_pairs={{0,16},{16,0},{1,17},{17,1},{2,18},{18,2},{3,19},{19,3},{4,20},{20... | collective-permute-start | bytes 393224 | tf_op jit(solution)/shard_map/ppermute | solution.py:241
  86.6 5.0 %collective-permute-start.18 = (bf16[256,256]{1,0:T(8,128)(2,1)S(1)}, bf16[256,256]{1,0:T(8,128)(2,1)S(1)}, u32[]{:S(2)}, u32[]{:S(2)}) collective-permute-start(bf16[256,256]{1,0:T(8,128)(2,1)S(1)} %get-tuple-element.58), channel_id=1, source_target_pairs={{0,16},{16,0},{1,17},{17,1},{2,18},{18,2},{3,19},{19,3},{4,20},{20... | collective-permute-start | bytes 393224 | tf_op jit(solution)/shard_map/ppermute | solution.py:241

commit v5 on v4

--- a/solution.py
+++ b/solution.py
@@ -287,7 +287,9 @@
 
     def send_until(count, *earlier):
         for index in range(len(past), min(count, len(sizes))):
-            past.append(shifted(after(cuts[index], *earlier), "seq", 1))
+            count = lax.axis_size("seq")
+            pairs = [(i, (i + 1) % count) for i in range(count if index not in (len(sizes) - 2, len(sizes) - 1) else count - 1)]
+            past.append(lax.ppermute(after(cuts[index], *earlier), "seq", pairs))
 
     half = HEAD_DIM // 2
     states, cut = block_states(key_vectors, values, sizes[0])
@@ -305,7 +307,7 @@
             running = after(running, past[0])
         other = from_partner(running, "seq", level, level == far_n - 1)
         if level < far_n - 1:
-            send_until(1 + level, running)
+            send_until(2, running)
             running = added(running, other)
         buckets += [other, from_partner(other, "seq", 0)]
     send_until(len(sizes), other)

time: 95.1 us -> 92.5 us (0.973)
  waiting for transfers between devices: 33.4 us -> 26.7 us
  starting transfers between devices: 24.8 us -> 28.8 us
    ppermute x0 -> x6, starting transfers between devices: none -> 13.2 us  [send_until(): past.append(lax.ppermute(after(cuts[index], *earlier), 'seq', pairs))]
    ppermute x12 -> x6, waiting for transfers between devices: 13.2 us -> 3.48 us  [shifted(): lax.ppermute(value, axis, [(i, (i + steps) % count) for i in range(count)])]
    ppermute x12 -> x6, starting transfers between devices: 16.6 us -> 7.38 us  [shifted(): lax.ppermute(value, axis, [(i, (i + steps) % count) for i in range(count)])]
    ppermute x0 -> x6, waiting for transfers between devices: none -> 2.92 us  [send_until(): past.append(lax.ppermute(after(cuts[index], *earlier), 'seq', pairs))]
  transfers between devices with their start and end apart: 19 -> 19, of which waited for: 8 -> 7; matrix products, arithmetic and copies ran while one was open for 7% -> 7% of each run, Pallas kernels for 24% -> 25%
where the time goes in v5:
time: 92.5 us; the launch traced here: 92.2 us
  Pallas kernels  29.7 us (32%)
  starting transfers between devices  28.8 us (31%)
  waiting for transfers between devices  26.7 us (29%)
  other arithmetic  3.55 us (4%)
  local copies, waits for them, and re-layouts  3.19 us (3%)
    pallas_call x6, Pallas kernels, attend(): pl.pallas_call(functools.partial(attend_kernel, qb, step, near_n, slots),...  22.8 us
    ppermute x7, waiting for transfers between devices, from_partner(): lax.ppermute(value, axis, [(i, i ^ 1 << level) for i in range(count) if n...  20.3 us
    ppermute x6, starting transfers between devices, send_until(): past.append(lax.ppermute(after(cuts[index], *earlier), 'seq', pairs))  13.2 us
    ppermute x7, starting transfers between devices, from_partner(): lax.ppermute(value, axis, [(i, i ^ 1 << level) for i in range(count) if n...  8.17 us
    ppermute x6, starting transfers between devices, shifted(): lax.ppermute(value, axis, [(i, (i + steps) % count) for i in range(count)])  7.38 us
    pallas_call x1, Pallas kernels, block_states(): pl.pallas_call(functools.partial(state_kernel, step), grid=(heads // step...  3.62 us
    ppermute x6, waiting for transfers between devices, shifted(): lax.ppermute(value, axis, [(i, (i + steps) % count) for i in range(count)])  3.48 us
    pallas_call x1, Pallas kernels, norm(): pl.pallas_call(functools.partial(norm_kernel, slots, offsets, local_width...  3.29 us
  transfers between devices with their start and end apart: 19, of which 7 were waited for; matrix products, arithmetic and copies ran while one was open for 7% of the time, Pallas kernels for 25%

profile of v5, /device:TPU:0, one launch (start us, length us, event | category | flops | bytes accessed | tf_op | source)
XLA Modules:
  0.0 92.2 jit_solution(17857421707107183990)
XLA Ops:
  0.0 3.6 %block_states.1 = (bf16[16,128,128]{2,1,0:T(8,128)(2,1)}, bf16[2,512,256]{2,1,0:T(8,128)(2,1)}) custom-call(bf16[512,2048]{1,0:T(8,128)(2,1)} %k_ref.13, bf16[512,2048]{1,0:T(8,128)(2,1)} %v_ref.13), custom_call_target="tpu_custom_call" | custom-call | flops 5280000000 | bytes 17280000 | tf_op jit(solution)/shard_map/block_states/pallas_call | solution.py:57
  3.6 0.5 collective-permute-start
  4.1 2.6 %collective-permute-start.1 = (bf16[16,128,128]{2,1,0:T(8,128)(2,1)}, bf16[16,128,128]{2,1,0:T(8,128)(2,1)S(1)}, u32[]{:S(2)}, u32[]{:S(2)}) collective-permute-start(bf16[16,128,128]{2,1,0:T(8,128)(2,1)} %get-tuple-element.33), channel_id=1, source_target_pairs={{0,1},{1,0},{2,3},{3,2},{4,5},{5,4},{6,7},{7,6},{8,9},{9,8},{10,11... | collective-permute-start | bytes 1572872 | tf_op jit(solution)/shard_map/ppermute | solution.py:246
  6.8 0.1 convert_add_fusion
  6.9 0.1 broadcast_multiply_fusion
  7.0 1.5 %collective-permute-done.1.rest_0_ = bf16[16,128,128]{2,1,0:T(8,128)(2,1)S(1)} collective-permute-done((bf16[16,128,128]{2,1,0:T(8,128)(2,1)}, bf16[16,128,128]{2,1,0:T(8,128)(2,1)S(1)}, u32[]{:S(2)}, u32[]{:S(2)}) %collective-permute-start.1) | collective-permute-done | bytes 524320 | tf_op jit(solution)/shard_map/ppermute | solution.py:246
  8.5 1.8 %add_convert_fusion.2 = bf16[16,64,128]{2,1,0:T(8,128)(2,1)} fusion(bf16[16,128,128]{2,1,0:T(8,128)(2,1)S(1)} %collective-permute-done.1.rest_0_, s32[]{:T(128)S(6)} %select_n.27, bf16[16,128,128]{2,1,0:T(8,128)(2,1)} %get-tuple-element.33), kind=kLoop, calls=%fused_computation.11 | loop fusion | flops 524288 | bytes 786436 | tf_op jit(solution)/shard_map/convert_element_type | solution.py:250
  10.2 1.5 %collective-permute-start.2 = (bf16[16,64,128]{2,1,0:T(8,128)(2,1)}, bf16[16,64,128]{2,1,0:T(8,128)(2,1)S(1)}, u32[]{:S(2)}, u32[]{:S(2)}) collective-permute-start(bf16[16,64,128]{2,1,0:T(8,128)(2,1)} %add_convert_fusion.2), channel_id=1, source_target_pairs={{0,2},{1,3},{2,0},{3,1},{4,6},{5,7},{6,4},{7,5},{8,10},{9,11},{10,... | collective-permute-start | bytes 786440 | tf_op jit(solution)/shard_map/ppermute | solution.py:246
  11.7 0.1 pad_add_fusion.place_ref
  11.8 0.3 copy.8
  12.1 0.8 pad.8
  12.9 1.6 %copy.9 = f32[8,512,32]{2,1,0:T(8,128)S(1)} copy(f32[8,512,32]{1,2,0:T(8,128)} %bitcast.29) | data formatting | bytes 1048576 | tf_op jit(solution)/shard_map/reshape | solution.py:278
  14.6 0.1 pad.9.lw_ref
  14.8 0.1 add_select_fusion.table_ref
  14.8 6.9 %collective-permute-done.2.rest_1_ = bf16[16,64,128]{2,1,0:T(8,128)(2,1)S(1)} collective-permute-done((bf16[16,64,128]{2,1,0:T(8,128)(2,1)}, bf16[16,64,128]{2,1,0:T(8,128)(2,1)S(1)}, u32[]{:S(2)}, u32[]{:S(2)}) %collective-permute-start.2) | collective-permute-done | bytes 262176 | tf_op jit(solution)/shard_map/ppermute | solution.py:246
  21.8 1.0 %add_convert_fusion.1 = bf16[16,64,128]{2,1,0:T(8,128)(2,1)S(1)} fusion(bf16[16,64,128]{2,1,0:T(8,128)(2,1)S(1)} %collective-permute-done.2.rest_1_, bf16[16,64,128]{2,1,0:T(8,128)(2,1)} %add_convert_fusion.2), kind=kLoop, calls=%fused_computation.10 | loop fusion | flops 524288 | bytes 786432 | tf_op jit(solution)/shard_map/convert_element_type | solution.py:250
  22.8 0.3 collective-permute-start.4
  23.1 0.2 slice_bitcast_fusion
  23.3 0.1 pad_maximum_fusion
  23.4 0.1 collective-permute-start.8
  23.4 7.7 %collective-permute-done.4.rest_3_ = bf16[16,64,128]{2,1,0:T(8,128)(2,1)S(1)} collective-permute-done((bf16[16,64,128]{2,1,0:T(8,128)(2,1)S(1)}, bf16[16,64,128]{2,1,0:T(8,128)(2,1)S(1)}, u32[]{:S(2)}, u32[]{:S(2)}) %collective-permute-start.4) | collective-permute-done | bytes 262176 | tf_op jit(solution)/shard_map/ppermute | solution.py:246
  31.1 0.1 add_convert_fusion
  31.2 3.2 %collective-permute-start.6 = (bf16[16,64,128]{2,1,0:T(8,128)(2,1)S(1)}, bf16[16,64,128]{2,1,0:T(8,128)(2,1)S(1)}, u32[]{:S(2)}, u32[]{:S(2)}) collective-permute-start(bf16[16,64,128]{2,1,0:T(8,128)(2,1)S(1)} %add_convert_fusion), channel_id=1, source_target_pairs={{0,8},{1,9},{2,10},{3,11},{4,12},{5,13},{6,14},{7,15},{16,24},{17,... | collective-permute-start | bytes 786440 | tf_op jit(solution)/shard_map/ppermute | solution.py:246
  34.4 0.1 slice_bitcast_fusion.4
  34.6 0.1 collective-permute-start.3
  34.7 0.5 collective-permute-start.5
  35.2 4.1 %collective-permute-done.6.rest_5_ = bf16[16,64,128]{2,1,0:T(8,128)(2,1)S(1)} collective-permute-done((bf16[16,64,128]{2,1,0:T(8,128)(2,1)S(1)}, bf16[16,64,128]{2,1,0:T(8,128)(2,1)S(1)}, u32[]{:S(2)}, u32[]{:S(2)}) %collective-permute-start.6) | collective-permute-done | bytes 262176 | tf_op jit(solution)/shard_map/ppermute | solution.py:246
  39.3 0.1 pad_maximum_fusion.1
  39.4 0.6 collective-permute-start.9
  40.1 6.7 %collective-permute-start.10 = (bf16[2,512,256]{2,1,0:T(8,128)(2,1)S(1)}, bf16[2,512,256]{2,1,0:T(8,128)(2,1)S(1)}, u32[]{:S(2)}, u32[]{:S(2)}) collective-permute-start(bf16[2,512,256]{2,1,0:T(8,128)(2,1)S(1)} %pad_maximum_fusion.2), channel_id=1, source_target_pairs={{0,1},{1,2},{2,3},{3,4},{4,5},{5,6},{6,7},{7,8},{8,9},{9,10},{10,1... | collective-permute-start | bytes 1572872 | tf_op jit(solution)/shard_map/ppermute | solution.py:292
  46.8 2.0 %collective-permute-start.11 = (bf16[2,512,256]{2,1,0:T(8,128)(2,1)S(1)}, bf16[2,512,256]{2,1,0:T(8,128)(2,1)S(1)}, u32[]{:S(2)}, u32[]{:S(2)}) collective-permute-start(bf16[2,512,256]{2,1,0:T(8,128)(2,1)S(1)} %pad_maximum_fusion.3), channel_id=1, source_target_pairs={{0,1},{1,2},{2,3},{3,4},{4,5},{5,6},{6,7},{7,8},{8,9},{9,10},{10,1... | collective-permute-start | bytes 1572872 | tf_op jit(solution)/shard_map/ppermute | solution.py:292
  48.8 3.4 %collective-permute-start.12 = (bf16[2,512,256]{2,1,0:T(8,128)(2,1)S(1)}, bf16[2,512,256]{2,1,0:T(8,128)(2,1)S(1)}, u32[]{:S(2)}, u32[]{:S(2)}) collective-permute-start(bf16[2,512,256]{2,1,0:T(8,128)(2,1)S(1)} %pad_maximum_fusion.4), channel_id=1, source_target_pairs={{0,1},{1,2},{2,3},{3,4},{4,5},{5,6},{6,7},{7,8},{8,9},{9,10},{10,1... | collective-permute-start | bytes 1572872 | tf_op jit(solution)/shard_map/ppermute | solution.py:292
  52.2 2.9 %attend.6 = (bf16[256,256]{1,0:T(8,128)(2,1)S(1)}, bf16[256,256]{1,0:T(8,128)(2,1)S(1)}) custom-call(s32[3]{0:T(128)S(1)} %pad_add_fusion.place_ref, bf16[512,2048]{1,0:T(8,128)(2,1)S(1)} %copy-done.2, bf16[512,2048]{1,0:T(8,128)(2,1)S(1)} %copy-done, bf16[512,2048]{1,0:T(8,128)(2,1)S(1)} %copy-done.1, ...), custom_call_target="tpu_custom_call" | custom-call | flops 3520000000 | bytes 11520000 | tf_op jit(solution)/shard_map/attend/pallas_call | solution.py:173
  55.1 1.6 %collective-permute-start.13 = (bf16[256,256]{1,0:T(8,128)(2,1)S(1)}, bf16[256,256]{1,0:T(8,128)(2,1)S(1)}, u32[]{:S(2)}, u32[]{:S(2)}) collective-permute-start(bf16[256,256]{1,0:T(8,128)(2,1)S(1)} %get-tuple-element.39), channel_id=1, source_target_pairs={{0,16},{16,0},{1,17},{17,1},{2,18},{18,2},{3,19},{19,3},{4,20},{20... | collective-permute-start | bytes 393224 | tf_op jit(solution)/shard_map/ppermute | solution.py:241
  56.7 5.7 %attend.7 = (bf16[256,512]{1,0:T(8,128)(2,1)S(1)}, bf16[256,512]{1,0:T(8,128)(2,1)S(1)}) custom-call(s32[3]{0:T(128)S(1)} %pad_add_fusion.place_ref, bf16[512,2048]{1,0:T(8,128)(2,1)S(1)} %copy-done.2, bf16[512,2048]{1,0:T(8,128)(2,1)S(1)} %copy-done, bf16[512,2048]{1,0:T(8,128)(2,1)S(1)} %copy-done.1, ...), custom_call_target="tpu_custom_call" | custom-call | flops 7040000000 | bytes 23040000 | tf_op jit(solution)/shard_map/attend/pallas_call | solution.py:173
  62.4 2.9 %collective-permute-done.9.past_ref = bf16[2,512,512]{2,1,0:T(8,128)(2,1)S(1)} collective-permute-done((bf16[2,512,512]{2,1,0:T(8,128)(2,1)S(1)}, bf16[2,512,512]{2,1,0:T(8,128)(2,1)S(1)}, u32[]{:S(2)}, u32[]{:S(2)}) %collective-permute-start.9) | collective-permute-done | bytes 1048608 | tf_op jit(solution)/shard_map/ppermute | solution.py:292
  65.3 1.5 %collective-permute-start.14 = (bf16[256,512]{1,0:T(8,128)(2,1)S(1)}, bf16[256,512]{1,0:T(8,128)(2,1)S(1)}, u32[]{:S(2)}, u32[]{:S(2)}) collective-permute-start(bf16[256,512]{1,0:T(8,128)(2,1)S(1)} %get-tuple-element.43), channel_id=1, source_target_pairs={{0,16},{16,0},{1,17},{17,1},{2,18},{18,2},{3,19},{19,3},{4,20},{20... | collective-permute-start | bytes 786440 | tf_op jit(solution)/shard_map/ppermute | solution.py:241
  66.8 5.5 %attend.8 = (bf16[256,512]{1,0:T(8,128)(2,1)S(1)}, bf16[256,512]{1,0:T(8,128)(2,1)S(1)}) custom-call(s32[3]{0:T(128)S(1)} %pad_add_fusion.place_ref, bf16[512,2048]{1,0:T(8,128)(2,1)S(1)} %copy-done.2, bf16[512,2048]{1,0:T(8,128)(2,1)S(1)} %copy-done, bf16[512,2048]{1,0:T(8,128)(2,1)S(1)} %copy-done.1, ...), custom_call_target="tpu_custom_call" | custom-call | flops 7040000000 | bytes 23040000 | tf_op jit(solution)/shard_map/attend/pallas_call | solution.py:173
  72.4 0.6 collective-permute-start.15
  73.0 2.9 %attend.9 = (bf16[256,256]{1,0:T(8,128)(2,1)S(1)}, bf16[256,256]{1,0:T(8,128)(2,1)S(1)}) custom-call(s32[3]{0:T(128)S(1)} %pad_add_fusion.place_ref, bf16[512,2048]{1,0:T(8,128)(2,1)S(1)} %copy-done.2, bf16[512,2048]{1,0:T(8,128)(2,1)S(1)} %copy-done, bf16[512,2048]{1,0:T(8,128)(2,1)S(1)} %copy-done.1, ...), custom_call_target="tpu_custom_call" | custom-call | flops 3520000000 | bytes 11520000 | tf_op jit(solution)/shard_map/attend/pallas_call | solution.py:173
  75.9 1.6 %collective-permute-start.16 = (bf16[256,256]{1,0:T(8,128)(2,1)S(1)}, bf16[256,256]{1,0:T(8,128)(2,1)S(1)}, u32[]{:S(2)}, u32[]{:S(2)}) collective-permute-start(bf16[256,256]{1,0:T(8,128)(2,1)S(1)} %get-tuple-element.51), channel_id=1, source_target_pairs={{0,16},{16,0},{1,17},{17,1},{2,18},{18,2},{3,19},{19,3},{4,20},{20... | collective-permute-start | bytes 393224 | tf_op jit(solution)/shard_map/ppermute | solution.py:241
  77.4 2.9 %attend.10 = (bf16[256,256]{1,0:T(8,128)(2,1)S(1)}, bf16[256,256]{1,0:T(8,128)(2,1)S(1)}) custom-call(s32[3]{0:T(128)S(1)} %pad_add_fusion.place_ref, bf16[512,2048]{1,0:T(8,128)(2,1)S(1)} %copy-done.2, bf16[512,2048]{1,0:T(8,128)(2,1)S(1)} %copy-done, bf16[512,2048]{1,0:T(8,128)(2,1)S(1)} %copy-done.1, ...), custom_call_target="tpu_custom_call" | custom-call | flops 3520000000 | bytes 11520000 | tf_op jit(solution)/shard_map/attend/pallas_call | solution.py:173
  80.4 0.6 collective-permute-start.17
  81.0 2.9 %attend.11 = (bf16[256,256]{1,0:T(8,128)(2,1)S(1)}, bf16[256,256]{1,0:T(8,128)(2,1)S(1)}) custom-call(s32[3]{0:T(128)S(1)} %pad_add_fusion.place_ref, bf16[512,2048]{1,0:T(8,128)(2,1)S(1)} %copy-done.2, bf16[512,2048]{1,0:T(8,128)(2,1)S(1)} %copy-done, bf16[512,2048]{1,0:T(8,128)(2,1)S(1)} %copy-done.1, ...), custom_call_target="tpu_custom_call" | custom-call | flops 3520000000 | bytes 11520000 | tf_op jit(solution)/shard_map/attend/pallas_call | solution.py:173
  83.9 1.6 %collective-permute-start.18 = (bf16[256,256]{1,0:T(8,128)(2,1)S(1)}, bf16[256,256]{1,0:T(8,128)(2,1)S(1)}, u32[]{:S(2)}, u32[]{:S(2)}) collective-permute-start(bf16[256,256]{1,0:T(8,128)(2,1)S(1)} %get-tuple-element.58), channel_id=1, source_target_pairs={{0,16},{16,0},{1,17},{17,1},{2,18},{18,2},{3,19},{19,3},{4,20},{20... | collective-permute-start | bytes 393224 | tf_op jit(solution)/shard_map/ppermute | solution.py:241
  85.4 0.1 collective-permute-done.17.rest_10_
  85.6 3.3 %collective-permute-done.18.rest_11_ = bf16[256,256]{1,0:T(8,128)(2,1)S(1)} collective-permute-done((bf16[256,256]{1,0:T(8,128)(2,1)S(1)}, bf16[256,256]{1,0:T(8,128)(2,1)S(1)}, u32[]{:S(2)}, u32[]{:S(2)}) %collective-permute-start.18) | collective-permute-done | bytes 131104 | tf_op jit(solution)/shard_map/ppermute | solution.py:241
  88.9 3.3 %norm.1 = bf16[256,4096]{1,0:T(8,128)(2,1)} custom-call(s32[1]{0:T(128)} %bitcast.place_ref, bf16[256,4096]{1,0:T(8,128)(2,1)S(1)} %copy-done.3, f32[1,4096]{1,0:T(1,128)S(1)} %bitcast.28, bf16[256,256]{1,0:T(8,128)(2,1)S(1)} %get-tuple-element.35.rest_0_, bf16[256,512]{1,0:T(8,128)(2,1)S(1)} %get-tuple-element.41.rest_1_, ...), custom_call_target="tpu_custom_call" | custom-call | flops 3520000000 | bytes 11520000 | tf_op jit(solution)/shard_map/norm/pallas_call | solution.py:219
  (31 shorter events, 0.3 us)
Async XLA Ops:
  0.0 6.8 %copy-start.5 = (f32[14,16,512]{2,1,0:T(8,128)S(1)}, f32[14,16,512]{2,1,0:T(8,128)}, u32[]{:S(2)}) copy-start(f32[14,16,512]{2,1,0:T(8,128)} %param.9) | copy-start | bytes 1376260
  3.6 19.2 %collective-permute-start = (bf16[2,512,256]{2,1,0:T(8,128)(2,1)}, bf16[2,512,256]{2,1,0:T(8,128)(2,1)S(1)}, u32[]{:S(2)}, u32[]{:S(2)}) collective-permute-start(bf16[2,512,256]{2,1,0:T(8,128)(2,1)} %get-tuple-element.32), channel_id=1, source_target_pairs={{0,1},{1,2},{2,3},{3,4},{4,5},{5,6},{6,7},{7,8},{8,9},{9,10},{10,1... | collective-permute-start | bytes 1572872 | tf_op jit(solution)/shard_map/ppermute | solution.py:292
  4.1 4.4 %collective-permute-start.1 = (bf16[16,128,128]{2,1,0:T(8,128)(2,1)}, bf16[16,128,128]{2,1,0:T(8,128)(2,1)S(1)}, u32[]{:S(2)}, u32[]{:S(2)}) collective-permute-start(bf16[16,128,128]{2,1,0:T(8,128)(2,1)} %get-tuple-element.33), channel_id=1, source_target_pairs={{0,1},{1,0},{2,3},{3,2},{4,5},{5,4},{6,7},{7,6},{8,9},{9,8},{10,11... | collective-permute-start | bytes 1572872 | tf_op jit(solution)/shard_map/ppermute | solution.py:246
  10.2 11.5 %collective-permute-start.2 = (bf16[16,64,128]{2,1,0:T(8,128)(2,1)}, bf16[16,64,128]{2,1,0:T(8,128)(2,1)S(1)}, u32[]{:S(2)}, u32[]{:S(2)}) collective-permute-start(bf16[16,64,128]{2,1,0:T(8,128)(2,1)} %add_convert_fusion.2), channel_id=1, source_target_pairs={{0,2},{1,3},{2,0},{3,1},{4,6},{5,7},{6,4},{7,5},{8,10},{9,11},{10,... | collective-permute-start | bytes 786440 | tf_op jit(solution)/shard_map/ppermute | solution.py:246
  14.6 8.5 %copy-start = (bf16[512,2048]{1,0:T(8,128)(2,1)S(1)}, bf16[512,2048]{1,0:T(8,128)(2,1)}, u32[]{:S(2)}) copy-start(bf16[512,2048]{1,0:T(8,128)(2,1)} %k_ref.13) | copy-start | bytes 6291460
  14.6 8.5 %copy-start.1 = (bf16[512,2048]{1,0:T(8,128)(2,1)S(1)}, bf16[512,2048]{1,0:T(8,128)(2,1)}, u32[]{:S(2)}) copy-start(bf16[512,2048]{1,0:T(8,128)(2,1)} %v_ref.13) | copy-start | bytes 6291460
  22.8 8.3 %collective-permute-start.4 = (bf16[16,64,128]{2,1,0:T(8,128)(2,1)S(1)}, bf16[16,64,128]{2,1,0:T(8,128)(2,1)S(1)}, u32[]{:S(2)}, u32[]{:S(2)}) collective-permute-start(bf16[16,64,128]{2,1,0:T(8,128)(2,1)S(1)} %add_convert_fusion.1), channel_id=1, source_target_pairs={{0,4},{1,5},{2,6},{3,7},{4,0},{5,1},{6,2},{7,3},{8,12},{9,13},{10,... | collective-permute-start | bytes 786440 | tf_op jit(solution)/shard_map/ppermute | solution.py:246
  23.4 31.7 %collective-permute-start.8 = (bf16[2,512,512]{2,1,0:T(8,128)(2,1)S(1)}, bf16[2,512,512]{2,1,0:T(8,128)(2,1)S(1)}, u32[]{:S(2)}, u32[]{:S(2)}) collective-permute-start(bf16[2,512,512]{2,1,0:T(8,128)(2,1)S(1)} %pad_maximum_fusion), channel_id=1, source_target_pairs={{0,1},{1,2},{2,3},{3,4},{4,5},{5,6},{6,7},{7,8},{8,9},{9,10},{10,1... | collective-permute-start | bytes 3145736 | tf_op jit(solution)/shard_map/ppermute | solution.py:292
  31.2 8.1 %collective-permute-start.6 = (bf16[16,64,128]{2,1,0:T(8,128)(2,1)S(1)}, bf16[16,64,128]{2,1,0:T(8,128)(2,1)S(1)}, u32[]{:S(2)}, u32[]{:S(2)}) collective-permute-start(bf16[16,64,128]{2,1,0:T(8,128)(2,1)S(1)} %add_convert_fusion), channel_id=1, source_target_pairs={{0,8},{1,9},{2,10},{3,11},{4,12},{5,13},{6,14},{7,15},{16,24},{17,... | collective-permute-start | bytes 786440 | tf_op jit(solution)/shard_map/ppermute | solution.py:246
  34.5 17.7 %copy-start.2 = (bf16[512,2048]{1,0:T(8,128)(2,1)S(1)}, bf16[512,2048]{1,0:T(8,128)(2,1)}, u32[]{:S(2)}) copy-start(bf16[512,2048]{1,0:T(8,128)(2,1)} %q_ref.11) | copy-start | bytes 6291460
  34.6 5.4 %collective-permute-start.3 = (bf16[16,64,128]{2,1,0:T(8,128)(2,1)S(1)}, bf16[16,64,128]{2,1,0:T(8,128)(2,1)S(1)}, u32[]{:S(2)}, u32[]{:S(2)}) collective-permute-start(bf16[16,64,128]{2,1,0:T(8,128)(2,1)S(1)} %collective-permute-done.2.rest_1_), channel_id=1, source_target_pairs={{0,1},{1,0},{2,3},{3,2},{4,5},{5,4},{6,7},{7,6},{8,9},{9,8},{10,11... | collective-permute-start | bytes 786440 | tf_op jit(solution)/shard_map/ppermute | solution.py:246
  34.7 12.1 %collective-permute-start.5 = (bf16[16,64,128]{2,1,0:T(8,128)(2,1)S(1)}, bf16[16,64,128]{2,1,0:T(8,128)(2,1)S(1)}, u32[]{:S(2)}, u32[]{:S(2)}) collective-permute-start(bf16[16,64,128]{2,1,0:T(8,128)(2,1)S(1)} %collective-permute-done.4.rest_3_), channel_id=1, source_target_pairs={{0,1},{1,0},{2,3},{3,2},{4,5},{5,4},{6,7},{7,6},{8,9},{9,8},{10,11... | collective-permute-start | bytes 786440 | tf_op jit(solution)/shard_map/ppermute | solution.py:246
  39.3 9.4 %collective-permute-start.7 = (bf16[16,64,128]{2,1,0:T(8,128)(2,1)S(1)}, bf16[16,64,128]{2,1,0:T(8,128)(2,1)S(1)}, u32[]{:S(2)}, u32[]{:S(2)}) collective-permute-start(bf16[16,64,128]{2,1,0:T(8,128)(2,1)S(1)} %collective-permute-done.6.rest_5_), channel_id=1, source_target_pairs={{0,1},{1,0},{2,3},{3,2},{4,5},{5,4},{6,7},{7,6},{8,9},{9,8},{10,11... | collective-permute-start | bytes 786440 | tf_op jit(solution)/shard_map/ppermute | solution.py:246
  39.4 25.9 %collective-permute-start.9 = (bf16[2,512,512]{2,1,0:T(8,128)(2,1)S(1)}, bf16[2,512,512]{2,1,0:T(8,128)(2,1)S(1)}, u32[]{:S(2)}, u32[]{:S(2)}) collective-permute-start(bf16[2,512,512]{2,1,0:T(8,128)(2,1)S(1)} %pad_maximum_fusion.1), channel_id=1, source_target_pairs={{0,1},{1,2},{2,3},{3,4},{4,5},{5,6},{6,7},{7,8},{8,9},{9,10},{10,1... | collective-permute-start | bytes 3145736 | tf_op jit(solution)/shard_map/ppermute | solution.py:292
  40.1 32.3 %collective-permute-start.10 = (bf16[2,512,256]{2,1,0:T(8,128)(2,1)S(1)}, bf16[2,512,256]{2,1,0:T(8,128)(2,1)S(1)}, u32[]{:S(2)}, u32[]{:S(2)}) collective-permute-start(bf16[2,512,256]{2,1,0:T(8,128)(2,1)S(1)} %pad_maximum_fusion.2), channel_id=1, source_target_pairs={{0,1},{1,2},{2,3},{3,4},{4,5},{5,6},{6,7},{7,8},{8,9},{9,10},{10,1... | collective-permute-start | bytes 1572872 | tf_op jit(solution)/shard_map/ppermute | solution.py:292
  46.8 29.1 %collective-permute-start.11 = (bf16[2,512,256]{2,1,0:T(8,128)(2,1)S(1)}, bf16[2,512,256]{2,1,0:T(8,128)(2,1)S(1)}, u32[]{:S(2)}, u32[]{:S(2)}) collective-permute-start(bf16[2,512,256]{2,1,0:T(8,128)(2,1)S(1)} %pad_maximum_fusion.3), channel_id=1, source_target_pairs={{0,1},{1,2},{2,3},{3,4},{4,5},{5,6},{6,7},{7,8},{8,9},{9,10},{10,1... | collective-permute-start | bytes 1572872 | tf_op jit(solution)/shard_map/ppermute | solution.py:292
  48.8 31.6 %collective-permute-start.12 = (bf16[2,512,256]{2,1,0:T(8,128)(2,1)S(1)}, bf16[2,512,256]{2,1,0:T(8,128)(2,1)S(1)}, u32[]{:S(2)}, u32[]{:S(2)}) collective-permute-start(bf16[2,512,256]{2,1,0:T(8,128)(2,1)S(1)} %pad_maximum_fusion.4), channel_id=1, source_target_pairs={{0,1},{1,2},{2,3},{3,4},{4,5},{5,6},{6,7},{7,8},{8,9},{9,10},{10,1... | collective-permute-start | bytes 1572872 | tf_op jit(solution)/shard_map/ppermute | solution.py:292
  55.1 28.7 %collective-permute-start.13 = (bf16[256,256]{1,0:T(8,128)(2,1)S(1)}, bf16[256,256]{1,0:T(8,128)(2,1)S(1)}, u32[]{:S(2)}, u32[]{:S(2)}) collective-permute-start(bf16[256,256]{1,0:T(8,128)(2,1)S(1)} %get-tuple-element.39), channel_id=1, source_target_pairs={{0,16},{16,0},{1,17},{17,1},{2,18},{18,2},{3,19},{19,3},{4,20},{20... | collective-permute-start | bytes 393224 | tf_op jit(solution)/shard_map/ppermute | solution.py:241
  65.3 20.1 %collective-permute-start.14 = (bf16[256,512]{1,0:T(8,128)(2,1)S(1)}, bf16[256,512]{1,0:T(8,128)(2,1)S(1)}, u32[]{:S(2)}, u32[]{:S(2)}) collective-permute-start(bf16[256,512]{1,0:T(8,128)(2,1)S(1)} %get-tuple-element.43), channel_id=1, source_target_pairs={{0,16},{16,0},{1,17},{17,1},{2,18},{18,2},{3,19},{19,3},{4,20},{20... | collective-permute-start | bytes 786440 | tf_op jit(solution)/shard_map/ppermute | solution.py:241
  72.4 16.5 %collective-permute-start.15 = (bf16[256,512]{1,0:T(8,128)(2,1)S(1)}, bf16[256,512]{1,0:T(8,128)(2,1)S(1)}, u32[]{:S(2)}, u32[]{:S(2)}) collective-permute-start(bf16[256,512]{1,0:T(8,128)(2,1)S(1)} %get-tuple-element.47), channel_id=1, source_target_pairs={{0,16},{16,0},{1,17},{17,1},{2,18},{18,2},{3,19},{19,3},{4,20},{20... | collective-permute-start | bytes 786440 | tf_op jit(solution)/shard_map/ppermute | solution.py:241
  75.9 9.5 %collective-permute-start.16 = (bf16[256,256]{1,0:T(8,128)(2,1)S(1)}, bf16[256,256]{1,0:T(8,128)(2,1)S(1)}, u32[]{:S(2)}, u32[]{:S(2)}) collective-permute-start(bf16[256,256]{1,0:T(8,128)(2,1)S(1)} %get-tuple-element.51), channel_id=1, source_target_pairs={{0,16},{16,0},{1,17},{17,1},{2,18},{18,2},{3,19},{19,3},{4,20},{20... | collective-permute-start | bytes 393224 | tf_op jit(solution)/shard_map/ppermute | solution.py:241
  80.3 8.6 %copy-start.3 = (bf16[256,4096]{1,0:T(8,128)(2,1)S(1)}, bf16[256,4096]{1,0:T(8,128)(2,1)}, u32[]{:S(2)}) copy-start(bf16[256,4096]{1,0:T(8,128)(2,1)} %gate_ref.1) | copy-start | bytes 6291460
  80.4 8.5 %copy-start.4 = (f32[4096]{0:T(1024)S(1)}, f32[4096]{0:T(1024)}, u32[]{:S(2)}) copy-start(f32[4096]{0:T(1024)} %param.11) | copy-start | bytes 49156
  80.4 5.2 %collective-permute-start.17 = (bf16[256,256]{1,0:T(8,128)(2,1)S(1)}, bf16[256,256]{1,0:T(8,128)(2,1)S(1)}, u32[]{:S(2)}, u32[]{:S(2)}) collective-permute-start(bf16[256,256]{1,0:T(8,128)(2,1)S(1)} %get-tuple-element.55), channel_id=1, source_target_pairs={{0,16},{16,0},{1,17},{17,1},{2,18},{18,2},{3,19},{19,3},{4,20},{20... | collective-permute-start | bytes 393224 | tf_op jit(solution)/shard_map/ppermute | solution.py:241
  83.9 5.0 %collective-permute-start.18 = (bf16[256,256]{1,0:T(8,128)(2,1)S(1)}, bf16[256,256]{1,0:T(8,128)(2,1)S(1)}, u32[]{:S(2)}, u32[]{:S(2)}) collective-permute-start(bf16[256,256]{1,0:T(8,128)(2,1)S(1)} %get-tuple-element.58), channel_id=1, source_target_pairs={{0,16},{16,0},{1,17},{17,1},{2,18},{18,2},{3,19},{19,3},{4,20},{20... | collective-permute-start | bytes 393224 | tf_op jit(solution)/shard_map/ppermute | solution.py:241
